TPU v7x, 768 devices: a whole 4x8x12 slice. The times are simulated.
768 devices in a mesh: fsdp: 12 (over z), grp: 64 (over y, x, core).
Axes of the slice: x: 4, y: 8, z: 12, core: 2. Of those that a mesh axis runs over, the one named last changes fastest.
Arguments:
- tokens: bfloat16 [98304, 4608], P(('fsdp', 'grp')), may hold values from -24 to 24
- w_values: bfloat16 [4608, 512], P(('fsdp', 'grp')), may hold values from -0.09375 to 0.09375
- w_scales: float32 [1152], replicated, may hold values from 0.25 to 4
- out_grad: bfloat16 [98304, 512], P(('fsdp', 'grp')), may hold values from -6 to 6
Outputs:
- projected: bfloat16 [98304, 512], P(('fsdp', 'grp'))
- token_grad: bfloat16 [98304, 4608], P(('fsdp', 'grp'))
- weight_grad: float32 [4608, 512], P(('fsdp', 'grp'))
All inputs are finite; a program needn't handle non-finite values.
Results may differ from a plain program's by a relative error of at most 0.019.
Values may be sent and summed in bfloat16 or wider, within the bound.
No kernel may reach another device: no remote copies, remote signals or barrier semaphores. Data moves between devices by JAX's collectives and lax.ppermute only.
A program may use at most 64 MiB of HBM per device.

v0:
```python
import math

import jax
import jax.numpy as jnp
from jax import lax
from jax.sharding import PartitionSpec as P

BLOCK_ROWS = 4


def body(tokens, w_values, w_scales, out_grad):
    row_count = w_values.shape[0]
    group_size = lax.axis_size("grp")
    outer_size = lax.axis_size("fsdp")
    token_count = tokens.shape[0]
    position = lax.axis_index("fsdp") * group_size + lax.axis_index("grp")
    row_ids = position * row_count + lax.iota(jnp.int32, row_count)
    block_ids = lax.iota(jnp.int32, w_scales.shape[0])
    matched = row_ids[:, None] // BLOCK_ROWS == block_ids[None, :]
    row_scale = jnp.sum(jnp.where(matched, w_scales[None, :], jnp.float32(0.0)), axis=1)
    local_rows = (w_values.astype(jnp.float32) * row_scale[:, None]).astype(jnp.bfloat16)
    shares = lax.psum_scatter(
        lax.dot_general(
            tokens, out_grad, (((0,), (0,)), ((), ())), preferred_element_type=jnp.float32
        ).astype(jnp.bfloat16),
        "fsdp",
        scatter_dimension=0,
        tiled=True,
    ).astype(jnp.float32)
    summed = lax.psum_scatter(shares, "grp", scatter_dimension=0, tiled=True)
    total_tokens = token_count * outer_size * group_size
    weight_grad = summed * (1.0 / math.sqrt(total_tokens))
    weights = lax.all_gather(local_rows, ("fsdp", "grp"), axis=0, tiled=True)
    projected = jnp.dot(tokens, weights, preferred_element_type=jnp.float32).astype(jnp.bfloat16)
    token_grad = lax.dot_general(
        out_grad, weights, (((1,), (1,)), ((), ())), preferred_element_type=jnp.float32
    ).astype(jnp.bfloat16)
    return (projected, token_grad, weight_grad)


def solution(mesh):
    return jax.shard_map(
        body,
        mesh=mesh,
        in_specs=(
            P(("fsdp", "grp"), None),
            P(("fsdp", "grp"), None),
            P(),
            P(("fsdp", "grp"), None),
        ),
        out_specs=(P(("fsdp", "grp"), None), P(("fsdp", "grp"), None), P(("fsdp", "grp"), None)),
        check_vma=False,
    )
```

profile of v0, /device:TPU:1, one launch (start us, length us, event | category | flops | bytes accessed | tf_op | source)
XLA Modules:
  0.0 482.0 jit_solution(16996902054034088671)
XLA Ops:
  8.0 0.0 copy-start
  8.0 0.0 all-gather.3.cloned.1.call-start
  8.1 1.0 select_reduce_fusion
  9.1 1.4 fusion.2
  10.4 0.0 all-gather.3.cloned.1.call-update
  10.4 0.0 reduce-scatter.2.cloned.1.call-start
  10.5 0.0 copy-done
  10.5 4.5 convolution_convert_fusion
  15.0 0.0 reduce-scatter.2.cloned.1.call-update
  15.1 1.3 dynamic-slice
  17.0 0.0 copy-start.1
  17.0 188.9 %all-gather.3.cloned.1.call-done = bf16[768,6,512]{2,1,0:T(8,128)(2,1)} async-done(((bf16[1,6,512]{2,1,0:T(8,128)(2,1)}), bf16[768,6,512]{2,1,0:T(8,128)(2,1)}) %all-gather.3.cloned.1.call-update) | async-done | bytes 4718608 | tf_op jit(solution)/shard_map/all_gather | solution.py:33
  205.9 8.8 %reshape.46 = bf16[4608,512]{1,0:T(8,128)(2,1)} reshape(bf16[768,6,512]{2,1,0:T(8,128)(2,1)} %all-gather.3.cloned.1.call-done) | data formatting | bytes 9437184
  214.7 0.0 copy-done.1
  214.7 3.7 fusion
  218.5 1.4 copy.14
  219.9 3.8 fusion.1
  223.6 0.8 copy.13
  224.4 0.0 reduce-scatter.2.cloned.1.call-done
  224.4 249.5 %all-reduce.2 = f32[384,512]{1,0:T(8,128)S(1)} all-reduce(bf16[384,512]{1,0:T(8,128)(2,1)} %reduce-scatter.2.cloned.1.call-done), channel_id=3, replica_groups=mesh['fsdp'=12,'grp'=64] {'grp'}, use_global_device_ids=true, to_apply=%region_2.3.clone | all-reduce | flops 196608 | bytes 1179648
  474.0 0.6 dynamic-slice_multiply_fusion
  (1 shorter events, 0.0 us)
Async XLA Ops:
  8.0 2.5 copy-start
  8.0 197.9 %all-gather.3.cloned.1.call-start = ((), (), s32[]{:S(2)}) async-start(), calls=%async_computation.2 | async-start | bytes 6299648 | tf_op jit(solution)/shard_map/all_gather | solution.py:33
  10.4 214.0 %reduce-scatter.2.cloned.1.call-start = ((), (), s32[]{:S(2)}) async-start(), calls=%async_computation.1 | async-start | bytes 5111808 | tf_op jit(solution)/shard_map/reduce_scatter | solution.py:22
  17.0 197.7 %copy-start.1 = (bf16[128,512]{1,0:T(8,128)(2,1)S(1)}, bf16[128,512]{1,0:T(8,128)(2,1)}, u32[]{:S(2)}) copy-start(bf16[128,512]{1,0:T(8,128)(2,1)} %param.7) | copy-start | bytes 393220
Sparse Core Ops, SparseCore 0:
  15.0 190.8 all-gather.2
Sparse Core Ops, SparseCore 1:
  15.2 74.8 reduce-scatter.1
where the time goes:
time: 486 us; the launch traced here: 482 us
  blocking collectives  250 us (51%)
  waiting for transfers between devices  189 us (39%)
  between operations  16.2 us (3%)
  local copies, waits for them, and re-layouts  12.3 us (3%)
  matrix products  12 us (2%)
    unnamed x1, blocking collectives  250 us
    all_gather x1, waiting for transfers between devices, body(): weights = lax.all_gather(local_rows, ('fsdp', 'grp'), axis=0, tiled=True)  189 us
    unnamed x8, local copies, waits for them, and re-layouts  12.3 us
  transfers between devices with their start and end apart: 2, of which 1 were waited for; matrix products, arithmetic and copies ran while one was open for 5% of the time, Pallas kernels for 0%

commit v1 on v0

v1 whole, which is shorter than its diff:
```python
import math

import numpy as np
import jax
import jax.numpy as jnp
from jax import lax
from jax.sharding import Mesh, PartitionSpec as P

BLOCK_ROWS = 4
NZ, NY, NX, NC = 12, 8, 4, 2
AXES = ("z", "y", "x", "c")
BF16 = jnp.bfloat16
F32 = jnp.float32


def block_moves():
    moves = []
    for block in range(NZ * NY * NX * NC):
        rest, z = divmod(block, NZ)
        rest, y = divmod(rest, NY)
        c, x = divmod(rest, NX)
        moves.append((block, ((z * NY + y) * NX + x) * NC + c))
    return moves


def scaled_rows(w_values, w_scales):
    rows = w_values.shape[0]
    first = lax.axis_index(AXES) * rows
    start = first // BLOCK_ROWS
    pair = lax.dynamic_slice(w_scales, (start,), (2,))
    block = (first + lax.iota(jnp.int32, rows)) // BLOCK_ROWS - start
    scale = jnp.where(block == 0, pair[0], pair[1])
    return (w_values.astype(F32) * scale[:, None]).astype(BF16)


def gather(rows, axis, size):
    out = lax.all_to_all(jnp.broadcast_to(rows[None], (size, *rows.shape)), axis, 0, 0)
    return out.reshape(-1, rows.shape[1])


def reduce(rows, axis, size):
    out = lax.all_to_all(rows.reshape(size, -1, rows.shape[1]), axis, 0, 0)
    return jnp.sum(out.astype(F32), axis=0)


def body(tokens, w_values, w_scales, out_grad):
    moves = block_moves()
    rows = lax.ppermute(scaled_rows(w_values, w_scales), AXES, moves)
    partial = lax.dot_general(
        tokens, out_grad, (((0,), (0,)), ((), ())), preferred_element_type=F32
    ).astype(BF16)
    total = reduce(partial, "c", NC).astype(BF16)
    total = reduce(total, "x", NX).astype(BF16)
    total = reduce(total, "y", NY).astype(BF16)
    total = reduce(total, "z", NZ)
    count = tokens.shape[0] * NZ * NY * NX * NC
    weight_grad = lax.ppermute(
        total * (1.0 / math.sqrt(count)), AXES, [(b, a) for a, b in moves]
    )
    rows = gather(rows, "z", NZ)
    rows = gather(rows, "y", NY)
    rows = gather(rows, "x", NX)
    weights = gather(rows, "c", NC)
    projected = jnp.dot(tokens, weights, preferred_element_type=F32).astype(BF16)
    token_grad = lax.dot_general(
        out_grad, weights, (((1,), (1,)), ((), ())), preferred_element_type=F32
    ).astype(BF16)
    return projected, token_grad, weight_grad


def solution(mesh):
    split = Mesh(mesh.devices.reshape(NZ, NY, NX, NC), AXES)
    by_rows = P(AXES, None)
    return jax.shard_map(
        body,
        mesh=split,
        in_specs=(by_rows, by_rows, P(), by_rows),
        out_specs=(by_rows, by_rows, by_rows),
        check_vma=False,
    )
```

time: 486 us -> 185 us (0.38)
  blocking collectives: 250 us -> 44.7 us
  waiting for transfers between devices: 189 us -> 80.3 us
  starting transfers between devices: 0.08 us -> 33.4 us
  between operations: 16.2 us -> 0.81 us
  matrix products: 12 us -> 5.12 us
  other arithmetic: 2.96 us -> 9.06 us
    unnamed x1 -> x0, blocking collectives: 250 us -> none
    all_gather x1 -> x0, waiting for transfers between devices: 189 us -> none  [body(): weights = lax.all_gather(local_rows, ('fsdp', 'grp'), axis=0, tiled=True)]
    all_to_all x0 -> x5, waiting for transfers between devices: none -> 70.9 us  [the longest x3 40.8 us: gather(): lax.all_to_all(jnp.broadcast_to(rows[None], (size, *rows.shape)), axis, 0...]
    all_to_all x0 -> x3, blocking collectives: none -> 44.7 us  [the longest x2 31.9 us: reduce(): out = lax.all_to_all(rows.reshape(size, -1, rows.shape[1]), axis, 0, 0)]
    all_to_all x0 -> x5, starting transfers between devices: none -> 23.7 us  [the longest x3 13.1 us: gather(): lax.all_to_all(jnp.broadcast_to(rows[None], (size, *rows.shape)), axis, 0...]
    ppermute x0 -> x2, starting transfers between devices: none -> 9.66 us  [the longest x1 7.75 us: body(): lax.ppermute(total * (1.0 / math.sqrt(count)), AXES, [(b, a) for a, b in...]
    ppermute x0 -> x2, waiting for transfers between devices: none -> 9.35 us  [the longest x1 9.35 us: body(): rows = lax.ppermute(scaled_rows(w_values, w_scales), AXES, moves)]
    unnamed x8 -> x9, local copies, waits for them, and re-layouts: 12.3 us -> 4.78 us
  transfers between devices with their start and end apart: 2 -> 7, of which waited for: 1 -> 6; matrix products, arithmetic and copies ran while one was open for 5% -> 6% of each run, Pallas kernels for 0% -> 0%
where the time goes in v1:
time: 185 us; the launch traced here: 184 us
  waiting for transfers between devices  80.3 us (43%)
  blocking collectives  44.7 us (24%)
  starting transfers between devices  33.4 us (18%)
  local copies, waits for them, and re-layouts  10.5 us (6%)
  other arithmetic  9.06 us (5%)
  matrix products  5.12 us (3%)
    all_to_all x3, waiting for transfers between devices, gather(): lax.all_to_all(jnp.broadcast_to(rows[None], (size, *rows.shape)), axis, 0...  40.8 us
    all_to_all x2, blocking collectives, reduce(): out = lax.all_to_all(rows.reshape(size, -1, rows.shape[1]), axis, 0, 0)  31.9 us
    all_to_all x2, waiting for transfers between devices, reduce(): out = lax.all_to_all(rows.reshape(size, -1, rows.shape[1]), axis, 0, 0)  30.1 us
    all_to_all x3, starting transfers between devices, gather(): lax.all_to_all(jnp.broadcast_to(rows[None], (size, *rows.shape)), axis, 0...  13.1 us
    all_to_all x1, blocking collectives, gather(): lax.all_to_all(jnp.broadcast_to(rows[None], (size, *rows.shape)), axis, 0...  12.7 us
    all_to_all x2, starting transfers between devices, reduce(): out = lax.all_to_all(rows.reshape(size, -1, rows.shape[1]), axis, 0, 0)  10.6 us
    ppermute x1, waiting for transfers between devices, body(): rows = lax.ppermute(scaled_rows(w_values, w_scales), AXES, moves)  9.35 us
    ppermute x1, starting transfers between devices, body(): lax.ppermute(total * (1.0 / math.sqrt(count)), AXES, [(b, a) for a, b in...  7.75 us
  transfers between devices with their start and end apart: 7, of which 6 were waited for; matrix products, arithmetic and copies ran while one was open for 6% of the time, Pallas kernels for 0%

profile of v1, /device:TPU:1, one launch (start us, length us, event | category | flops | bytes accessed | tf_op | source)
XLA Modules:
  0.0 183.8 jit_solution(8899662110232841230)
XLA Ops:
  0.6 1.3 copy-done
  1.9 2.3 %convolution_convert_fusion = bf16[4608,512]{1,0:T(8,128)(2,1)S(1)} fusion(bf16[128,4608]{1,0:T(8,128)(2,1)S(1)} %copy-done, bf16[128,512]{1,0:T(8,128)(2,1)} %param.7), kind=kOutput, calls=%fused_computation | convolution fusion | flops 606339072 | bytes 6029312 | tf_op jit(solution)/shard_map/dot_general | solution.py:49
  4.2 18.8 %all_to_all.40 = bf16[2,2304,512]{2,1,0:T(8,128)(2,1)} all-to-all(bf16[2,2304,512]{2,1,0:T(8,128)(2,1)S(1)} %bitcast.18), channel_id=1, replica_groups=mesh['z'=12,'y'=8,'x'=4,'c'=2] {'c'}, dimensions={0} | all-to-all | bytes 9437184 | tf_op jit(solution)/shard_map/all_to_all | solution.py:42
  23.0 5.3 %reduce_sum.45 = bf16[2304,512]{1,0:T(8,128)(2,1)} reduce(bf16[2,2304,512]{2,1,0:T(8,128)(2,1)} %all_to_all.40, bf16[]{:T(256)} %constant.58.clone.1), dimensions={0}, to_apply=%region_0.1 | reduce | flops 1179648 | bytes 7077890 | tf_op jit(solution)/shard_map/reduce_sum | solution.py:43
  28.3 3.8 %all-to-all-start.5 = ((bf16[4,576,512]{2,1,0:T(8,128)(2,1)}), bf16[4,576,512]{2,1,0:T(8,128)(2,1)S(1)}, u32[]{:S(2)}, u32[]{:S(2)}) async-start(bf16[4,576,512]{2,1,0:T(8,128)(2,1)} %bitcast.8), calls=%async_computation.5 | async-start | bytes 4718592 | tf_op jit(solution)/shard_map/all_to_all | solution.py:42
  32.1 0.8 dynamic_slice.3
  33.5 1.3 compare_select_fusion
  34.9 1.9 %collective-permute-start = (bf16[6,512]{1,0:T(8,128)(2,1)S(1)}, bf16[6,512]{1,0:T(8,128)(2,1)S(1)}, u32[]{:S(2)}, u32[]{:S(2)}) collective-permute-start(bf16[6,512]{1,0:T(8,128)(2,1)S(1)} %multiply_convert_fusion), channel_id=1, source_target_pairs={{0,0},{1,64},{2,128},{3,192},{4,256},{5,320},{6,384},{7,448},{8,51... | collective-permute-start | bytes 18440 | tf_op jit(solution)/shard_map/ppermute | solution.py:48
  36.8 9.4 %collective-permute-done = bf16[6,512]{1,0:T(8,128)(2,1)S(1)} collective-permute-done((bf16[6,512]{1,0:T(8,128)(2,1)S(1)}, bf16[6,512]{1,0:T(8,128)(2,1)S(1)}, u32[]{:S(2)}, u32[]{:S(2)}) %collective-permute-start) | collective-permute-done | bytes 6176 | tf_op jit(solution)/shard_map/ppermute | solution.py:48
  46.2 14.8 %all-to-all-done.5 = bf16[4,576,512]{2,1,0:T(8,128)(2,1)S(1)} async-done(((bf16[4,576,512]{2,1,0:T(8,128)(2,1)}), bf16[4,576,512]{2,1,0:T(8,128)(2,1)S(1)}, u32[]{:S(2)}, u32[]{:S(2)}) %all-to-all-start.5) | async-done | bytes 2359328 | tf_op jit(solution)/shard_map/all_to_all | solution.py:42
  61.0 0.6 broadcast_in_dim.38
  61.6 6.0 %all-to-all-start = ((bf16[12,6,512]{2,1,0:T(8,128)(2,1)}), bf16[12,6,512]{2,1,0:T(8,128)(2,1)}, u32[]{:S(2)}, u32[]{:S(2)}) async-start(bf16[12,6,512]{2,1,0:T(8,128)(2,1)} %broadcast_in_dim.38), calls=%async_computation | async-start | bytes 196608 | tf_op jit(solution)/shard_map/all_to_all | solution.py:37
  67.6 1.3 reduce_sum.46
  68.9 8.9 %all-to-all-done = bf16[12,6,512]{2,1,0:T(8,128)(2,1)} async-done(((bf16[12,6,512]{2,1,0:T(8,128)(2,1)}), bf16[12,6,512]{2,1,0:T(8,128)(2,1)}, u32[]{:S(2)}, u32[]{:S(2)}) %all-to-all-start) | async-done | bytes 73760 | tf_op jit(solution)/shard_map/all_to_all | solution.py:37
  77.8 6.8 %all-to-all-start.6 = ((bf16[8,72,512]{2,1,0:T(8,128)(2,1)}), bf16[8,72,512]{2,1,0:T(8,128)(2,1)S(1)}, u32[]{:S(2)}, u32[]{:S(2)}) async-start(bf16[8,72,512]{2,1,0:T(8,128)(2,1)} %bitcast.23), calls=%async_computation.6 | async-start | bytes 1179648 | tf_op jit(solution)/shard_map/all_to_all | solution.py:42
  84.6 0.9 broadcast_in_dim.39
  85.5 15.3 %all-to-all-done.6 = bf16[8,72,512]{2,1,0:T(8,128)(2,1)S(1)} async-done(((bf16[8,72,512]{2,1,0:T(8,128)(2,1)}), bf16[8,72,512]{2,1,0:T(8,128)(2,1)S(1)}, u32[]{:S(2)}, u32[]{:S(2)}) %all-to-all-start.6) | async-done | bytes 589856 | tf_op jit(solution)/shard_map/all_to_all | solution.py:42
  100.9 0.9 broadcast_in_dim.40
  101.7 3.5 %all-to-all-start.1 = ((bf16[8,72,512]{2,1,0:T(8,128)(2,1)}), bf16[8,72,512]{2,1,0:T(8,128)(2,1)S(1)}, u32[]{:S(2)}, u32[]{:S(2)}) async-start(bf16[8,72,512]{2,1,0:T(8,128)(2,1)} %broadcast_in_dim.40), calls=%async_computation.1 | async-start | bytes 1179648 | tf_op jit(solution)/shard_map/all_to_all | solution.py:37
  105.4 16.1 %all-to-all-done.1 = bf16[8,72,512]{2,1,0:T(8,128)(2,1)S(1)} async-done(((bf16[8,72,512]{2,1,0:T(8,128)(2,1)}), bf16[8,72,512]{2,1,0:T(8,128)(2,1)S(1)}, u32[]{:S(2)}, u32[]{:S(2)}) %all-to-all-start.1) | async-done | bytes 589856 | tf_op jit(solution)/shard_map/all_to_all | solution.py:37
  121.5 13.2 %all_to_all.41 = bf16[12,6,512]{2,1,0:T(8,128)(2,1)} all-to-all(bf16[12,6,512]{2,1,0:T(8,128)(2,1)S(1)} %reshape.51), channel_id=1, replica_groups=mesh['z'=12,'y'=8,'x'=4,'c'=2] {'z'}, dimensions={0} | all-to-all | bytes 147456 | tf_op jit(solution)/shard_map/all_to_all | solution.py:42
  134.7 1.6 broadcast_in_dim.42
  136.3 3.6 %all-to-all-start.2 = ((bf16[4,576,512]{2,1,0:T(8,128)(2,1)}), bf16[4,576,512]{2,1,0:T(8,128)(2,1)S(1)}, u32[]{:S(2)}, u32[]{:S(2)}) async-start(bf16[4,576,512]{2,1,0:T(8,128)(2,1)} %broadcast_in_dim.42), calls=%async_computation.2 | async-start | bytes 4718592 | tf_op jit(solution)/shard_map/all_to_all | solution.py:37
  139.9 0.9 convert_reduce_fusion
  140.9 7.8 %collective-permute-start.1 = (f32[6,512]{1,0:T(8,128)S(1)}, f32[6,512]{1,0:T(8,128)}, u32[]{:S(2)}, u32[]{:S(2)}) collective-permute-start(f32[6,512]{1,0:T(8,128)S(1)} %broadcast_multiply_fusion), channel_id=1, source_target_pairs={{0,0},{64,1},{128,2},{192,3},{256,4},{320,5},{384,6},{448,7},{512,... | collective-permute-start | bytes 36872 | tf_op jit(solution)/shard_map/ppermute | solution.py:57
  148.6 15.8 %all-to-all-done.2 = bf16[4,576,512]{2,1,0:T(8,128)(2,1)S(1)} async-done(((bf16[4,576,512]{2,1,0:T(8,128)(2,1)}), bf16[4,576,512]{2,1,0:T(8,128)(2,1)S(1)}, u32[]{:S(2)}, u32[]{:S(2)}) %all-to-all-start.2) | async-done | bytes 2359328 | tf_op jit(solution)/shard_map/all_to_all | solution.py:37
  164.7 12.7 %all_to_all.42 = bf16[2,2304,512]{2,1,0:T(8,128)(2,1)S(1)} all-to-all(bf16[2,2304,512]{2,1,0:T(8,128)(2,1)S(1)} %broadcast_in_dim.44), channel_id=1, replica_groups=mesh['z'=12,'y'=8,'x'=4,'c'=2] {'c'}, dimensions={0} | all-to-all | bytes 9437184 | tf_op jit(solution)/shard_map/all_to_all | solution.py:37
  177.5 1.4 fusion.1
  178.9 1.4 fusion
  180.3 1.4 copy.10
  181.7 0.8 copy.9
  182.5 1.3 copy.12
  (12 shorter events, 1.1 us)
Async XLA Ops:
  0.6 1.3 copy-start
  28.3 6.5 %copy-start.2 = (bf16[6,512]{1,0:T(8,128)(2,1)S(1)}, bf16[6,512]{1,0:T(8,128)(2,1)}, u32[]{:S(2)}) copy-start(bf16[6,512]{1,0:T(8,128)(2,1)} %param.5) | copy-start | bytes 18436
  28.3 32.6 %all-to-all-start.5 = ((bf16[4,576,512]{2,1,0:T(8,128)(2,1)}), bf16[4,576,512]{2,1,0:T(8,128)(2,1)S(1)}, u32[]{:S(2)}, u32[]{:S(2)}) async-start(bf16[4,576,512]{2,1,0:T(8,128)(2,1)} %bitcast.8), calls=%async_computation.5 | async-start | bytes 4718592 | tf_op jit(solution)/shard_map/all_to_all | solution.py:42
  34.9 11.3 %collective-permute-start = (bf16[6,512]{1,0:T(8,128)(2,1)S(1)}, bf16[6,512]{1,0:T(8,128)(2,1)S(1)}, u32[]{:S(2)}, u32[]{:S(2)}) collective-permute-start(bf16[6,512]{1,0:T(8,128)(2,1)S(1)} %multiply_convert_fusion), channel_id=1, source_target_pairs={{0,0},{1,64},{2,128},{3,192},{4,256},{5,320},{6,384},{7,448},{8,51... | collective-permute-start | bytes 18440 | tf_op jit(solution)/shard_map/ppermute | solution.py:48
  61.6 16.2 %all-to-all-start = ((bf16[12,6,512]{2,1,0:T(8,128)(2,1)}), bf16[12,6,512]{2,1,0:T(8,128)(2,1)}, u32[]{:S(2)}, u32[]{:S(2)}) async-start(bf16[12,6,512]{2,1,0:T(8,128)(2,1)} %broadcast_in_dim.38), calls=%async_computation | async-start | bytes 196608 | tf_op jit(solution)/shard_map/all_to_all | solution.py:37
  77.8 23.1 %all-to-all-start.6 = ((bf16[8,72,512]{2,1,0:T(8,128)(2,1)}), bf16[8,72,512]{2,1,0:T(8,128)(2,1)S(1)}, u32[]{:S(2)}, u32[]{:S(2)}) async-start(bf16[8,72,512]{2,1,0:T(8,128)(2,1)} %bitcast.23), calls=%async_computation.6 | async-start | bytes 1179648 | tf_op jit(solution)/shard_map/all_to_all | solution.py:42
  101.7 19.8 %all-to-all-start.1 = ((bf16[8,72,512]{2,1,0:T(8,128)(2,1)}), bf16[8,72,512]{2,1,0:T(8,128)(2,1)S(1)}, u32[]{:S(2)}, u32[]{:S(2)}) async-start(bf16[8,72,512]{2,1,0:T(8,128)(2,1)} %broadcast_in_dim.40), calls=%async_computation.1 | async-start | bytes 1179648 | tf_op jit(solution)/shard_map/all_to_all | solution.py:37
  136.3 28.1 %all-to-all-start.2 = ((bf16[4,576,512]{2,1,0:T(8,128)(2,1)}), bf16[4,576,512]{2,1,0:T(8,128)(2,1)S(1)}, u32[]{:S(2)}, u32[]{:S(2)}) async-start(bf16[4,576,512]{2,1,0:T(8,128)(2,1)} %broadcast_in_dim.42), calls=%async_computation.2 | async-start | bytes 4718592 | tf_op jit(solution)/shard_map/all_to_all | solution.py:37
  140.9 41.6 %collective-permute-start.1 = (f32[6,512]{1,0:T(8,128)S(1)}, f32[6,512]{1,0:T(8,128)}, u32[]{:S(2)}, u32[]{:S(2)}) collective-permute-start(f32[6,512]{1,0:T(8,128)S(1)} %broadcast_multiply_fusion), channel_id=1, source_target_pairs={{0,0},{64,1},{128,2},{192,3},{256,4},{320,5},{384,6},{448,7},{512,... | collective-permute-start | bytes 36872 | tf_op jit(solution)/shard_map/ppermute | solution.py:57
  177.5 1.4 copy-start.1

commit v2 on v1

--- a/solution.py
+++ b/solution.py
@@ -1,6 +1,5 @@
 import math
 
-import numpy as np
 import jax
 import jax.numpy as jnp
 from jax import lax
@@ -43,28 +42,46 @@
     return jnp.sum(out.astype(F32), axis=0)
 
 
+def swap(array):
+    return lax.ppermute(array, "c", [(0, 1), (1, 0)])
+
+
+def dot(a, b, over):
+    return lax.dot_general(a, b, ((over[:1], over[1:]), ((), ())), preferred_element_type=F32)
+
+
 def body(tokens, w_values, w_scales, out_grad):
     moves = block_moves()
+    core = lax.axis_index("c")
+    half = tokens.shape[1] // NC
+    low, high = tokens[:, :half], tokens[:, half:]
+    mine = jnp.where(core == 0, low, high)
+    theirs = swap(jnp.where(core == 0, high, low))
+    their_grad = swap(out_grad)
     rows = lax.ppermute(scaled_rows(w_values, w_scales), AXES, moves)
-    partial = lax.dot_general(
-        tokens, out_grad, (((0,), (0,)), ((), ())), preferred_element_type=F32
-    ).astype(BF16)
-    total = reduce(partial, "c", NC).astype(BF16)
-    total = reduce(total, "x", NX).astype(BF16)
+
+    partial = (dot(mine, out_grad, (0, 0)) + dot(theirs, their_grad, (0, 0))).astype(BF16)
+    partial, rows = lax.optimization_barrier((partial, rows))
+    total = lax.psum_scatter(partial, "x", scatter_dimension=0, tiled=True)
     total = reduce(total, "y", NY).astype(BF16)
     total = reduce(total, "z", NZ)
+
+    rows = gather(rows, "z", NZ)
+    rows = gather(rows, "y", NY)
+    weights = lax.all_gather(rows, "x", axis=0, tiled=True)
+    total, weights = lax.optimization_barrier((total, weights))
     count = tokens.shape[0] * NZ * NY * NX * NC
     weight_grad = lax.ppermute(
         total * (1.0 / math.sqrt(count)), AXES, [(b, a) for a, b in moves]
     )
-    rows = gather(rows, "z", NZ)
-    rows = gather(rows, "y", NY)
-    rows = gather(rows, "x", NX)
-    weights = gather(rows, "c", NC)
-    projected = jnp.dot(tokens, weights, preferred_element_type=F32).astype(BF16)
-    token_grad = lax.dot_general(
-        out_grad, weights, (((1,), (1,)), ((), ())), preferred_element_type=F32
-    ).astype(BF16)
+    for_them = swap(dot(theirs, weights, (1, 0)))
+    grad_for_them = swap(dot(their_grad, weights, (1, 1)).astype(BF16))
+    projected = (dot(mine, weights, (1, 0)) + for_them).astype(BF16)
+    grad = dot(out_grad, weights, (1, 1)).astype(BF16)
+    token_grad = jnp.concatenate(
+        [jnp.where(core == 0, grad, grad_for_them), jnp.where(core == 0, grad_for_them, grad)],
+        axis=1,
+    )
     return projected, token_grad, weight_grad
 
 

time: 185 us -> 158 us (0.85)
  the two profiles are of different devices: /device:TPU:1 before, /device:TPU:68 now
where the time goes in v2:
time: 158 us; the launch traced here: 157 us
  blocking collectives  84.9 us (54%)
  starting transfers between devices  30.1 us (19%)
  between operations  14.3 us (9%)
  waiting for transfers between devices  12.8 us (8%)
  matrix products  7.32 us (5%)
  local copies, waits for them, and re-layouts  5.46 us (3%)
  other arithmetic  2.41 us (2%)
    all_to_all x2, blocking collectives, reduce(): out = lax.all_to_all(rows.reshape(size, -1, rows.shape[1]), axis, 0, 0)  44.2 us
    all_to_all x2, blocking collectives, gather(): lax.all_to_all(jnp.broadcast_to(rows[None], (size, *rows.shape)), axis, 0...  40.7 us
    ppermute x1, starting transfers between devices, body(): rows = lax.ppermute(scaled_rows(w_values, w_scales), AXES, moves)  18.1 us
    ppermute x1, waiting for transfers between devices, body(): lax.ppermute(total * (1.0 / math.sqrt(count)), AXES, [(b, a) for a, b in...  12.7 us
    ppermute x4, starting transfers between devices, swap(): return lax.ppermute(array, 'c', [(0, 1), (1, 0)])  8.65 us
    dot_general x6, matrix products, dot(): lax.dot_general(a, b, ((over[:1], over[1:]), ((), ())), preferred_element...  7.32 us
    ppermute x1, starting transfers between devices, body(): lax.ppermute(total * (1.0 / math.sqrt(count)), AXES, [(b, a) for a, b in...  3.36 us
  transfers between devices with their start and end apart: 8, of which 1 were waited for; matrix products, arithmetic and copies ran while one was open for 5% of the time, Pallas kernels for 0%

profile of v2, /device:TPU:68, one launch (start us, length us, event | category | flops | bytes accessed | tf_op | source)
XLA Modules:
  0.0 157.3 jit_solution(3198974309803164691)
XLA Ops:
  7.2 1.3 fusion.5
  8.6 0.3 copy.13
  8.9 0.3 copy.14
  9.2 0.1 broadcast_select_fusion.2
  9.3 1.9 %collective-permute-start = (bf16[128,2304]{0,1:T(8,128)(2,1)S(1)}, bf16[128,2304]{0,1:T(8,128)(2,1)S(1)}, u32[]{:S(2)}, u32[]{:S(2)}) collective-permute-start(bf16[128,2304]{0,1:T(8,128)(2,1)S(1)} %broadcast_select_fusion.2), channel_id=1, source_target_pairs={{0,1},{1,0},{2,3},{3,2},{4,5},{5,4},{6,7},{7,6},{8,9},{9,8},{10,11... | collective-permute-start | bytes 1769480 | tf_op jit(solution)/shard_map/ppermute | solution.py:46
  11.2 2.4 %collective-permute-start.1 = (bf16[128,512]{1,0:T(8,128)(2,1)S(1)}, bf16[128,512]{1,0:T(8,128)(2,1)S(1)}, u32[]{:S(2)}, u32[]{:S(2)}) collective-permute-start(bf16[128,512]{1,0:T(8,128)(2,1)S(1)} %copy-done.1), channel_id=1, source_target_pairs={{0,1},{1,0},{2,3},{3,2},{4,5},{5,4},{6,7},{7,6},{8,9},{9,8},{10,11... | collective-permute-start | bytes 393224 | tf_op jit(solution)/shard_map/ppermute | solution.py:46
  13.6 0.8 dynamic_slice.3
  14.4 0.6 fusion.6
  15.0 1.3 compare_select_fusion
  16.3 0.1 multiply_convert_fusion
  16.4 18.1 %collective-permute-start.2 = (bf16[6,512]{1,0:T(8,128)(2,1)S(1)}, bf16[6,512]{1,0:T(8,128)(2,1)S(1)}, u32[]{:S(2)}, u32[]{:S(2)}) collective-permute-start(bf16[6,512]{1,0:T(8,128)(2,1)S(1)} %multiply_convert_fusion), channel_id=1, source_target_pairs={{0,0},{1,64},{2,128},{3,192},{4,256},{5,320},{6,384},{7,448},{8,51... | collective-permute-start | bytes 18440 | tf_op jit(solution)/shard_map/ppermute | solution.py:61
  34.5 0.8 fusion.4
  35.2 2.2 %fusion = bf16[2304,512]{1,0:T(8,128)(2,1)} fusion(f32[2304,512]{1,0:T(8,128)S(1)} %fusion.4, bf16[128,2304]{0,1:T(8,128)(2,1)S(1)} %collective-permute-done, bf16[128,512]{1,0:T(8,128)(2,1)S(1)} %collective-permute-done.1), kind=kOutput, calls=%fused_computation.1 | convolution fusion | flops 304349184 | bytes 7798784 | tf_op jit(solution)/shard_map/dot_general | solution.py:50
  37.5 0.0 all-gather.2.cloned.1.call-start
  37.5 17.4 %all_to_all.20 = bf16[12,6,512]{2,1,0:T(8,128)(2,1)S(1)} all-to-all(bf16[12,6,512]{2,1,0:T(8,128)(2,1)S(1)} %broadcast_in_dim.24), channel_id=1, replica_groups=mesh['z'=12,'y'=8,'x'=4,'c'=2] {'z'}, dimensions={0} | all-to-all | bytes 147456 | tf_op jit(solution)/shard_map/all_to_all | solution.py:36
  55.0 23.3 %all_to_all.21 = bf16[8,72,512]{2,1,0:T(8,128)(2,1)} all-to-all(bf16[8,72,512]{2,1,0:T(8,128)(2,1)S(1)} %broadcast_in_dim.26), channel_id=1, replica_groups=mesh['z'=12,'y'=8,'x'=4,'c'=2] {'y'}, dimensions={0} | all-to-all | bytes 1179648 | tf_op jit(solution)/shard_map/all_to_all | solution.py:36
  78.4 23.7 %all_to_all.22 = bf16[8,72,512]{2,1,0:T(8,128)(2,1)S(1)} all-to-all(bf16[8,72,512]{2,1,0:T(8,128)(2,1)} %bitcast.19), channel_id=1, replica_groups=mesh['z'=12,'y'=8,'x'=4,'c'=2] {'y'}, dimensions={0} | all-to-all | bytes 1179648 | tf_op jit(solution)/shard_map/all_to_all | solution.py:41
  102.0 0.1 reduce_sum.21
  102.1 20.5 %all_to_all.23 = bf16[12,6,512]{2,1,0:T(8,128)(2,1)S(1)} all-to-all(bf16[12,6,512]{2,1,0:T(8,128)(2,1)S(1)} %reshape.40), channel_id=1, replica_groups=mesh['z'=12,'y'=8,'x'=4,'c'=2] {'z'}, dimensions={0} | all-to-all | bytes 147456 | tf_op jit(solution)/shard_map/all_to_all | solution.py:41
  122.7 2.3 %fusion.3 = f32[128,512]{1,0:T(8,128)S(1)} fusion(bf16[2304,512]{1,0:T(8,128)(2,1)} %all-gather.2.cloned.1.call-done, bf16[128,2304]{0,1:T(8,128)(2,1)S(1)} %copy.13, bf16[128,2304]{0,1:T(8,128)(2,1)S(1)} %copy.14, pred[]{:T(512)S(6)} %eq.13), kind=kOutput, calls=%fused_computation.12 | convolution fusion | flops 302284800 | bytes 3801089 | tf_op jit(solution)/shard_map/dot_general | solution.py:50
  125.1 0.5 fusion.7
  125.6 1.9 %collective-permute-start.3 = (f32[128,512]{1,0:T(8,128)S(1)}, f32[128,512]{1,0:T(8,128)S(1)}, u32[]{:S(2)}, u32[]{:S(2)}) collective-permute-start(f32[128,512]{1,0:T(8,128)S(1)} %fusion.7), channel_id=1, source_target_pairs={{0,1},{1,0},{2,3},{3,2},{4,5},{5,4},{6,7},{7,6},{8,9},{9,8},{10,11... | collective-permute-start | bytes 786440 | tf_op jit(solution)/shard_map/ppermute | solution.py:46
  127.5 0.8 fusion.2
  128.3 2.4 %collective-permute-start.4 = (bf16[128,2304]{0,1:T(8,128)(2,1)S(1)}, bf16[128,2304]{0,1:T(8,128)(2,1)S(1)}, u32[]{:S(2)}, u32[]{:S(2)}) collective-permute-start(bf16[128,2304]{0,1:T(8,128)(2,1)S(1)} %fusion.2), channel_id=1, source_target_pairs={{0,1},{1,0},{2,3},{3,2},{4,5},{5,4},{6,7},{7,6},{8,9},{9,8},{10,11... | collective-permute-start | bytes 1769480 | tf_op jit(solution)/shard_map/ppermute | solution.py:46
  130.7 3.4 %collective-permute-start.5 = (f32[6,512]{1,0:T(8,128)S(1)}, f32[6,512]{1,0:T(8,128)S(1)}, u32[]{:S(2)}, u32[]{:S(2)}) collective-permute-start(f32[6,512]{1,0:T(8,128)S(1)} %broadcast_multiply_fusion), channel_id=1, source_target_pairs={{0,0},{64,1},{128,2},{192,3},{256,4},{320,5},{384,6},{448,7},{512,... | collective-permute-start | bytes 36872 | tf_op jit(solution)/shard_map/ppermute | solution.py:74
  134.1 0.8 fusion.1
  134.9 12.7 %collective-permute-done.5 = f32[6,512]{1,0:T(8,128)S(1)} collective-permute-done((f32[6,512]{1,0:T(8,128)S(1)}, f32[6,512]{1,0:T(8,128)S(1)}, u32[]{:S(2)}, u32[]{:S(2)}) %collective-permute-start.5) | collective-permute-done | bytes 12320 | tf_op jit(solution)/shard_map/ppermute | solution.py:74
  147.6 0.7 add_convert_fusion
  148.3 0.1 broadcast_select_fusion.1
  148.4 0.1 pad_maximum_fusion
  148.5 1.4 copy.12
  149.9 0.6 copy.16
  (22 shorter events, 0.3 us)
Async XLA Ops:
  7.2 71.2 %reduce-scatter.2.cloned.1.call-start = ((), (), s32[]{:S(2)}) async-start(), calls=%async_computation.5 | async-start | bytes 2949120 | tf_op jit(solution)/shard_map/reduce_scatter | solution.py:65
  8.5 2.6 %copy-start.1 = (bf16[128,512]{1,0:T(8,128)(2,1)S(1)}, bf16[128,512]{1,0:T(8,128)(2,1)}, u32[]{:S(2)}) copy-start(bf16[128,512]{1,0:T(8,128)(2,1)} %param.7) | copy-start | bytes 393220
  8.5 7.8 %copy-start.2 = (bf16[6,512]{1,0:T(8,128)(2,1)S(1)}, bf16[6,512]{1,0:T(8,128)(2,1)}, u32[]{:S(2)}) copy-start(bf16[6,512]{1,0:T(8,128)(2,1)} %param.5) | copy-start | bytes 18436
  9.3 26.0 %collective-permute-start = (bf16[128,2304]{0,1:T(8,128)(2,1)S(1)}, bf16[128,2304]{0,1:T(8,128)(2,1)S(1)}, u32[]{:S(2)}, u32[]{:S(2)}) collective-permute-start(bf16[128,2304]{0,1:T(8,128)(2,1)S(1)} %broadcast_select_fusion.2), channel_id=1, source_target_pairs={{0,1},{1,0},{2,3},{3,2},{4,5},{5,4},{6,7},{7,6},{8,9},{9,8},{10,11... | collective-permute-start | bytes 1769480 | tf_op jit(solution)/shard_map/ppermute | solution.py:46
  11.2 24.0 %collective-permute-start.1 = (bf16[128,512]{1,0:T(8,128)(2,1)S(1)}, bf16[128,512]{1,0:T(8,128)(2,1)S(1)}, u32[]{:S(2)}, u32[]{:S(2)}) collective-permute-start(bf16[128,512]{1,0:T(8,128)(2,1)S(1)} %copy-done.1), channel_id=1, source_target_pairs={{0,1},{1,0},{2,3},{3,2},{4,5},{5,4},{6,7},{7,6},{8,9},{9,8},{10,11... | collective-permute-start | bytes 393224 | tf_op jit(solution)/shard_map/ppermute | solution.py:46
  16.4 21.0 %collective-permute-start.2 = (bf16[6,512]{1,0:T(8,128)(2,1)S(1)}, bf16[6,512]{1,0:T(8,128)(2,1)S(1)}, u32[]{:S(2)}, u32[]{:S(2)}) collective-permute-start(bf16[6,512]{1,0:T(8,128)(2,1)S(1)} %multiply_convert_fusion), channel_id=1, source_target_pairs={{0,0},{1,64},{2,128},{3,192},{4,256},{5,320},{6,384},{7,448},{8,51... | collective-permute-start | bytes 18440 | tf_op jit(solution)/shard_map/ppermute | solution.py:61
  37.5 85.3 %all-gather.2.cloned.1.call-start = ((), (), s32[]{:S(2)}) async-start(), calls=%async_computation.6 | async-start | bytes 2949120 | tf_op jit(solution)/shard_map/all_gather | solution.py:71
  122.7 2.4 %copy-start = (bf16[2304,512]{1,0:T(8,128)(2,1)S(1)}, bf16[2304,512]{1,0:T(8,128)(2,1)}, u32[]{:S(2)}) copy-start(bf16[2304,512]{1,0:T(8,128)(2,1)} %all-gather.2.cloned.1.call-done) | copy-start | bytes 7077892
  125.6 22.0 %collective-permute-start.3 = (f32[128,512]{1,0:T(8,128)S(1)}, f32[128,512]{1,0:T(8,128)S(1)}, u32[]{:S(2)}, u32[]{:S(2)}) collective-permute-start(f32[128,512]{1,0:T(8,128)S(1)} %fusion.7), channel_id=1, source_target_pairs={{0,1},{1,0},{2,3},{3,2},{4,5},{5,4},{6,7},{7,6},{8,9},{9,8},{10,11... | collective-permute-start | bytes 786440 | tf_op jit(solution)/shard_map/ppermute | solution.py:46
  128.3 20.0 %collective-permute-start.4 = (bf16[128,2304]{0,1:T(8,128)(2,1)S(1)}, bf16[128,2304]{0,1:T(8,128)(2,1)S(1)}, u32[]{:S(2)}, u32[]{:S(2)}) collective-permute-start(bf16[128,2304]{0,1:T(8,128)(2,1)S(1)} %fusion.2), channel_id=1, source_target_pairs={{0,1},{1,0},{2,3},{3,2},{4,5},{5,4},{6,7},{7,6},{8,9},{9,8},{10,11... | collective-permute-start | bytes 1769480 | tf_op jit(solution)/shard_map/ppermute | solution.py:46
  130.7 16.8 %collective-permute-start.5 = (f32[6,512]{1,0:T(8,128)S(1)}, f32[6,512]{1,0:T(8,128)S(1)}, u32[]{:S(2)}, u32[]{:S(2)}) collective-permute-start(f32[6,512]{1,0:T(8,128)S(1)} %broadcast_multiply_fusion), channel_id=1, source_target_pairs={{0,0},{64,1},{128,2},{192,3},{256,4},{320,5},{384,6},{448,7},{512,... | collective-permute-start | bytes 36872 | tf_op jit(solution)/shard_map/ppermute | solution.py:74
Sparse Core Ops, SparseCore 0:
  37.6 38.7 reduce-scatter.1
  78.7 41.2 all-gather.1

commit v3 on v1

v3 whole, which is shorter than its diff:
```python
import math

import jax
import jax.numpy as jnp
from jax import lax
from jax.experimental import pallas as pl
from jax.experimental.pallas import tpu as pltpu
from jax.sharding import Mesh, PartitionSpec as P

BLOCK_ROWS = 4
NZ, NY, NX, NC = 12, 8, 4, 2
AXES = ("z", "y", "x", "c")
BF16 = jnp.bfloat16
F32 = jnp.float32
PARAMS = pltpu.CompilerParams(vmem_limit_bytes=40 * 2**20)


def block_moves():
    moves = []
    for block in range(NZ * NY * NX * NC):
        rest, z = divmod(block, NZ)
        rest, y = divmod(rest, NY)
        c, x = divmod(rest, NX)
        moves.append((block, ((z * NY + y) * NX + x) * NC + c))
    return moves


def scaled_rows(w_values, w_scales):
    rows = w_values.shape[0]
    first = lax.axis_index(AXES) * rows
    start = first // BLOCK_ROWS
    pair = lax.dynamic_slice(w_scales, (start,), (2,))
    block = (first + lax.iota(jnp.int32, rows)) // BLOCK_ROWS - start
    scale = jnp.where(block == 0, pair[0], pair[1])
    return (w_values.astype(F32) * scale[:, None]).astype(BF16)


def swap(array):
    return lax.ppermute(array, "c", [(0, 1), (1, 0)])


def along_x(array, step):
    return lax.ppermute(array, "x", [(i, (i + step) % NX) for i in range(NX)])


def dot(a, b, over):
    return lax.dot_general(a, b, ((over[:1], over[1:]), ((), ())), preferred_element_type=F32)


def whole(shape):
    return pl.BlockSpec(shape, lambda i, place: (0,) * len(shape))


def call(kernel, outs, in_specs, scratch, flops, args):
    moved = sum(math.prod(s.shape) * s.dtype.itemsize for s in outs)
    return pl.pallas_call(
        kernel,
        out_shape=outs,
        grid_spec=pltpu.PrefetchScalarGridSpec(
            num_scalar_prefetch=1,
            grid=(1,),
            in_specs=in_specs,
            out_specs=[whole(s.shape) for s in outs],
            scratch_shapes=scratch,
        ),
        compiler_params=PARAMS,
        cost_estimate=pl.CostEstimate(flops=flops, bytes_accessed=2 * moved, transcendentals=0),
    )(*args)


def partials(place, tokens, grad, theirs):
    count, half = tokens.shape[0], tokens.shape[1] // NC
    cols = grad.shape[1]
    rows = half // NX
    chunk = 256

    def kernel(place_ref, tokens_ref, grad_ref, theirs_ref, *rest):
        outs, total = rest[:NX], rest[NX]
        grads = jnp.concatenate([grad_ref[...], theirs_ref[:, half:]], axis=0)
        for k in range(0, half, chunk):
            both = jnp.concatenate(
                [tokens_ref[:, k : k + chunk], theirs_ref[:, k : k + chunk]], axis=0
            )
            total[k : k + chunk] = dot(both, grads, (0, 0)).astype(BF16)
        x = place_ref[1]
        for step in range(NX):
            block = lax.rem(x + step, NX)
            outs[step][...] = total[pl.ds(pl.multiple_of(block * rows, rows), rows), :]

    return call(
        kernel,
        [jax.ShapeDtypeStruct((rows, cols), BF16)] * NX,
        [
            pl.BlockSpec((count, half), lambda i, place: (0, place[0])),
            whole(grad.shape),
            whole(theirs.shape),
        ],
        [pltpu.VMEM((half, cols), BF16)],
        4 * count * half * cols,
        (place, tokens, grad, theirs),
    )


def forward(place, tokens, grad, blocks, theirs=None):
    own = theirs is None
    half = blocks[0].shape[0] * NX
    rows, cols = blocks[0].shape
    count = tokens.shape[0] if own else theirs.shape[0]

    def kernel(place_ref, *refs):
        if own:
            tokens_ref, grad_ref, *block_refs, part_ref, out_ref, weights = refs
            token, gradient = tokens_ref[...], grad_ref[...]
        else:
            theirs_ref, *block_refs, out_ref, weights = refs
            token, gradient = theirs_ref[:, :half], theirs_ref[:, half:]
        x = place_ref[1]
        for step in range(NX):
            block = lax.rem(x + NX - step, NX)
            weights[pl.ds(pl.multiple_of(block * rows, rows), rows), :] = block_refs[step][...]
        part = dot(token, weights[...], (1, 0))
        columns = dot(gradient, weights[...], (1, 1)).astype(BF16)
        out_ref[:, :half] = columns
        if own:
            part_ref[...] = part
        else:
            out_ref[:, half:] = part.astype(BF16)

    block_specs = [whole(b.shape) for b in blocks]
    if own:
        outs = [
            jax.ShapeDtypeStruct((count, cols), F32),
            jax.ShapeDtypeStruct((count, half), BF16),
        ]
        specs = [
            pl.BlockSpec((count, half), lambda i, place: (0, place[0])),
            whole(grad.shape),
            *block_specs,
        ]
        args = (place, tokens, grad, *blocks)
    else:
        outs = [jax.ShapeDtypeStruct((count, half + cols), BF16)]
        specs = [whole(theirs.shape), *block_specs]
        args = (place, theirs, *blocks)
    return call(
        kernel, outs, specs, [pltpu.VMEM((half, cols), BF16)], 4 * count * half * cols, args
    )


def assemble(place, part, columns, received):
    count, half = columns.shape
    cols = part.shape[1]

    def kernel(place_ref, part_ref, columns_ref, received_ref, projected_ref, out_ref):
        projected_ref[...] = (part_ref[...] + received_ref[:, half:].astype(F32)).astype(BF16)
        core = place_ref[0]

        @pl.when(core == 0)
        def _():
            out_ref[:, :half] = columns_ref[...]
            out_ref[:, half:] = received_ref[:, :half]

        @pl.when(core == 1)
        def _():
            out_ref[:, :half] = received_ref[:, :half]
            out_ref[:, half:] = columns_ref[...]

    return call(
        kernel,
        [
            jax.ShapeDtypeStruct((count, cols), BF16),
            jax.ShapeDtypeStruct((count, NC * half), BF16),
        ],
        [whole(part.shape), whole(columns.shape), whole(received.shape)],
        [],
        count * cols,
        (place, part, columns, received),
    )


def body(tokens, w_values, w_scales, out_grad):
    moves = block_moves()
    core, x = lax.axis_index("c"), lax.axis_index("x")
    place = jnp.stack([core, x]).astype(jnp.int32)
    half = tokens.shape[1] // NC
    cols = out_grad.shape[1]
    others = lax.dynamic_slice(tokens, (0, (1 - core) * half), (tokens.shape[0], half))
    theirs = swap(jnp.concatenate([others, out_grad], axis=1))
    rows = lax.ppermute(scaled_rows(w_values, w_scales), AXES, moves)

    parts = partials(place, tokens, out_grad, theirs)
    rows, *parts = lax.optimization_barrier((rows, *parts))
    parts = [parts[0], *(along_x(parts[step], step) for step in range(1, NX))]

    rows = lax.all_to_all(jnp.broadcast_to(rows[None], (NZ, *rows.shape)), "z", 0, 0)
    rows = rows.reshape(-1, cols)
    total = sum(p.astype(F32) for p in parts).astype(BF16)
    both = jnp.concatenate(
        [
            total.reshape(NY, -1, cols),
            jnp.broadcast_to(rows[None], (NY, *rows.shape)),
        ],
        axis=1,
    )
    both = lax.all_to_all(both, "y", 0, 0)
    share = both.shape[1] // 2
    rows = both[:, share:].reshape(-1, cols)
    blocks = [rows, *(along_x(rows, step) for step in range(1, NX))]

    total = jnp.sum(both[:, :share].astype(F32), axis=0).astype(BF16)
    total = lax.all_to_all(total.reshape(NZ, -1, cols), "z", 0, 0)
    total = jnp.sum(total.astype(F32), axis=0)
    total, *blocks = lax.optimization_barrier((total, *blocks))
    count = tokens.shape[0] * NZ * NY * NX * NC
    weight_grad = lax.ppermute(
        total * (1.0 / math.sqrt(count)), AXES, [(b, a) for a, b in moves]
    )

    (for_them,) = forward(place, None, None, blocks, theirs)
    received = swap(for_them)
    part, columns = forward(place, tokens, out_grad, blocks)
    projected, token_grad = assemble(place, part, columns, received)
    return projected, token_grad, weight_grad


def solution(mesh):
    split = Mesh(mesh.devices.reshape(NZ, NY, NX, NC), AXES)
    by_rows = P(AXES, None)
    return jax.shard_map(
        body,
        mesh=split,
        in_specs=(by_rows, by_rows, P(), by_rows),
        out_specs=(by_rows, by_rows, by_rows),
        check_vma=False,
    )
```

time: 185 us -> 157 us (0.85)
  the two profiles are of different devices: /device:TPU:1 before, /device:TPU:67 now
where the time goes in v3:
time: 157 us; the launch traced here: 156 us
  blocking collectives  68.9 us (44%)
  starting transfers between devices  50 us (32%)
  waiting for transfers between devices  17.8 us (11%)
  Pallas kernels  8.21 us (5%)
  local copies, waits for them, and re-layouts  6 us (4%)
  other arithmetic  4.05 us (3%)
    all_to_all x1, blocking collectives, body(): both = lax.all_to_all(both, 'y', 0, 0)  32.8 us
    all_to_all x1, blocking collectives, body(): total = lax.all_to_all(total.reshape(NZ, -1, cols), 'z', 0, 0)  19.9 us
    ppermute x1, starting transfers between devices, body(): rows = lax.ppermute(scaled_rows(w_values, w_scales), AXES, moves)  18.3 us
    ppermute x6, starting transfers between devices, along_x(): return lax.ppermute(array, 'x', [(i, (i + step) % NX) for i in range(NX)])  17.6 us
    all_to_all x1, blocking collectives, body(): lax.all_to_all(jnp.broadcast_to(rows[None], (NZ, *rows.shape)), 'z', 0, 0)  16.1 us
    ppermute x6, waiting for transfers between devices, along_x(): return lax.ppermute(array, 'x', [(i, (i + step) % NX) for i in range(NX)])  12 us
    ppermute x1, starting transfers between devices, body(): lax.ppermute(total * (1.0 / math.sqrt(count)), AXES, [(b, a) for a, b in...  8.34 us
    pallas_call x4, Pallas kernels, call(): pl.pallas_call(kernel, out_shape=outs, grid_spec=pltpu.PrefetchScalarGrid...  8.21 us
  transfers between devices with their start and end apart: 10, of which 3 were waited for; matrix products, arithmetic and copies ran while one was open for 3% of the time, Pallas kernels for 3%

profile of v3, /device:TPU:67, one launch (start us, length us, event | category | flops | bytes accessed | tf_op | source)
XLA Modules:
  0.0 155.9 jit_solution(3791184440934067754)
XLA Ops:
  0.7 1.2 constant_dynamic-slice_fusion
  1.9 2.6 %collective-permute-start.1 = (bf16[128,2816]{1,0:T(8,128)(2,1)S(1)}, bf16[128,2816]{1,0:T(8,128)(2,1)S(1)}, u32[]{:S(2)}, u32[]{:S(2)}) collective-permute-start(bf16[128,2816]{1,0:T(8,128)(2,1)S(1)} %pad_maximum_fusion.1), channel_id=1, source_target_pairs={{0,1},{1,0},{2,3},{3,2},{4,5},{5,4},{6,7},{7,6},{8,9},{9,8},{10,11... | collective-permute-start | bytes 2162696 | tf_op jit(solution)/shard_map/ppermute | solution.py:39
  4.6 0.8 dynamic_slice.6
  5.4 0.6 fusion.1
  6.0 1.3 compare_select_fusion
  7.3 0.1 multiply_convert_fusion
  7.4 18.3 %collective-permute-start = (bf16[6,512]{1,0:T(8,128)(2,1)S(1)}, bf16[6,512]{1,0:T(8,128)(2,1)S(1)}, u32[]{:S(2)}, u32[]{:S(2)}) collective-permute-start(bf16[6,512]{1,0:T(8,128)(2,1)S(1)} %multiply_convert_fusion), channel_id=1, source_target_pairs={{0,0},{1,64},{2,128},{3,192},{4,256},{5,320},{6,384},{7,448},{8,51... | collective-permute-start | bytes 18440 | tf_op jit(solution)/shard_map/ppermute | solution.py:189
  25.7 0.1 pad_add_fusion.place_ref
  25.8 2.5 %shard_map.67 = (bf16[576,512]{1,0:T(8,128)(2,1)S(1)}, bf16[576,512]{1,0:T(8,128)(2,1)}, bf16[576,512]{1,0:T(8,128)(2,1)}, bf16[576,512]{1,0:T(8,128)(2,1)S(1)}) custom-call(s32[2]{0:T(128)S(1)} %pad_add_fusion.place_ref, bf16[128,4608]{1,0:T(8,128)(2,1)S(1)} %copy-done, bf16[128,512]{1,0:T(8,128)(2,1)S(1)} %copy-done.3, ...), custom_call_target="tpu_custom_call" | custom-call | flops 603979776 | bytes 4718592 | tf_op jit(solution)/shard_map/pallas_call | solution.py:56
  28.3 2.5 %collective-permute-start.2 = (bf16[576,512]{1,0:T(8,128)(2,1)}, bf16[576,512]{1,0:T(8,128)(2,1)}, u32[]{:S(2)}, u32[]{:S(2)}) collective-permute-start(bf16[576,512]{1,0:T(8,128)(2,1)} %get-tuple-element.26), channel_id=1, source_target_pairs={{0,2},{2,4},{4,6},{6,0},{1,3},{3,5},{5,7},{7,1},{8,10},{10,12},{12... | collective-permute-start | bytes 1769480 | tf_op jit(solution)/shard_map/ppermute | solution.py:43
  30.8 2.6 %collective-permute-start.3 = (bf16[576,512]{1,0:T(8,128)(2,1)}, bf16[576,512]{1,0:T(8,128)(2,1)}, u32[]{:S(2)}, u32[]{:S(2)}) collective-permute-start(bf16[576,512]{1,0:T(8,128)(2,1)} %get-tuple-element.27), channel_id=1, source_target_pairs={{0,4},{2,6},{4,0},{6,2},{1,5},{3,7},{5,1},{7,3},{8,12},{10,14},{12... | collective-permute-start | bytes 1769480 | tf_op jit(solution)/shard_map/ppermute | solution.py:43
  33.4 4.0 %collective-permute-start.4 = (bf16[576,512]{1,0:T(8,128)(2,1)S(1)}, bf16[576,512]{1,0:T(8,128)(2,1)}, u32[]{:S(2)}, u32[]{:S(2)}) collective-permute-start(bf16[576,512]{1,0:T(8,128)(2,1)S(1)} %get-tuple-element.28), channel_id=1, source_target_pairs={{0,6},{2,0},{4,2},{6,4},{1,7},{3,1},{5,3},{7,5},{8,14},{10,8},{12,... | collective-permute-start | bytes 1769480 | tf_op jit(solution)/shard_map/ppermute | solution.py:43
  37.4 16.1 %all_to_all.15 = bf16[12,6,512]{2,1,0:T(8,128)(2,1)S(1)} all-to-all(bf16[12,6,512]{2,1,0:T(8,128)(2,1)S(1)} %broadcast_in_dim.24), channel_id=1, replica_groups=mesh['z'=12,'y'=8,'x'=4,'c'=2] {'z'}, dimensions={0} | all-to-all | bytes 147456 | tf_op jit(solution)/shard_map/all_to_all | solution.py:195
  53.5 8.9 %collective-permute-done.4 = bf16[576,512]{1,0:T(8,128)(2,1)} collective-permute-done((bf16[576,512]{1,0:T(8,128)(2,1)S(1)}, bf16[576,512]{1,0:T(8,128)(2,1)}, u32[]{:S(2)}, u32[]{:S(2)}) %collective-permute-start.4) | collective-permute-done | bytes 589856 | tf_op jit(solution)/shard_map/ppermute | solution.py:43
  62.4 1.7 %add_convert_fusion = bf16[576,512]{1,0:T(8,128)(2,1)S(1)} fusion(bf16[576,512]{1,0:T(8,128)(2,1)} %collective-permute-done.4, bf16[576,512]{1,0:T(8,128)(2,1)} %collective-permute-done.3, bf16[576,512]{1,0:T(8,128)(2,1)} %collective-permute-done.2, bf16[576,512]{1,0:T(8,128)(2,1)S(1)} %get-tuple-element.25), kind=kLoop, calls=%fused_computation.1 | loop fusion | flops 2359296 | bytes 2949120 | tf_op jit(solution)/shard_map/convert_element_type | solution.py:197
  64.2 0.1 pad_maximum_fusion
  64.3 32.8 %all_to_all.16 = bf16[8,144,512]{2,1,0:T(8,128)(2,1)S(1)} all-to-all(bf16[8,144,512]{2,1,0:T(8,128)(2,1)S(1)} %pad_maximum_fusion), channel_id=1, replica_groups=mesh['z'=12,'y'=8,'x'=4,'c'=2] {'y'}, dimensions={0} | all-to-all | bytes 2359296 | tf_op jit(solution)/shard_map/all_to_all | solution.py:205
  97.1 0.7 fusion
  97.8 1.9 %collective-permute-start.5 = (bf16[576,512]{1,0:T(8,128)(2,1)S(1)}, bf16[576,512]{1,0:T(8,128)(2,1)S(1)}, u32[]{:S(2)}, u32[]{:S(2)}) collective-permute-start(bf16[576,512]{1,0:T(8,128)(2,1)S(1)} %bitcast.6), channel_id=1, source_target_pairs={{0,2},{2,4},{4,6},{6,0},{1,3},{3,5},{5,7},{7,1},{8,10},{10,12},{12... | collective-permute-start | bytes 1769480 | tf_op jit(solution)/shard_map/ppermute | solution.py:43
  99.8 2.7 %collective-permute-start.6 = (bf16[576,512]{1,0:T(8,128)(2,1)S(1)}, bf16[576,512]{1,0:T(8,128)(2,1)S(1)}, u32[]{:S(2)}, u32[]{:S(2)}) collective-permute-start(bf16[576,512]{1,0:T(8,128)(2,1)S(1)} %bitcast.7), channel_id=1, source_target_pairs={{0,4},{2,6},{4,0},{6,2},{1,5},{3,7},{5,1},{7,3},{8,12},{10,14},{12... | collective-permute-start | bytes 1769480 | tf_op jit(solution)/shard_map/ppermute | solution.py:43
  102.4 4.0 %collective-permute-start.7 = (bf16[576,512]{1,0:T(8,128)(2,1)S(1)}, bf16[576,512]{1,0:T(8,128)(2,1)S(1)}, u32[]{:S(2)}, u32[]{:S(2)}) collective-permute-start(bf16[576,512]{1,0:T(8,128)(2,1)S(1)} %bitcast.8), channel_id=1, source_target_pairs={{0,6},{2,0},{4,2},{6,4},{1,7},{3,1},{5,3},{7,5},{8,14},{10,8},{12,... | collective-permute-start | bytes 1769480 | tf_op jit(solution)/shard_map/ppermute | solution.py:43
  106.4 1.6 reshape.40
  108.0 19.9 %all_to_all.17 = bf16[12,6,512]{2,1,0:T(8,128)(2,1)S(1)} all-to-all(bf16[12,6,512]{2,1,0:T(8,128)(2,1)} %reshape.40), channel_id=1, replica_groups=mesh['z'=12,'y'=8,'x'=4,'c'=2] {'z'}, dimensions={0} | all-to-all | bytes 147456 | tf_op jit(solution)/shard_map/all_to_all | solution.py:211
  127.9 3.1 %collective-permute-done.7.refs_5_.refs_4_ = bf16[576,512]{1,0:T(8,128)(2,1)S(1)} collective-permute-done((bf16[576,512]{1,0:T(8,128)(2,1)S(1)}, bf16[576,512]{1,0:T(8,128)(2,1)S(1)}, u32[]{:S(2)}, u32[]{:S(2)}) %collective-permute-start.7) | collective-permute-done | bytes 589856 | tf_op jit(solution)/shard_map/ppermute | solution.py:43
  131.1 1.1 copy-done.2
  132.2 2.0 %shard_map.69 = bf16[128,2816]{1,0:T(8,128)(2,1)S(1)} custom-call(s32[2]{0:T(128)S(1)} %pad_add_fusion.place_ref, bf16[128,2816]{1,0:T(8,128)(2,1)S(1)} %copy-done.2, bf16[576,512]{1,0:T(8,128)(2,1)S(1)} %bitcast.9, bf16[576,512]{1,0:T(8,128)(2,1)S(1)} %collective-permute-done.5.refs_3_.refs_2_, bf16[576,512]{1,0:T(8,128)(2,1)S(1)} %collective-permute-done.6.refs_4_.refs_3_, ...), custom_call_target="tpu_custom_call" | custom-call | flops 603979776 | bytes 1441792 | tf_op jit(solution)/shard_map/pallas_call | solution.py:56
  134.2 3.2 %collective-permute-start.8 = (bf16[128,2816]{1,0:T(8,128)(2,1)S(1)}, bf16[128,2816]{1,0:T(8,128)(2,1)S(1)}, u32[]{:S(2)}, u32[]{:S(2)}) collective-permute-start(bf16[128,2816]{1,0:T(8,128)(2,1)S(1)} %shard_map.69), channel_id=1, source_target_pairs={{0,1},{1,0},{2,3},{3,2},{4,5},{5,4},{6,7},{7,6},{8,9},{9,8},{10,11... | collective-permute-start | bytes 2162696 | tf_op jit(solution)/shard_map/ppermute | solution.py:39
  137.4 8.3 %collective-permute-start.9 = (f32[6,512]{1,0:T(8,128)S(1)}, f32[6,512]{1,0:T(8,128)S(1)}, u32[]{:S(2)}, u32[]{:S(2)}) collective-permute-start(f32[6,512]{1,0:T(8,128)S(1)} %broadcast_multiply_fusion), channel_id=1, source_target_pairs={{0,0},{64,1},{128,2},{192,3},{256,4},{320,5},{384,6},{448,7},{512,... | collective-permute-start | bytes 36872 | tf_op jit(solution)/shard_map/ppermute | solution.py:215
  145.8 2.0 %shard_map.68 = (f32[128,512]{1,0:T(8,128)S(1)}, bf16[128,2304]{1,0:T(8,128)(2,1)S(1)}) custom-call(s32[2]{0:T(128)S(1)} %pad_add_fusion.place_ref, bf16[128,4608]{1,0:T(8,128)(2,1)S(1)} %copy-done, bf16[128,512]{1,0:T(8,128)(2,1)S(1)} %copy-done.4, bf16[576,512]{1,0:T(8,128)(2,1)S(1)} %bitcast.10, ...), custom_call_target="tpu_custom_call" | custom-call | flops 603979776 | bytes 1703936 | tf_op jit(solution)/shard_map/pallas_call | solution.py:56
  147.8 5.8 %collective-permute-done.9 = f32[6,512]{1,0:T(8,128)S(1)} collective-permute-done((f32[6,512]{1,0:T(8,128)S(1)}, f32[6,512]{1,0:T(8,128)S(1)}, u32[]{:S(2)}, u32[]{:S(2)}) %collective-permute-start.9) | collective-permute-done | bytes 12320 | tf_op jit(solution)/shard_map/ppermute | solution.py:215
  153.6 1.7 %shard_map.70 = (bf16[128,512]{1,0:T(8,128)(2,1)}, bf16[128,4608]{1,0:T(8,128)(2,1)}) custom-call(s32[2]{0:T(128)S(1)} %pad_add_fusion.place_ref, f32[128,512]{1,0:T(8,128)S(1)} %get-tuple-element.34.part_ref, bf16[128,2304]{1,0:T(8,128)(2,1)S(1)} %get-tuple-element.35.columns_ref, bf16[128,2816]{1,0:T(8,128)(2,1)S(1)} %collective-permute-done.8.received_ref), custom_call_target="tpu_custom_call" | custom-call | flops 65536 | bytes 2621440 | tf_op jit(solution)/shard_map/pallas_call | solution.py:56
  155.3 0.6 copy.8
  (24 shorter events, 0.2 us)
Async XLA Ops:
  0.6 1.3 copy-start.3
  0.6 6.6 %copy-start.5 = (bf16[6,512]{1,0:T(8,128)(2,1)S(1)}, bf16[6,512]{1,0:T(8,128)(2,1)}, u32[]{:S(2)}) copy-start(bf16[6,512]{1,0:T(8,128)(2,1)} %param.5) | copy-start | bytes 18436
  0.7 25.1 %copy-start = (bf16[128,4608]{1,0:T(8,128)(2,1)S(1)}, bf16[128,4608]{1,0:T(8,128)(2,1)}, u32[]{:S(2)}) copy-start(bf16[128,4608]{1,0:T(8,128)(2,1)} %refs_0_.1) | copy-start | bytes 3538948
  1.9 23.8 %collective-permute-start.1 = (bf16[128,2816]{1,0:T(8,128)(2,1)S(1)}, bf16[128,2816]{1,0:T(8,128)(2,1)S(1)}, u32[]{:S(2)}, u32[]{:S(2)}) collective-permute-start(bf16[128,2816]{1,0:T(8,128)(2,1)S(1)} %pad_maximum_fusion.1), channel_id=1, source_target_pairs={{0,1},{1,0},{2,3},{3,2},{4,5},{5,4},{6,7},{7,6},{8,9},{9,8},{10,11... | collective-permute-start | bytes 2162696 | tf_op jit(solution)/shard_map/ppermute | solution.py:39
  7.4 20.9 %collective-permute-start = (bf16[6,512]{1,0:T(8,128)(2,1)S(1)}, bf16[6,512]{1,0:T(8,128)(2,1)S(1)}, u32[]{:S(2)}, u32[]{:S(2)}) collective-permute-start(bf16[6,512]{1,0:T(8,128)(2,1)S(1)} %multiply_convert_fusion), channel_id=1, source_target_pairs={{0,0},{1,64},{2,128},{3,192},{4,256},{5,320},{6,384},{7,448},{8,51... | collective-permute-start | bytes 18440 | tf_op jit(solution)/shard_map/ppermute | solution.py:189
  25.8 27.7 %copy-start.1 = (bf16[128,2816]{1,0:T(8,128)(2,1)}, bf16[128,2816]{1,0:T(8,128)(2,1)S(1)}, u32[]{:S(2)}) copy-start(bf16[128,2816]{1,0:T(8,128)(2,1)S(1)} %collective-permute-done.1.theirs_ref.refs_0_) | copy-start | bytes 2162692
  28.3 25.3 %collective-permute-start.2 = (bf16[576,512]{1,0:T(8,128)(2,1)}, bf16[576,512]{1,0:T(8,128)(2,1)}, u32[]{:S(2)}, u32[]{:S(2)}) collective-permute-start(bf16[576,512]{1,0:T(8,128)(2,1)} %get-tuple-element.26), channel_id=1, source_target_pairs={{0,2},{2,4},{4,6},{6,0},{1,3},{3,5},{5,7},{7,1},{8,10},{10,12},{12... | collective-permute-start | bytes 1769480 | tf_op jit(solution)/shard_map/ppermute | solution.py:43
  30.8 22.7 %collective-permute-start.3 = (bf16[576,512]{1,0:T(8,128)(2,1)}, bf16[576,512]{1,0:T(8,128)(2,1)}, u32[]{:S(2)}, u32[]{:S(2)}) collective-permute-start(bf16[576,512]{1,0:T(8,128)(2,1)} %get-tuple-element.27), channel_id=1, source_target_pairs={{0,4},{2,6},{4,0},{6,2},{1,5},{3,7},{5,1},{7,3},{8,12},{10,14},{12... | collective-permute-start | bytes 1769480 | tf_op jit(solution)/shard_map/ppermute | solution.py:43
  33.4 29.0 %collective-permute-start.4 = (bf16[576,512]{1,0:T(8,128)(2,1)S(1)}, bf16[576,512]{1,0:T(8,128)(2,1)}, u32[]{:S(2)}, u32[]{:S(2)}) collective-permute-start(bf16[576,512]{1,0:T(8,128)(2,1)S(1)} %get-tuple-element.28), channel_id=1, source_target_pairs={{0,6},{2,0},{4,2},{6,4},{1,7},{3,1},{5,3},{7,5},{8,14},{10,8},{12,... | collective-permute-start | bytes 1769480 | tf_op jit(solution)/shard_map/ppermute | solution.py:43
  97.8 30.1 %collective-permute-start.5 = (bf16[576,512]{1,0:T(8,128)(2,1)S(1)}, bf16[576,512]{1,0:T(8,128)(2,1)S(1)}, u32[]{:S(2)}, u32[]{:S(2)}) collective-permute-start(bf16[576,512]{1,0:T(8,128)(2,1)S(1)} %bitcast.6), channel_id=1, source_target_pairs={{0,2},{2,4},{4,6},{6,0},{1,3},{3,5},{5,7},{7,1},{8,10},{10,12},{12... | collective-permute-start | bytes 1769480 | tf_op jit(solution)/shard_map/ppermute | solution.py:43
  99.8 28.2 %collective-permute-start.6 = (bf16[576,512]{1,0:T(8,128)(2,1)S(1)}, bf16[576,512]{1,0:T(8,128)(2,1)S(1)}, u32[]{:S(2)}, u32[]{:S(2)}) collective-permute-start(bf16[576,512]{1,0:T(8,128)(2,1)S(1)} %bitcast.7), channel_id=1, source_target_pairs={{0,4},{2,6},{4,0},{6,2},{1,5},{3,7},{5,1},{7,3},{8,12},{10,14},{12... | collective-permute-start | bytes 1769480 | tf_op jit(solution)/shard_map/ppermute | solution.py:43
  102.4 28.6 %collective-permute-start.7 = (bf16[576,512]{1,0:T(8,128)(2,1)S(1)}, bf16[576,512]{1,0:T(8,128)(2,1)S(1)}, u32[]{:S(2)}, u32[]{:S(2)}) collective-permute-start(bf16[576,512]{1,0:T(8,128)(2,1)S(1)} %bitcast.8), channel_id=1, source_target_pairs={{0,6},{2,0},{4,2},{6,4},{1,7},{3,1},{5,3},{7,5},{8,14},{10,8},{12,... | collective-permute-start | bytes 1769480 | tf_op jit(solution)/shard_map/ppermute | solution.py:43
  108.0 37.8 %copy-start.4 = (bf16[128,512]{1,0:T(8,128)(2,1)S(1)}, bf16[128,512]{1,0:T(8,128)(2,1)}, u32[]{:S(2)}) copy-start(bf16[128,512]{1,0:T(8,128)(2,1)} %refs_1_.1) | copy-start | bytes 393220
  131.1 1.1 copy-start.2
  134.2 19.4 %collective-permute-start.8 = (bf16[128,2816]{1,0:T(8,128)(2,1)S(1)}, bf16[128,2816]{1,0:T(8,128)(2,1)S(1)}, u32[]{:S(2)}, u32[]{:S(2)}) collective-permute-start(bf16[128,2816]{1,0:T(8,128)(2,1)S(1)} %shard_map.69), channel_id=1, source_target_pairs={{0,1},{1,0},{2,3},{3,2},{4,5},{5,4},{6,7},{7,6},{8,9},{9,8},{10,11... | collective-permute-start | bytes 2162696 | tf_op jit(solution)/shard_map/ppermute | solution.py:39
  137.4 16.2 %collective-permute-start.9 = (f32[6,512]{1,0:T(8,128)S(1)}, f32[6,512]{1,0:T(8,128)S(1)}, u32[]{:S(2)}, u32[]{:S(2)}) collective-permute-start(f32[6,512]{1,0:T(8,128)S(1)} %broadcast_multiply_fusion), channel_id=1, source_target_pairs={{0,0},{64,1},{128,2},{192,3},{256,4},{320,5},{384,6},{448,7},{512,... | collective-permute-start | bytes 36872 | tf_op jit(solution)/shard_map/ppermute | solution.py:215

commit v4 on v3

--- a/solution.py
+++ b/solution.py
@@ -10,6 +10,7 @@
 BLOCK_ROWS = 4
 NZ, NY, NX, NC = 12, 8, 4, 2
 AXES = ("z", "y", "x", "c")
+PLANE = ("z", "y")
 BF16 = jnp.bfloat16
 F32 = jnp.float32
 PARAMS = pltpu.CompilerParams(vmem_limit_bytes=40 * 2**20)
@@ -18,8 +19,8 @@
 def block_moves():
     moves = []
     for block in range(NZ * NY * NX * NC):
-        rest, z = divmod(block, NZ)
-        rest, y = divmod(rest, NY)
+        rest, y = divmod(block, NY)
+        rest, z = divmod(rest, NZ)
         c, x = divmod(rest, NX)
         moves.append((block, ((z * NY + y) * NX + x) * NC + c))
     return moves
@@ -47,25 +48,22 @@
     return lax.dot_general(a, b, ((over[:1], over[1:]), ((), ())), preferred_element_type=F32)
 
 
-def whole(shape):
-    return pl.BlockSpec(shape, lambda i, place: (0,) * len(shape))
-
-
-def call(kernel, outs, in_specs, scratch, flops, args):
+def call(kernel, outs, scratch, flops, place, *args):
     moved = sum(math.prod(s.shape) * s.dtype.itemsize for s in outs)
+    vmem = pl.BlockSpec(memory_space=pltpu.VMEM)
     return pl.pallas_call(
         kernel,
         out_shape=outs,
-        grid_spec=pltpu.PrefetchScalarGridSpec(
-            num_scalar_prefetch=1,
-            grid=(1,),
-            in_specs=in_specs,
-            out_specs=[whole(s.shape) for s in outs],
-            scratch_shapes=scratch,
-        ),
+        in_specs=[pl.BlockSpec(memory_space=pltpu.SMEM), *[vmem] * len(args)],
+        out_specs=[vmem] * len(outs),
+        scratch_shapes=scratch,
         compiler_params=PARAMS,
         cost_estimate=pl.CostEstimate(flops=flops, bytes_accessed=2 * moved, transcendentals=0),
-    )(*args)
+    )(place, *args)
+
+
+def core_columns(place_ref, half):
+    return pl.multiple_of(place_ref[0] * half, half)
 
 
 def partials(place, tokens, grad, theirs):
@@ -77,10 +75,10 @@
     def kernel(place_ref, tokens_ref, grad_ref, theirs_ref, *rest):
         outs, total = rest[:NX], rest[NX]
         grads = jnp.concatenate([grad_ref[...], theirs_ref[:, half:]], axis=0)
+        first = core_columns(place_ref, half)
         for k in range(0, half, chunk):
-            both = jnp.concatenate(
-                [tokens_ref[:, k : k + chunk], theirs_ref[:, k : k + chunk]], axis=0
-            )
+            mine = tokens_ref[:, pl.ds(pl.multiple_of(first + k, chunk), chunk)]
+            both = jnp.concatenate([mine, theirs_ref[:, k : k + chunk]], axis=0)
             total[k : k + chunk] = dot(both, grads, (0, 0)).astype(BF16)
         x = place_ref[1]
         for step in range(NX):
@@ -90,14 +88,12 @@
     return call(
         kernel,
         [jax.ShapeDtypeStruct((rows, cols), BF16)] * NX,
-        [
-            pl.BlockSpec((count, half), lambda i, place: (0, place[0])),
-            whole(grad.shape),
-            whole(theirs.shape),
-        ],
         [pltpu.VMEM((half, cols), BF16)],
         4 * count * half * cols,
-        (place, tokens, grad, theirs),
+        place,
+        tokens,
+        grad,
+        theirs,
     )
 
 
@@ -110,7 +106,8 @@
     def kernel(place_ref, *refs):
         if own:
             tokens_ref, grad_ref, *block_refs, part_ref, out_ref, weights = refs
-            token, gradient = tokens_ref[...], grad_ref[...]
+            token = tokens_ref[:, pl.ds(core_columns(place_ref, half), half)]
+            gradient = grad_ref[...]
         else:
             theirs_ref, *block_refs, out_ref, weights = refs
             token, gradient = theirs_ref[:, :half], theirs_ref[:, half:]
@@ -126,24 +123,17 @@
         else:
             out_ref[:, half:] = part.astype(BF16)
 
-    block_specs = [whole(b.shape) for b in blocks]
     if own:
         outs = [
             jax.ShapeDtypeStruct((count, cols), F32),
             jax.ShapeDtypeStruct((count, half), BF16),
         ]
-        specs = [
-            pl.BlockSpec((count, half), lambda i, place: (0, place[0])),
-            whole(grad.shape),
-            *block_specs,
-        ]
-        args = (place, tokens, grad, *blocks)
+        args = (tokens, grad, *blocks)
     else:
         outs = [jax.ShapeDtypeStruct((count, half + cols), BF16)]
-        specs = [whole(theirs.shape), *block_specs]
-        args = (place, theirs, *blocks)
+        args = (theirs, *blocks)
     return call(
-        kernel, outs, specs, [pltpu.VMEM((half, cols), BF16)], 4 * count * half * cols, args
+        kernel, outs, [pltpu.VMEM((half, cols), BF16)], 4 * count * half * cols, place, *args
     )
 
 
@@ -171,10 +161,12 @@
             jax.ShapeDtypeStruct((count, cols), BF16),
             jax.ShapeDtypeStruct((count, NC * half), BF16),
         ],
-        [whole(part.shape), whole(columns.shape), whole(received.shape)],
         [],
         count * cols,
-        (place, part, columns, received),
+        place,
+        part,
+        columns,
+        received,
     )
 
 
@@ -192,23 +184,12 @@
     rows, *parts = lax.optimization_barrier((rows, *parts))
     parts = [parts[0], *(along_x(parts[step], step) for step in range(1, NX))]
 
-    rows = lax.all_to_all(jnp.broadcast_to(rows[None], (NZ, *rows.shape)), "z", 0, 0)
+    rows = lax.all_to_all(jnp.broadcast_to(rows[None], (NZ * NY, *rows.shape)), PLANE, 0, 0)
     rows = rows.reshape(-1, cols)
     total = sum(p.astype(F32) for p in parts).astype(BF16)
-    both = jnp.concatenate(
-        [
-            total.reshape(NY, -1, cols),
-            jnp.broadcast_to(rows[None], (NY, *rows.shape)),
-        ],
-        axis=1,
-    )
-    both = lax.all_to_all(both, "y", 0, 0)
-    share = both.shape[1] // 2
-    rows = both[:, share:].reshape(-1, cols)
+    total, rows = lax.optimization_barrier((total, rows))
     blocks = [rows, *(along_x(rows, step) for step in range(1, NX))]
-
-    total = jnp.sum(both[:, :share].astype(F32), axis=0).astype(BF16)
-    total = lax.all_to_all(total.reshape(NZ, -1, cols), "z", 0, 0)
+    total = lax.all_to_all(total.reshape(NZ * NY, -1, cols), PLANE, 0, 0)
     total = jnp.sum(total.astype(F32), axis=0)
     total, *blocks = lax.optimization_barrier((total, *blocks))
     count = tokens.shape[0] * NZ * NY * NX * NC

time: 157 us -> 152 us (0.968)
  the two profiles are of different devices: /device:TPU:67 before, /device:TPU:3 now
where the time goes in v4:
time: 152 us
  starting transfers between devices  76.1 us (50%)
  waiting for transfers between devices  58 us (38%)
  Pallas kernels  7.17 us (5%)
  local copies, waits for them, and re-layouts  6.29 us (4%)
  other arithmetic  3.2 us (2%)
    ppermute x6, waiting for transfers between devices, along_x(): return lax.ppermute(array, 'x', [(i, (i + step) % NX) for i in range(NX)])  22.9 us
    ppermute x6, starting transfers between devices, along_x(): return lax.ppermute(array, 'x', [(i, (i + step) % NX) for i in range(NX)])  21.7 us
    all_to_all x1, waiting for transfers between devices, body(): total = lax.all_to_all(total.reshape(NZ * NY, -1, cols), PLANE, 0, 0)  20.6 us
    all_to_all x1, starting transfers between devices, body(): total = lax.all_to_all(total.reshape(NZ * NY, -1, cols), PLANE, 0, 0)  15.1 us
    ppermute x1, waiting for transfers between devices, body(): rows = lax.ppermute(scaled_rows(w_values, w_scales), AXES, moves)  14.4 us
    ppermute x1, starting transfers between devices, body(): lax.ppermute(total * (1.0 / math.sqrt(count)), AXES, [(b, a) for a, b in...  13.3 us
    all_to_all x1, starting transfers between devices, body(): lax.all_to_all(jnp.broadcast_to(rows[None], (NZ * NY, *rows.shape)), PLAN...  11.9 us
    ppermute x2, starting transfers between devices, swap(): return lax.ppermute(array, 'c', [(0, 1), (1, 0)])  9.01 us
  transfers between devices with their start and end apart: 12, of which 6 were waited for; matrix products, arithmetic and copies ran while one was open for 3% of the time, Pallas kernels for 2%

profile of v4, /device:TPU:3, one launch (start us, length us, event | category | flops | bytes accessed | tf_op | source)
XLA Modules:
  0.0 151.7 jit_solution(12354219834233936545)
XLA Ops:
  0.7 1.2 constant_dynamic-slice_fusion
  1.9 2.6 %collective-permute-start.1 = (bf16[128,2816]{1,0:T(8,128)(2,1)S(1)}, bf16[128,2816]{1,0:T(8,128)(2,1)S(1)}, u32[]{:S(2)}, u32[]{:S(2)}) collective-permute-start(bf16[128,2816]{1,0:T(8,128)(2,1)S(1)} %pad_maximum_fusion), channel_id=1, source_target_pairs={{0,1},{1,0},{2,3},{3,2},{4,5},{5,4},{6,7},{7,6},{8,9},{9,8},{10,11... | collective-permute-start | bytes 2162696 | tf_op jit(solution)/shard_map/ppermute | solution.py:40
  4.6 0.8 dynamic_slice.6
  5.4 0.6 fusion
  6.0 1.3 compare_select_fusion
  7.4 5.1 %collective-permute-start = (bf16[6,512]{1,0:T(8,128)(2,1)S(1)}, bf16[6,512]{1,0:T(8,128)(2,1)S(1)}, u32[]{:S(2)}, u32[]{:S(2)}) collective-permute-start(bf16[6,512]{1,0:T(8,128)(2,1)S(1)} %multiply_convert_fusion), channel_id=1, source_target_pairs={{0,0},{1,8},{2,16},{3,24},{4,32},{5,40},{6,48},{7,56},{8,64},{9,72... | collective-permute-start | bytes 18440 | tf_op jit(solution)/shard_map/ppermute | solution.py:181
  12.6 1.5 shard_map.67
  14.1 0.8 copy-done.5
  14.9 14.4 %collective-permute-done = bf16[6,512]{1,0:T(8,128)(2,1)S(1)} collective-permute-done((bf16[6,512]{1,0:T(8,128)(2,1)S(1)}, bf16[6,512]{1,0:T(8,128)(2,1)S(1)}, u32[]{:S(2)}, u32[]{:S(2)}) %collective-permute-start) | collective-permute-done | bytes 6176 | tf_op jit(solution)/shard_map/ppermute | solution.py:181
  29.3 0.9 broadcast_in_dim.17
  30.2 11.9 %all-to-all-start = ((bf16[96,6,512]{2,1,0:T(8,128)(2,1)}), bf16[96,6,512]{2,1,0:T(8,128)(2,1)S(1)}, u32[]{:S(2)}, u32[]{:S(2)}) async-start(bf16[96,6,512]{2,1,0:T(8,128)(2,1)} %broadcast_in_dim.17), calls=%async_computation | async-start | bytes 1572864 | tf_op jit(solution)/shard_map/all_to_all | solution.py:187
  42.1 1.9 %collective-permute-start.2 = (bf16[576,512]{1,0:T(8,128)(2,1)}, bf16[576,512]{1,0:T(8,128)(2,1)S(1)}, u32[]{:S(2)}, u32[]{:S(2)}) collective-permute-start(bf16[576,512]{1,0:T(8,128)(2,1)} %copy-done.6), channel_id=1, source_target_pairs={{0,2},{2,4},{4,6},{6,0},{1,3},{3,5},{5,7},{7,1},{8,10},{10,12},{12... | collective-permute-start | bytes 1769480 | tf_op jit(solution)/shard_map/ppermute | solution.py:44
  44.1 4.7 %collective-permute-start.3 = (bf16[576,512]{1,0:T(8,128)(2,1)}, bf16[576,512]{1,0:T(8,128)(2,1)S(1)}, u32[]{:S(2)}, u32[]{:S(2)}) collective-permute-start(bf16[576,512]{1,0:T(8,128)(2,1)} %copy-done.5), channel_id=1, source_target_pairs={{0,4},{2,6},{4,0},{6,2},{1,5},{3,7},{5,1},{7,3},{8,12},{10,14},{12... | collective-permute-start | bytes 1769480 | tf_op jit(solution)/shard_map/ppermute | solution.py:44
  48.8 4.0 %collective-permute-start.4 = (bf16[576,512]{1,0:T(8,128)(2,1)S(1)}, bf16[576,512]{1,0:T(8,128)(2,1)S(1)}, u32[]{:S(2)}, u32[]{:S(2)}) collective-permute-start(bf16[576,512]{1,0:T(8,128)(2,1)S(1)} %get-tuple-element.30), channel_id=1, source_target_pairs={{0,6},{2,0},{4,2},{6,4},{1,7},{3,1},{5,3},{7,5},{8,14},{10,8},{12,... | collective-permute-start | bytes 1769480 | tf_op jit(solution)/shard_map/ppermute | solution.py:44
  52.8 2.9 %collective-permute-done.2 = bf16[576,512]{1,0:T(8,128)(2,1)S(1)} collective-permute-done((bf16[576,512]{1,0:T(8,128)(2,1)}, bf16[576,512]{1,0:T(8,128)(2,1)S(1)}, u32[]{:S(2)}, u32[]{:S(2)}) %collective-permute-start.2) | collective-permute-done | bytes 589856 | tf_op jit(solution)/shard_map/ppermute | solution.py:44
  55.7 2.4 %collective-permute-done.3 = bf16[576,512]{1,0:T(8,128)(2,1)S(1)} collective-permute-done((bf16[576,512]{1,0:T(8,128)(2,1)}, bf16[576,512]{1,0:T(8,128)(2,1)S(1)}, u32[]{:S(2)}, u32[]{:S(2)}) %collective-permute-start.3) | collective-permute-done | bytes 589856 | tf_op jit(solution)/shard_map/ppermute | solution.py:44
  58.1 17.3 %collective-permute-done.4 = bf16[576,512]{1,0:T(8,128)(2,1)S(1)} collective-permute-done((bf16[576,512]{1,0:T(8,128)(2,1)S(1)}, bf16[576,512]{1,0:T(8,128)(2,1)S(1)}, u32[]{:S(2)}, u32[]{:S(2)}) %collective-permute-start.4) | collective-permute-done | bytes 589856 | tf_op jit(solution)/shard_map/ppermute | solution.py:44
  75.4 0.3 add_convert_fusion
  76.0 1.1 reshape.36
  77.0 15.1 %all-to-all-start.1 = ((bf16[96,6,512]{2,1,0:T(8,128)(2,1)}), bf16[96,6,512]{2,1,0:T(8,128)(2,1)}, u32[]{:S(2)}, u32[]{:S(2)}) async-start(bf16[96,6,512]{2,1,0:T(8,128)(2,1)} %reshape.36), calls=%async_computation.1 | async-start | bytes 1572864 | tf_op jit(solution)/shard_map/all_to_all | solution.py:192
  92.1 2.7 %collective-permute-start.7 = (bf16[576,512]{1,0:T(8,128)(2,1)S(1)}, bf16[576,512]{1,0:T(8,128)(2,1)S(1)}, u32[]{:S(2)}, u32[]{:S(2)}) collective-permute-start(bf16[576,512]{1,0:T(8,128)(2,1)S(1)} %reshape.35.refs_2_.refs_1_), channel_id=1, source_target_pairs={{0,6},{2,0},{4,2},{6,4},{1,7},{3,1},{5,3},{7,5},{8,14},{10,8},{12,... | collective-permute-start | bytes 1769480 | tf_op jit(solution)/shard_map/ppermute | solution.py:44
  94.8 4.4 %collective-permute-start.6 = (bf16[576,512]{1,0:T(8,128)(2,1)S(1)}, bf16[576,512]{1,0:T(8,128)(2,1)S(1)}, u32[]{:S(2)}, u32[]{:S(2)}) collective-permute-start(bf16[576,512]{1,0:T(8,128)(2,1)S(1)} %reshape.35.refs_2_.refs_1_), channel_id=1, source_target_pairs={{0,4},{2,6},{4,0},{6,2},{1,5},{3,7},{5,1},{7,3},{8,12},{10,14},{12... | collective-permute-start | bytes 1769480 | tf_op jit(solution)/shard_map/ppermute | solution.py:44
  99.3 4.0 %collective-permute-start.5 = (bf16[576,512]{1,0:T(8,128)(2,1)S(1)}, bf16[576,512]{1,0:T(8,128)(2,1)S(1)}, u32[]{:S(2)}, u32[]{:S(2)}) collective-permute-start(bf16[576,512]{1,0:T(8,128)(2,1)S(1)} %reshape.35.refs_2_.refs_1_), channel_id=1, source_target_pairs={{0,2},{2,4},{4,6},{6,0},{1,3},{3,5},{5,7},{7,1},{8,10},{10,12},{12... | collective-permute-start | bytes 1769480 | tf_op jit(solution)/shard_map/ppermute | solution.py:44
  103.2 20.6 %all-to-all-done.1 = bf16[96,6,512]{2,1,0:T(8,128)(2,1)} async-done(((bf16[96,6,512]{2,1,0:T(8,128)(2,1)}), bf16[96,6,512]{2,1,0:T(8,128)(2,1)}, u32[]{:S(2)}, u32[]{:S(2)}) %all-to-all-start.1) | async-done | bytes 589856 | tf_op jit(solution)/shard_map/all_to_all | solution.py:192
  123.9 1.4 convert_reduce_fusion
  125.3 0.2 collective-permute-done.5.refs_3_.refs_2_
  125.5 2.0 %shard_map.69 = bf16[128,2816]{1,0:T(8,128)(2,1)S(1)} custom-call(s32[2]{0:T(128)S(1)} %pad_add_fusion.place_ref, bf16[128,2816]{1,0:T(8,128)(2,1)S(1)} %copy-done.2, bf16[576,512]{1,0:T(8,128)(2,1)S(1)} %reshape.35.refs_2_.refs_1_, bf16[576,512]{1,0:T(8,128)(2,1)S(1)} %collective-permute-done.5.refs_3_.refs_2_, ...), custom_call_target="tpu_custom_call" | custom-call | flops 603979776 | bytes 1441792 | tf_op jit(solution)/shard_map/pallas_call | solution.py:54
  127.5 6.4 %collective-permute-start.8 = (bf16[128,2816]{1,0:T(8,128)(2,1)S(1)}, bf16[128,2816]{1,0:T(8,128)(2,1)S(1)}, u32[]{:S(2)}, u32[]{:S(2)}) collective-permute-start(bf16[128,2816]{1,0:T(8,128)(2,1)S(1)} %shard_map.69), channel_id=1, source_target_pairs={{0,1},{1,0},{2,3},{3,2},{4,5},{5,4},{6,7},{7,6},{8,9},{9,8},{10,11... | collective-permute-start | bytes 2162696 | tf_op jit(solution)/shard_map/ppermute | solution.py:40
  134.0 13.3 %collective-permute-start.9 = (f32[6,512]{1,0:T(8,128)S(1)}, f32[6,512]{1,0:T(8,128)S(1)}, u32[]{:S(2)}, u32[]{:S(2)}) collective-permute-start(f32[6,512]{1,0:T(8,128)S(1)} %broadcast_multiply_fusion), channel_id=1, source_target_pairs={{0,0},{8,1},{16,2},{24,3},{32,4},{40,5},{48,6},{56,7},{64,8},{72,9... | collective-permute-start | bytes 36872 | tf_op jit(solution)/shard_map/ppermute | solution.py:196
  147.3 2.0 %shard_map.68 = (f32[128,512]{1,0:T(8,128)S(1)}, bf16[128,2304]{1,0:T(8,128)(2,1)S(1)}) custom-call(s32[2]{0:T(128)S(1)} %pad_add_fusion.place_ref, bf16[128,4608]{1,0:T(8,128)(2,1)S(1)} %copy-done, bf16[128,512]{1,0:T(8,128)(2,1)S(1)} %copy-done.4, bf16[576,512]{1,0:T(8,128)(2,1)S(1)} %reshape.35.refs_2_.refs_1_, ...), custom_call_target="tpu_custom_call" | custom-call | flops 603979776 | bytes 1703936 | tf_op jit(solution)/shard_map/pallas_call | solution.py:54
  149.3 1.7 %shard_map.70 = (bf16[128,512]{1,0:T(8,128)(2,1)}, bf16[128,4608]{1,0:T(8,128)(2,1)}) custom-call(s32[2]{0:T(128)S(1)} %pad_add_fusion.place_ref, f32[128,512]{1,0:T(8,128)S(1)} %get-tuple-element.38.part_ref, bf16[128,2304]{1,0:T(8,128)(2,1)S(1)} %get-tuple-element.39.columns_ref, bf16[128,2816]{1,0:T(8,128)(2,1)S(1)} %collective-permute-done.8.received_ref), custom_call_target="tpu_custom_call" | custom-call | flops 65536 | bytes 2621440 | tf_op jit(solution)/shard_map/pallas_call | solution.py:54
  151.0 0.6 copy.8
  (26 shorter events, 0.4 us)
Async XLA Ops:
  0.6 1.3 copy-start.3
  0.6 6.6 %copy-start.7 = (bf16[6,512]{1,0:T(8,128)(2,1)S(1)}, bf16[6,512]{1,0:T(8,128)(2,1)}, u32[]{:S(2)}) copy-start(bf16[6,512]{1,0:T(8,128)(2,1)} %param.5) | copy-start | bytes 18436
  0.7 11.9 %copy-start = (bf16[128,4608]{1,0:T(8,128)(2,1)S(1)}, bf16[128,4608]{1,0:T(8,128)(2,1)}, u32[]{:S(2)}) copy-start(bf16[128,4608]{1,0:T(8,128)(2,1)} %refs_0_.1) | copy-start | bytes 3538948
  1.9 10.6 %collective-permute-start.1 = (bf16[128,2816]{1,0:T(8,128)(2,1)S(1)}, bf16[128,2816]{1,0:T(8,128)(2,1)S(1)}, u32[]{:S(2)}, u32[]{:S(2)}) collective-permute-start(bf16[128,2816]{1,0:T(8,128)(2,1)S(1)} %pad_maximum_fusion), channel_id=1, source_target_pairs={{0,1},{1,0},{2,3},{3,2},{4,5},{5,4},{6,7},{7,6},{8,9},{9,8},{10,11... | collective-permute-start | bytes 2162696 | tf_op jit(solution)/shard_map/ppermute | solution.py:40
  7.4 21.9 %collective-permute-start = (bf16[6,512]{1,0:T(8,128)(2,1)S(1)}, bf16[6,512]{1,0:T(8,128)(2,1)S(1)}, u32[]{:S(2)}, u32[]{:S(2)}) collective-permute-start(bf16[6,512]{1,0:T(8,128)(2,1)S(1)} %multiply_convert_fusion), channel_id=1, source_target_pairs={{0,0},{1,8},{2,16},{3,24},{4,32},{5,40},{6,48},{7,56},{8,64},{9,72... | collective-permute-start | bytes 18440 | tf_op jit(solution)/shard_map/ppermute | solution.py:181
  12.6 17.7 %copy-start.1 = (bf16[128,2816]{1,0:T(8,128)(2,1)}, bf16[128,2816]{1,0:T(8,128)(2,1)S(1)}, u32[]{:S(2)}) copy-start(bf16[128,2816]{1,0:T(8,128)(2,1)S(1)} %collective-permute-done.1.theirs_ref.refs_0_) | copy-start | bytes 2162692
  14.0 0.8 copy-start.5
  14.9 14.4 %copy-start.6 = (bf16[576,512]{1,0:T(8,128)(2,1)}, bf16[576,512]{1,0:T(8,128)(2,1)S(1)}, u32[]{:S(2)}) copy-start(bf16[576,512]{1,0:T(8,128)(2,1)S(1)} %get-tuple-element.28) | copy-start | bytes 1769476
  30.2 45.5 %all-to-all-start = ((bf16[96,6,512]{2,1,0:T(8,128)(2,1)}), bf16[96,6,512]{2,1,0:T(8,128)(2,1)S(1)}, u32[]{:S(2)}, u32[]{:S(2)}) async-start(bf16[96,6,512]{2,1,0:T(8,128)(2,1)} %broadcast_in_dim.17), calls=%async_computation | async-start | bytes 1572864 | tf_op jit(solution)/shard_map/all_to_all | solution.py:187
  42.1 13.6 %collective-permute-start.2 = (bf16[576,512]{1,0:T(8,128)(2,1)}, bf16[576,512]{1,0:T(8,128)(2,1)S(1)}, u32[]{:S(2)}, u32[]{:S(2)}) collective-permute-start(bf16[576,512]{1,0:T(8,128)(2,1)} %copy-done.6), channel_id=1, source_target_pairs={{0,2},{2,4},{4,6},{6,0},{1,3},{3,5},{5,7},{7,1},{8,10},{10,12},{12... | collective-permute-start | bytes 1769480 | tf_op jit(solution)/shard_map/ppermute | solution.py:44
  44.1 14.0 %collective-permute-start.3 = (bf16[576,512]{1,0:T(8,128)(2,1)}, bf16[576,512]{1,0:T(8,128)(2,1)S(1)}, u32[]{:S(2)}, u32[]{:S(2)}) collective-permute-start(bf16[576,512]{1,0:T(8,128)(2,1)} %copy-done.5), channel_id=1, source_target_pairs={{0,4},{2,6},{4,0},{6,2},{1,5},{3,7},{5,1},{7,3},{8,12},{10,14},{12... | collective-permute-start | bytes 1769480 | tf_op jit(solution)/shard_map/ppermute | solution.py:44
  48.8 26.6 %collective-permute-start.4 = (bf16[576,512]{1,0:T(8,128)(2,1)S(1)}, bf16[576,512]{1,0:T(8,128)(2,1)S(1)}, u32[]{:S(2)}, u32[]{:S(2)}) collective-permute-start(bf16[576,512]{1,0:T(8,128)(2,1)S(1)} %get-tuple-element.30), channel_id=1, source_target_pairs={{0,6},{2,0},{4,2},{6,4},{1,7},{3,1},{5,3},{7,5},{8,14},{10,8},{12,... | collective-permute-start | bytes 1769480 | tf_op jit(solution)/shard_map/ppermute | solution.py:44
  77.0 46.9 %all-to-all-start.1 = ((bf16[96,6,512]{2,1,0:T(8,128)(2,1)}), bf16[96,6,512]{2,1,0:T(8,128)(2,1)}, u32[]{:S(2)}, u32[]{:S(2)}) async-start(bf16[96,6,512]{2,1,0:T(8,128)(2,1)} %reshape.36), calls=%async_computation.1 | async-start | bytes 1572864 | tf_op jit(solution)/shard_map/all_to_all | solution.py:192
  92.1 33.2 %collective-permute-start.7 = (bf16[576,512]{1,0:T(8,128)(2,1)S(1)}, bf16[576,512]{1,0:T(8,128)(2,1)S(1)}, u32[]{:S(2)}, u32[]{:S(2)}) collective-permute-start(bf16[576,512]{1,0:T(8,128)(2,1)S(1)} %reshape.35.refs_2_.refs_1_), channel_id=1, source_target_pairs={{0,6},{2,0},{4,2},{6,4},{1,7},{3,1},{5,3},{7,5},{8,14},{10,8},{12,... | collective-permute-start | bytes 1769480 | tf_op jit(solution)/shard_map/ppermute | solution.py:44
  94.8 30.5 %collective-permute-start.6 = (bf16[576,512]{1,0:T(8,128)(2,1)S(1)}, bf16[576,512]{1,0:T(8,128)(2,1)S(1)}, u32[]{:S(2)}, u32[]{:S(2)}) collective-permute-start(bf16[576,512]{1,0:T(8,128)(2,1)S(1)} %reshape.35.refs_2_.refs_1_), channel_id=1, source_target_pairs={{0,4},{2,6},{4,0},{6,2},{1,5},{3,7},{5,1},{7,3},{8,12},{10,14},{12... | collective-permute-start | bytes 1769480 | tf_op jit(solution)/shard_map/ppermute | solution.py:44
  99.3 26.3 %collective-permute-start.5 = (bf16[576,512]{1,0:T(8,128)(2,1)S(1)}, bf16[576,512]{1,0:T(8,128)(2,1)S(1)}, u32[]{:S(2)}, u32[]{:S(2)}) collective-permute-start(bf16[576,512]{1,0:T(8,128)(2,1)S(1)} %reshape.35.refs_2_.refs_1_), channel_id=1, source_target_pairs={{0,2},{2,4},{4,6},{6,0},{1,3},{3,5},{5,7},{7,1},{8,10},{10,12},{12... | collective-permute-start | bytes 1769480 | tf_op jit(solution)/shard_map/ppermute | solution.py:44
  123.9 1.6 %copy-start.2 = (bf16[128,2816]{1,0:T(8,128)(2,1)S(1)}, bf16[128,2816]{1,0:T(8,128)(2,1)}, u32[]{:S(2)}) copy-start(bf16[128,2816]{1,0:T(8,128)(2,1)} %copy-done.1) | copy-start | bytes 2162692
  125.3 22.0 %copy-start.4 = (bf16[128,512]{1,0:T(8,128)(2,1)S(1)}, bf16[128,512]{1,0:T(8,128)(2,1)}, u32[]{:S(2)}) copy-start(bf16[128,512]{1,0:T(8,128)(2,1)} %refs_1_.1) | copy-start | bytes 393220
  127.5 21.8 %collective-permute-start.8 = (bf16[128,2816]{1,0:T(8,128)(2,1)S(1)}, bf16[128,2816]{1,0:T(8,128)(2,1)S(1)}, u32[]{:S(2)}, u32[]{:S(2)}) collective-permute-start(bf16[128,2816]{1,0:T(8,128)(2,1)S(1)} %shard_map.69), channel_id=1, source_target_pairs={{0,1},{1,0},{2,3},{3,2},{4,5},{5,4},{6,7},{7,6},{8,9},{9,8},{10,11... | collective-permute-start | bytes 2162696 | tf_op jit(solution)/shard_map/ppermute | solution.py:40
  134.0 15.3 %collective-permute-start.9 = (f32[6,512]{1,0:T(8,128)S(1)}, f32[6,512]{1,0:T(8,128)S(1)}, u32[]{:S(2)}, u32[]{:S(2)}) collective-permute-start(f32[6,512]{1,0:T(8,128)S(1)} %broadcast_multiply_fusion), channel_id=1, source_target_pairs={{0,0},{8,1},{16,2},{24,3},{32,4},{40,5},{48,6},{56,7},{64,8},{72,9... | collective-permute-start | bytes 36872 | tf_op jit(solution)/shard_map/ppermute | solution.py:196

commit v5 on v4

--- a/solution.py
+++ b/solution.py
@@ -13,7 +13,8 @@
 PLANE = ("z", "y")
 BF16 = jnp.bfloat16
 F32 = jnp.float32
-PARAMS = pltpu.CompilerParams(vmem_limit_bytes=40 * 2**20)
+LONG = 10**11
+PARAMS = pltpu.CompilerParams(vmem_limit_bytes=16 * 2**20)
 
 
 def block_moves():
@@ -97,44 +98,51 @@
     )
 
 
-def forward(place, tokens, grad, blocks, theirs=None):
-    own = theirs is None
-    half = blocks[0].shape[0] * NX
+def forward(place, tokens, grad, theirs, blocks):
     rows, cols = blocks[0].shape
-    count = tokens.shape[0] if own else theirs.shape[0]
-
-    def kernel(place_ref, *refs):
-        if own:
-            tokens_ref, grad_ref, *block_refs, part_ref, out_ref, weights = refs
-            token = tokens_ref[:, pl.ds(core_columns(place_ref, half), half)]
-            gradient = grad_ref[...]
-        else:
-            theirs_ref, *block_refs, out_ref, weights = refs
-            token, gradient = theirs_ref[:, :half], theirs_ref[:, half:]
+    half = rows * NX
+    count = tokens.shape[0]
+
+    def kernel(place_ref, tokens_ref, grad_ref, theirs_ref, *rest):
+        block_refs, (for_them, part_ref, columns_ref, weights) = rest[:NX], rest[NX:]
         x = place_ref[1]
         for step in range(NX):
             block = lax.rem(x + NX - step, NX)
             weights[pl.ds(pl.multiple_of(block * rows, rows), rows), :] = block_refs[step][...]
-        part = dot(token, weights[...], (1, 0))
-        columns = dot(gradient, weights[...], (1, 1)).astype(BF16)
-        out_ref[:, :half] = columns
-        if own:
-            part_ref[...] = part
-        else:
-            out_ref[:, half:] = part.astype(BF16)
-
-    if own:
-        outs = [
+        mine = tokens_ref[:, pl.ds(core_columns(place_ref, half), half)]
+        tokens_both = jnp.concatenate([theirs_ref[:, :half], mine], axis=0)
+        part = dot(tokens_both, weights[...], (1, 0))
+        for_them[:, half:] = part[:count].astype(BF16)
+        part_ref[...] = part[count:]
+        grads = jnp.concatenate([theirs_ref[:, half:], grad_ref[...]], axis=0)
+        columns = dot(grads, weights[...], (1, 1)).astype(BF16)
+        for_them[:, :half] = columns[:count]
+        columns_ref[...] = columns[count:]
+
+    return call(
+        kernel,
+        [
+            jax.ShapeDtypeStruct((count, half + cols), BF16),
             jax.ShapeDtypeStruct((count, cols), F32),
             jax.ShapeDtypeStruct((count, half), BF16),
-        ]
-        args = (tokens, grad, *blocks)
-    else:
-        outs = [jax.ShapeDtypeStruct((count, half + cols), BF16)]
-        args = (theirs, *blocks)
-    return call(
-        kernel, outs, [pltpu.VMEM((half, cols), BF16)], 4 * count * half * cols, place, *args
-    )
+        ],
+        [pltpu.VMEM((half, cols), BF16)],
+        LONG,
+        place,
+        tokens,
+        grad,
+        theirs,
+        *blocks,
+    )
+
+
+def add_up(place, parts):
+    def kernel(place_ref, *refs):
+        *part_refs, out_ref = refs
+        out_ref[...] = sum(p[...].astype(F32) for p in part_refs).astype(BF16)
+
+    out = jax.ShapeDtypeStruct(parts[0].shape, BF16)
+    return call(kernel, [out], [], LONG, place, *parts)[0]
 
 
 def assemble(place, part, columns, received):
@@ -178,28 +186,27 @@
     cols = out_grad.shape[1]
     others = lax.dynamic_slice(tokens, (0, (1 - core) * half), (tokens.shape[0], half))
     theirs = swap(jnp.concatenate([others, out_grad], axis=1))
-    rows = lax.ppermute(scaled_rows(w_values, w_scales), AXES, moves)
+    rows = scaled_rows(w_values, w_scales)
 
     parts = partials(place, tokens, out_grad, theirs)
     rows, *parts = lax.optimization_barrier((rows, *parts))
+    rows = lax.ppermute(rows, AXES, moves)
     parts = [parts[0], *(along_x(parts[step], step) for step in range(1, NX))]
 
     rows = lax.all_to_all(jnp.broadcast_to(rows[None], (NZ * NY, *rows.shape)), PLANE, 0, 0)
     rows = rows.reshape(-1, cols)
-    total = sum(p.astype(F32) for p in parts).astype(BF16)
+    total = add_up(place, parts)
     total, rows = lax.optimization_barrier((total, rows))
     blocks = [rows, *(along_x(rows, step) for step in range(1, NX))]
     total = lax.all_to_all(total.reshape(NZ * NY, -1, cols), PLANE, 0, 0)
     total = jnp.sum(total.astype(F32), axis=0)
-    total, *blocks = lax.optimization_barrier((total, *blocks))
     count = tokens.shape[0] * NZ * NY * NX * NC
     weight_grad = lax.ppermute(
         total * (1.0 / math.sqrt(count)), AXES, [(b, a) for a, b in moves]
     )
 
-    (for_them,) = forward(place, None, None, blocks, theirs)
+    for_them, part, columns = forward(place, tokens, out_grad, theirs, blocks)
     received = swap(for_them)
-    part, columns = forward(place, tokens, out_grad, blocks)
     projected, token_grad = assemble(place, part, columns, received)
     return projected, token_grad, weight_grad
 

time: 152 us -> 166 us (1.092)
  the two profiles are of different devices: /device:TPU:3 before, /device:TPU:150 now
where the time goes in v5:
time: 166 us; the launch traced here: 165 us
  starting transfers between devices  74 us (45%)
  waiting for transfers between devices  68.3 us (41%)
  local copies, waits for them, and re-layouts  9.49 us (6%)
  Pallas kernels  9.48 us (6%)
  other arithmetic  2.84 us (2%)
    all_to_all x1, waiting for transfers between devices, body(): lax.all_to_all(jnp.broadcast_to(rows[None], (NZ * NY, *rows.shape)), PLAN...  26.2 us
    ppermute x6, starting transfers between devices, along_x(): return lax.ppermute(array, 'x', [(i, (i + step) % NX) for i in range(NX)])  22.6 us
    all_to_all x1, starting transfers between devices, body(): lax.all_to_all(jnp.broadcast_to(rows[None], (NZ * NY, *rows.shape)), PLAN...  20 us
    ppermute x1, starting transfers between devices, body(): rows = lax.ppermute(rows, AXES, moves)  17.1 us
    all_to_all x1, waiting for transfers between devices, body(): total = lax.all_to_all(total.reshape(NZ * NY, -1, cols), PLANE, 0, 0)  14.9 us
    ppermute x1, waiting for transfers between devices, body(): lax.ppermute(total * (1.0 / math.sqrt(count)), AXES, [(b, a) for a, b in...  13 us
    ppermute x6, waiting for transfers between devices, along_x(): return lax.ppermute(array, 'x', [(i, (i + step) % NX) for i in range(NX)])  12.8 us
    pallas_call x4, Pallas kernels, call(): pl.pallas_call(kernel, out_shape=outs, in_specs=[pl.BlockSpec(memory_spac...  9.48 us
  transfers between devices with their start and end apart: 12, of which 6 were waited for; matrix products, arithmetic and copies ran while one was open for 4% of the time, Pallas kernels for 4%

profile of v5, /device:TPU:150, one launch (start us, length us, event | category | flops | bytes accessed | tf_op | source)
XLA Modules:
  0.0 165.0 jit_solution(10781547332865970141)
XLA Ops:
  0.7 1.2 constant_dynamic-slice_fusion
  1.9 1.9 %collective-permute-start = (bf16[128,2816]{1,0:T(8,128)(2,1)S(1)}, bf16[128,2816]{1,0:T(8,128)(2,1)S(1)}, u32[]{:S(2)}, u32[]{:S(2)}) collective-permute-start(bf16[128,2816]{1,0:T(8,128)(2,1)S(1)} %pad_maximum_fusion), channel_id=1, source_target_pairs={{0,1},{1,0},{2,3},{3,2},{4,5},{5,4},{6,7},{7,6},{8,9},{9,8},{10,11... | collective-permute-start | bytes 2162696 | tf_op jit(solution)/shard_map/ppermute | solution.py:41
  3.9 0.8 dynamic_slice.7
  5.4 1.3 compare_select_fusion
  6.8 2.5 %shard_map.67 = (bf16[576,512]{1,0:T(8,128)(2,1)S(1)}, bf16[576,512]{1,0:T(8,128)(2,1)}, bf16[576,512]{1,0:T(8,128)(2,1)}, bf16[576,512]{1,0:T(8,128)(2,1)S(1)}) custom-call(s32[2]{0:T(128)S(1)} %pad_add_fusion.place_ref, bf16[128,4608]{1,0:T(8,128)(2,1)S(1)} %copy-done, bf16[128,512]{1,0:T(8,128)(2,1)S(1)} %copy-done.1, ...), custom_call_target="tpu_custom_call" | custom-call | flops 603979776 | bytes 4718592 | tf_op jit(solution)/shard_map/pallas_call | solution.py:55
  9.3 0.8 copy-done.4
  10.1 2.3 %collective-permute-start.1 = (bf16[576,512]{1,0:T(8,128)(2,1)}, bf16[576,512]{1,0:T(8,128)(2,1)S(1)}, u32[]{:S(2)}, u32[]{:S(2)}) collective-permute-start(bf16[576,512]{1,0:T(8,128)(2,1)} %get-tuple-element.24), channel_id=1, source_target_pairs={{0,2},{2,4},{4,6},{6,0},{1,3},{3,5},{5,7},{7,1},{8,10},{10,12},{12... | collective-permute-start | bytes 1769480 | tf_op jit(solution)/shard_map/ppermute | solution.py:45
  12.4 4.3 %collective-permute-start.2 = (bf16[576,512]{1,0:T(8,128)(2,1)}, bf16[576,512]{1,0:T(8,128)(2,1)}, u32[]{:S(2)}, u32[]{:S(2)}) collective-permute-start(bf16[576,512]{1,0:T(8,128)(2,1)} %get-tuple-element.25), channel_id=1, source_target_pairs={{0,4},{2,6},{4,0},{6,2},{1,5},{3,7},{5,1},{7,3},{8,12},{10,14},{12... | collective-permute-start | bytes 1769480 | tf_op jit(solution)/shard_map/ppermute | solution.py:45
  16.8 1.9 %collective-permute-start.3 = (bf16[576,512]{1,0:T(8,128)(2,1)S(1)}, bf16[576,512]{1,0:T(8,128)(2,1)}, u32[]{:S(2)}, u32[]{:S(2)}) collective-permute-start(bf16[576,512]{1,0:T(8,128)(2,1)S(1)} %get-tuple-element.26), channel_id=1, source_target_pairs={{0,6},{2,0},{4,2},{6,4},{1,7},{3,1},{5,3},{7,5},{8,14},{10,8},{12,... | collective-permute-start | bytes 1769480 | tf_op jit(solution)/shard_map/ppermute | solution.py:45
  18.7 17.1 %collective-permute-start.4 = (bf16[6,512]{1,0:T(8,128)(2,1)S(1)}, bf16[6,512]{1,0:T(8,128)(2,1)S(1)}, u32[]{:S(2)}, u32[]{:S(2)}) collective-permute-start(bf16[6,512]{1,0:T(8,128)(2,1)S(1)} %multiply_convert_fusion), channel_id=1, source_target_pairs={{0,0},{1,8},{2,16},{3,24},{4,32},{5,40},{6,48},{7,56},{8,64},{9,72... | collective-permute-start | bytes 18440 | tf_op jit(solution)/shard_map/ppermute | solution.py:193
  35.8 1.3 collective-permute-done.4
  37.2 0.9 broadcast_in_dim.17
  38.1 20.0 %all-to-all-start = ((bf16[96,6,512]{2,1,0:T(8,128)(2,1)}), bf16[96,6,512]{2,1,0:T(8,128)(2,1)}, u32[]{:S(2)}, u32[]{:S(2)}) async-start(bf16[96,6,512]{2,1,0:T(8,128)(2,1)} %broadcast_in_dim.17), calls=%async_computation | async-start | bytes 1572864 | tf_op jit(solution)/shard_map/all_to_all | solution.py:196
  58.2 1.1 copy-done.5
  59.2 1.5 shard_map.68
  60.8 26.2 %all-to-all-done = bf16[96,6,512]{2,1,0:T(8,128)(2,1)} async-done(((bf16[96,6,512]{2,1,0:T(8,128)(2,1)}), bf16[96,6,512]{2,1,0:T(8,128)(2,1)}, u32[]{:S(2)}, u32[]{:S(2)}) %all-to-all-start) | async-done | bytes 589856 | tf_op jit(solution)/shard_map/all_to_all | solution.py:196
  87.0 1.3 reshape.35.rest_0_
  88.3 7.5 %collective-permute-start.7 = (bf16[576,512]{1,0:T(8,128)(2,1)S(1)}, bf16[576,512]{1,0:T(8,128)(2,1)S(1)}, u32[]{:S(2)}, u32[]{:S(2)}) collective-permute-start(bf16[576,512]{1,0:T(8,128)(2,1)S(1)} %reshape.35.rest_0_), channel_id=1, source_target_pairs={{0,6},{2,0},{4,2},{6,4},{1,7},{3,1},{5,3},{7,5},{8,14},{10,8},{12,... | collective-permute-start | bytes 1769480 | tf_op jit(solution)/shard_map/ppermute | solution.py:45
  95.8 2.7 %collective-permute-start.6 = (bf16[576,512]{1,0:T(8,128)(2,1)S(1)}, bf16[576,512]{1,0:T(8,128)(2,1)}, u32[]{:S(2)}, u32[]{:S(2)}) collective-permute-start(bf16[576,512]{1,0:T(8,128)(2,1)S(1)} %reshape.35.rest_0_), channel_id=1, source_target_pairs={{0,4},{2,6},{4,0},{6,2},{1,5},{3,7},{5,1},{7,3},{8,12},{10,14},{12... | collective-permute-start | bytes 1769480 | tf_op jit(solution)/shard_map/ppermute | solution.py:45
  98.5 3.8 %collective-permute-start.5 = (bf16[576,512]{1,0:T(8,128)(2,1)S(1)}, bf16[576,512]{1,0:T(8,128)(2,1)}, u32[]{:S(2)}, u32[]{:S(2)}) collective-permute-start(bf16[576,512]{1,0:T(8,128)(2,1)S(1)} %reshape.35.rest_0_), channel_id=1, source_target_pairs={{0,2},{2,4},{4,6},{6,0},{1,3},{3,5},{5,7},{7,1},{8,10},{10,12},{12... | collective-permute-start | bytes 1769480 | tf_op jit(solution)/shard_map/ppermute | solution.py:45
  102.3 1.1 reshape.36
  103.4 8.3 %all-to-all-start.1 = ((bf16[96,6,512]{2,1,0:T(8,128)(2,1)}), bf16[96,6,512]{2,1,0:T(8,128)(2,1)}, u32[]{:S(2)}, u32[]{:S(2)}) async-start(bf16[96,6,512]{2,1,0:T(8,128)(2,1)} %reshape.36), calls=%async_computation.1 | async-start | bytes 1572864 | tf_op jit(solution)/shard_map/all_to_all | solution.py:201
  111.7 11.2 %collective-permute-done.6.rest_2_ = bf16[576,512]{1,0:T(8,128)(2,1)} collective-permute-done((bf16[576,512]{1,0:T(8,128)(2,1)S(1)}, bf16[576,512]{1,0:T(8,128)(2,1)}, u32[]{:S(2)}, u32[]{:S(2)}) %collective-permute-start.6) | collective-permute-done | bytes 589856 | tf_op jit(solution)/shard_map/ppermute | solution.py:45
  122.8 1.6 collective-permute-done.5.rest_1_
  124.5 1.1 copy-done.3
  125.6 3.7 %shard_map.69 = (bf16[128,2816]{1,0:T(8,128)(2,1)}, f32[128,512]{1,0:T(8,128)S(1)}, bf16[128,2304]{1,0:T(8,128)(2,1)S(1)}) custom-call(s32[2]{0:T(128)S(1)} %pad_add_fusion.place_ref, bf16[128,4608]{1,0:T(8,128)(2,1)S(1)} %copy-done, bf16[128,512]{1,0:T(8,128)(2,1)S(1)} %copy-done.1, bf16[128,2816]{1,0:T(8,128)(2,1)S(1)} %copy-done.3, ...), custom_call_target="tpu_custom_call" | custom-call | flops 99999997952 | bytes 3145728 | tf_op jit(solution)/shard_map/pallas_call | solution.py:55
  129.3 1.9 %collective-permute-start.8 = (bf16[128,2816]{1,0:T(8,128)(2,1)}, bf16[128,2816]{1,0:T(8,128)(2,1)S(1)}, u32[]{:S(2)}, u32[]{:S(2)}) collective-permute-start(bf16[128,2816]{1,0:T(8,128)(2,1)} %get-tuple-element.31), channel_id=1, source_target_pairs={{0,1},{1,0},{2,3},{3,2},{4,5},{5,4},{6,7},{7,6},{8,9},{9,8},{10,11... | collective-permute-start | bytes 2162696 | tf_op jit(solution)/shard_map/ppermute | solution.py:41
  131.2 14.9 %all-to-all-done.1 = bf16[96,6,512]{2,1,0:T(8,128)(2,1)} async-done(((bf16[96,6,512]{2,1,0:T(8,128)(2,1)}), bf16[96,6,512]{2,1,0:T(8,128)(2,1)}, u32[]{:S(2)}, u32[]{:S(2)}) %all-to-all-start.1) | async-done | bytes 589856 | tf_op jit(solution)/shard_map/all_to_all | solution.py:201
  146.1 1.3 convert_reduce_fusion
  147.5 2.2 %collective-permute-start.9 = (f32[6,512]{1,0:T(8,128)S(1)}, f32[6,512]{1,0:T(8,128)S(1)}, u32[]{:S(2)}, u32[]{:S(2)}) collective-permute-start(f32[6,512]{1,0:T(8,128)S(1)} %broadcast_multiply_fusion), channel_id=1, source_target_pairs={{0,0},{8,1},{16,2},{24,3},{32,4},{40,5},{48,6},{56,7},{64,8},{72,9... | collective-permute-start | bytes 36872 | tf_op jit(solution)/shard_map/ppermute | solution.py:204
  149.6 1.7 %shard_map.70 = (bf16[128,512]{1,0:T(8,128)(2,1)}, bf16[128,4608]{1,0:T(8,128)(2,1)}) custom-call(s32[2]{0:T(128)S(1)} %pad_add_fusion.place_ref, f32[128,512]{1,0:T(8,128)S(1)} %get-tuple-element.29.part_ref, bf16[128,2304]{1,0:T(8,128)(2,1)S(1)} %get-tuple-element.30.columns_ref, bf16[128,2816]{1,0:T(8,128)(2,1)S(1)} %collective-permute-done.8.received_ref), custom_call_target="tpu_custom_call" | custom-call | flops 65536 | bytes 2621440 | tf_op jit(solution)/shard_map/pallas_call | solution.py:55
  151.3 13.0 %collective-permute-done.9 = f32[6,512]{1,0:T(8,128)S(1)} collective-permute-done((f32[6,512]{1,0:T(8,128)S(1)}, f32[6,512]{1,0:T(8,128)S(1)}, u32[]{:S(2)}, u32[]{:S(2)}) %collective-permute-start.9) | collective-permute-done | bytes 12320 | tf_op jit(solution)/shard_map/ppermute | solution.py:204
  (23 shorter events, 1.4 us)
Async XLA Ops:
  0.6 1.2 copy-start.1
  0.6 6.0 %copy-start.6 = (bf16[6,512]{1,0:T(8,128)(2,1)S(1)}, bf16[6,512]{1,0:T(8,128)(2,1)}, u32[]{:S(2)}) copy-start(bf16[6,512]{1,0:T(8,128)(2,1)} %param.5) | copy-start | bytes 18436
  0.7 6.1 %copy-start = (bf16[128,4608]{1,0:T(8,128)(2,1)S(1)}, bf16[128,4608]{1,0:T(8,128)(2,1)}, u32[]{:S(2)}) copy-start(bf16[128,4608]{1,0:T(8,128)(2,1)} %tokens_ref.3) | copy-start | bytes 3538948
  1.9 4.8 %collective-permute-start = (bf16[128,2816]{1,0:T(8,128)(2,1)S(1)}, bf16[128,2816]{1,0:T(8,128)(2,1)S(1)}, u32[]{:S(2)}, u32[]{:S(2)}) collective-permute-start(bf16[128,2816]{1,0:T(8,128)(2,1)S(1)} %pad_maximum_fusion), channel_id=1, source_target_pairs={{0,1},{1,0},{2,3},{3,2},{4,5},{5,4},{6,7},{7,6},{8,9},{9,8},{10,11... | collective-permute-start | bytes 2162696 | tf_op jit(solution)/shard_map/ppermute | solution.py:41
  6.7 31.3 %copy-start.2 = (bf16[128,2816]{1,0:T(8,128)(2,1)}, bf16[128,2816]{1,0:T(8,128)(2,1)S(1)}, u32[]{:S(2)}) copy-start(bf16[128,2816]{1,0:T(8,128)(2,1)S(1)} %collective-permute-done.theirs_ref) | copy-start | bytes 2162692
  9.3 0.8 copy-start.4
  10.1 48.1 %collective-permute-start.1 = (bf16[576,512]{1,0:T(8,128)(2,1)}, bf16[576,512]{1,0:T(8,128)(2,1)S(1)}, u32[]{:S(2)}, u32[]{:S(2)}) collective-permute-start(bf16[576,512]{1,0:T(8,128)(2,1)} %get-tuple-element.24), channel_id=1, source_target_pairs={{0,2},{2,4},{4,6},{6,0},{1,3},{3,5},{5,7},{7,1},{8,10},{10,12},{12... | collective-permute-start | bytes 1769480 | tf_op jit(solution)/shard_map/ppermute | solution.py:45
  12.4 45.7 %collective-permute-start.2 = (bf16[576,512]{1,0:T(8,128)(2,1)}, bf16[576,512]{1,0:T(8,128)(2,1)}, u32[]{:S(2)}, u32[]{:S(2)}) collective-permute-start(bf16[576,512]{1,0:T(8,128)(2,1)} %get-tuple-element.25), channel_id=1, source_target_pairs={{0,4},{2,6},{4,0},{6,2},{1,5},{3,7},{5,1},{7,3},{8,12},{10,14},{12... | collective-permute-start | bytes 1769480 | tf_op jit(solution)/shard_map/ppermute | solution.py:45
  16.8 41.4 %collective-permute-start.3 = (bf16[576,512]{1,0:T(8,128)(2,1)S(1)}, bf16[576,512]{1,0:T(8,128)(2,1)}, u32[]{:S(2)}, u32[]{:S(2)}) collective-permute-start(bf16[576,512]{1,0:T(8,128)(2,1)S(1)} %get-tuple-element.26), channel_id=1, source_target_pairs={{0,6},{2,0},{4,2},{6,4},{1,7},{3,1},{5,3},{7,5},{8,14},{10,8},{12,... | collective-permute-start | bytes 1769480 | tf_op jit(solution)/shard_map/ppermute | solution.py:45
  18.7 18.4 %collective-permute-start.4 = (bf16[6,512]{1,0:T(8,128)(2,1)S(1)}, bf16[6,512]{1,0:T(8,128)(2,1)S(1)}, u32[]{:S(2)}, u32[]{:S(2)}) collective-permute-start(bf16[6,512]{1,0:T(8,128)(2,1)S(1)} %multiply_convert_fusion), channel_id=1, source_target_pairs={{0,0},{1,8},{2,16},{3,24},{4,32},{5,40},{6,48},{7,56},{8,64},{9,72... | collective-permute-start | bytes 18440 | tf_op jit(solution)/shard_map/ppermute | solution.py:193
  38.1 48.9 %all-to-all-start = ((bf16[96,6,512]{2,1,0:T(8,128)(2,1)}), bf16[96,6,512]{2,1,0:T(8,128)(2,1)}, u32[]{:S(2)}, u32[]{:S(2)}) async-start(bf16[96,6,512]{2,1,0:T(8,128)(2,1)} %broadcast_in_dim.17), calls=%async_computation | async-start | bytes 1572864 | tf_op jit(solution)/shard_map/all_to_all | solution.py:196
  58.2 1.1 copy-start.5
  88.3 23.4 %collective-permute-start.7 = (bf16[576,512]{1,0:T(8,128)(2,1)S(1)}, bf16[576,512]{1,0:T(8,128)(2,1)S(1)}, u32[]{:S(2)}, u32[]{:S(2)}) collective-permute-start(bf16[576,512]{1,0:T(8,128)(2,1)S(1)} %reshape.35.rest_0_), channel_id=1, source_target_pairs={{0,6},{2,0},{4,2},{6,4},{1,7},{3,1},{5,3},{7,5},{8,14},{10,8},{12,... | collective-permute-start | bytes 1769480 | tf_op jit(solution)/shard_map/ppermute | solution.py:45
  95.8 27.1 %collective-permute-start.6 = (bf16[576,512]{1,0:T(8,128)(2,1)S(1)}, bf16[576,512]{1,0:T(8,128)(2,1)}, u32[]{:S(2)}, u32[]{:S(2)}) collective-permute-start(bf16[576,512]{1,0:T(8,128)(2,1)S(1)} %reshape.35.rest_0_), channel_id=1, source_target_pairs={{0,4},{2,6},{4,0},{6,2},{1,5},{3,7},{5,1},{7,3},{8,12},{10,14},{12... | collective-permute-start | bytes 1769480 | tf_op jit(solution)/shard_map/ppermute | solution.py:45
  98.5 26.0 %collective-permute-start.5 = (bf16[576,512]{1,0:T(8,128)(2,1)S(1)}, bf16[576,512]{1,0:T(8,128)(2,1)}, u32[]{:S(2)}, u32[]{:S(2)}) collective-permute-start(bf16[576,512]{1,0:T(8,128)(2,1)S(1)} %reshape.35.rest_0_), channel_id=1, source_target_pairs={{0,2},{2,4},{4,6},{6,0},{1,3},{3,5},{5,7},{7,1},{8,10},{10,12},{12... | collective-permute-start | bytes 1769480 | tf_op jit(solution)/shard_map/ppermute | solution.py:45
  103.4 42.8 %all-to-all-start.1 = ((bf16[96,6,512]{2,1,0:T(8,128)(2,1)}), bf16[96,6,512]{2,1,0:T(8,128)(2,1)}, u32[]{:S(2)}, u32[]{:S(2)}) async-start(bf16[96,6,512]{2,1,0:T(8,128)(2,1)} %reshape.36), calls=%async_computation.1 | async-start | bytes 1572864 | tf_op jit(solution)/shard_map/all_to_all | solution.py:201
  124.5 1.1 copy-start.3
  129.3 20.3 %collective-permute-start.8 = (bf16[128,2816]{1,0:T(8,128)(2,1)}, bf16[128,2816]{1,0:T(8,128)(2,1)S(1)}, u32[]{:S(2)}, u32[]{:S(2)}) collective-permute-start(bf16[128,2816]{1,0:T(8,128)(2,1)} %get-tuple-element.31), channel_id=1, source_target_pairs={{0,1},{1,0},{2,3},{3,2},{4,5},{5,4},{6,7},{7,6},{8,9},{9,8},{10,11... | collective-permute-start | bytes 2162696 | tf_op jit(solution)/shard_map/ppermute | solution.py:41
  147.5 16.9 %collective-permute-start.9 = (f32[6,512]{1,0:T(8,128)S(1)}, f32[6,512]{1,0:T(8,128)S(1)}, u32[]{:S(2)}, u32[]{:S(2)}) collective-permute-start(f32[6,512]{1,0:T(8,128)S(1)} %broadcast_multiply_fusion), channel_id=1, source_target_pairs={{0,0},{8,1},{16,2},{24,3},{32,4},{40,5},{48,6},{56,7},{64,8},{72,9... | collective-permute-start | bytes 36872 | tf_op jit(solution)/shard_map/ppermute | solution.py:204

commit v6 on v1

v6 whole, which is shorter than its diff:
```python
import math

import numpy as np
import jax
import jax.numpy as jnp
from jax import lax
from jax.experimental import pallas as pl
from jax.experimental.pallas import tpu as pltpu
from jax.sharding import Mesh, PartitionSpec as P

BLOCK_ROWS = 4
AXES = {"z_far": 6, "z_near": 2, "y_far": 4, "y_near": 2, "x": 4, "c": 2}
NEAR, FAR = ("z_near", "y_near", "x"), ("z_far", "y_far")
NC = AXES["c"]


def devices(axes):
    return math.prod(AXES[a] for a in axes)


BF16 = jnp.bfloat16
F32 = jnp.float32
PARAMS = pltpu.CompilerParams(vmem_limit_bytes=16 * 2**20)


def block_moves():
    names = list(AXES)
    order = [names.index(a) for a in ("c", *NEAR, *FAR)]
    holders = np.arange(devices(names)).reshape(list(AXES.values())).transpose(order).reshape(-1)
    return [(block, int(holder)) for block, holder in enumerate(holders)]


def scaled_rows(w_values, w_scales):
    rows = w_values.shape[0]
    first = lax.axis_index(tuple(AXES)) * rows
    start = first // BLOCK_ROWS
    pair = lax.dynamic_slice(w_scales, (start,), (2,))
    block = (first + lax.iota(jnp.int32, rows)) // BLOCK_ROWS - start
    scale = jnp.where(block == 0, pair[0], pair[1])
    return (w_values.astype(F32) * scale[:, None]).astype(BF16)


def swap(array):
    return lax.ppermute(array, "c", [(0, 1), (1, 0)])


def gather(rows, axes):
    size = devices(axes)
    out = lax.all_to_all(jnp.broadcast_to(rows[None], (size, *rows.shape)), axes, 0, 0)
    return out.reshape(-1, rows.shape[1])


def reduce(rows, axes):
    out = lax.all_to_all(rows.reshape(devices(axes), -1, rows.shape[1]), axes, 0, 0)
    return jnp.sum(out.astype(F32), axis=0)


def dot(a, b, over):
    return lax.dot_general(a, b, ((over[:1], over[1:]), ((), ())), preferred_element_type=F32)


def call(kernel, outs, flops, place, *args):
    moved = sum(math.prod(s.shape) * s.dtype.itemsize for s in outs)
    vmem = pl.BlockSpec(memory_space=pltpu.VMEM)
    return pl.pallas_call(
        kernel,
        out_shape=outs,
        in_specs=[pl.BlockSpec(memory_space=pltpu.SMEM), *[vmem] * len(args)],
        out_specs=[vmem] * len(outs),
        compiler_params=PARAMS,
        cost_estimate=pl.CostEstimate(flops=flops, bytes_accessed=2 * moved, transcendentals=0),
    )(place, *args)


def core_columns(place_ref, half):
    return pl.multiple_of(place_ref[0] * half, half)


def partials(place, tokens, grad, theirs):
    half, cols = tokens.shape[1] // NC, grad.shape[1]
    chunk = 256

    def kernel(place_ref, tokens_ref, grad_ref, theirs_ref, out_ref):
        grads = jnp.concatenate([grad_ref[...], theirs_ref[:, half:]], axis=0)
        first = core_columns(place_ref, half)
        for k in range(0, half, chunk):
            mine = tokens_ref[:, pl.ds(pl.multiple_of(first + k, chunk), chunk)]
            both = jnp.concatenate([mine, theirs_ref[:, k : k + chunk]], axis=0)
            out_ref[k : k + chunk] = dot(both, grads, (0, 0)).astype(BF16)

    out = jax.ShapeDtypeStruct((half, cols), BF16)
    return call(kernel, [out], 4 * tokens.size * cols // NC, place, tokens, grad, theirs)[0]


def forward(place, tokens, grad, theirs, weights):
    half, cols = weights.shape
    count = tokens.shape[0]

    def kernel(place_ref, tokens_ref, grad_ref, theirs_ref, weights_ref, *outs):
        for_them, part_ref, columns_ref = outs
        mine = tokens_ref[:, pl.ds(core_columns(place_ref, half), half)]
        tokens_both = jnp.concatenate([theirs_ref[:, :half], mine], axis=0)
        part = dot(tokens_both, weights_ref[...], (1, 0))
        for_them[:, half:] = part[:count].astype(BF16)
        part_ref[...] = part[count:]
        grads = jnp.concatenate([theirs_ref[:, half:], grad_ref[...]], axis=0)
        columns = dot(grads, weights_ref[...], (1, 1)).astype(BF16)
        for_them[:, :half] = columns[:count]
        columns_ref[...] = columns[count:]

    outs = [
        jax.ShapeDtypeStruct((count, half + cols), BF16),
        jax.ShapeDtypeStruct((count, cols), F32),
        jax.ShapeDtypeStruct((count, half), BF16),
    ]
    return call(kernel, outs, 8 * count * half * cols, place, tokens, grad, theirs, weights)


def assemble(place, part, columns, received):
    count, half = columns.shape
    cols = part.shape[1]

    def kernel(place_ref, part_ref, columns_ref, received_ref, projected_ref, out_ref):
        projected_ref[...] = (part_ref[...] + received_ref[:, half:].astype(F32)).astype(BF16)
        core = place_ref[0]

        @pl.when(core == 0)
        def _():
            out_ref[:, :half] = columns_ref[...]
            out_ref[:, half:] = received_ref[:, :half]

        @pl.when(core == 1)
        def _():
            out_ref[:, :half] = received_ref[:, :half]
            out_ref[:, half:] = columns_ref[...]

    return call(
        kernel,
        [
            jax.ShapeDtypeStruct((count, cols), BF16),
            jax.ShapeDtypeStruct((count, NC * half), BF16),
        ],
        count * cols,
        place,
        part,
        columns,
        received,
    )


def body(tokens, w_values, w_scales, out_grad):
    moves = block_moves()
    core = lax.axis_index("c")
    place = core.astype(jnp.int32).reshape(1)
    count, half = tokens.shape[0], tokens.shape[1] // NC
    others = lax.dynamic_slice(tokens, (0, (1 - core) * half), (count, half))
    theirs = swap(jnp.concatenate([others, out_grad], axis=1))
    rows = lax.ppermute(scaled_rows(w_values, w_scales), tuple(AXES), moves)

    partial = partials(place, tokens, out_grad, theirs)
    rows = gather(rows, FAR)
    total = reduce(partial, NEAR).astype(BF16)
    weights = gather(rows, NEAR)
    total = reduce(total, FAR)
    weight_grad = lax.ppermute(
        total * (1.0 / math.sqrt(count * devices(AXES))), tuple(AXES), [(b, a) for a, b in moves]
    )

    for_them, part, columns = forward(place, tokens, out_grad, theirs, weights)
    projected, token_grad = assemble(place, part, columns, swap(for_them))
    return projected, token_grad, weight_grad


def solution(mesh):
    split = Mesh(mesh.devices.reshape(list(AXES.values())), tuple(AXES))
    by_rows = P(tuple(AXES), None)
    return jax.shard_map(
        body,
        mesh=split,
        in_specs=(by_rows, by_rows, P(), by_rows),
        out_specs=(by_rows, by_rows, by_rows),
        check_vma=False,
    )
```

time: 185 us -> 176 us (0.951)
  the two profiles are of different devices: /device:TPU:1 before, /device:TPU:14 now
where the time goes in v6:
time: 176 us; the launch traced here: 175 us
  waiting for transfers between devices  88.4 us (50%)
  starting transfers between devices  57.8 us (33%)
  local copies, waits for them, and re-layouts  16.1 us (9%)
  other arithmetic  6 us (3%)
  Pallas kernels  5.62 us (3%)
    all_to_all x2, waiting for transfers between devices, gather(): lax.all_to_all(jnp.broadcast_to(rows[None], (size, *rows.shape)), axes, 0...  38.1 us
    all_to_all x2, waiting for transfers between devices, reduce(): lax.all_to_all(rows.reshape(devices(axes), -1, rows.shape[1]), axes, 0, 0)  36.1 us
    all_to_all x2, starting transfers between devices, gather(): lax.all_to_all(jnp.broadcast_to(rows[None], (size, *rows.shape)), axes, 0...  20.3 us
    ppermute x1, starting transfers between devices, body(): rows = lax.ppermute(scaled_rows(w_values, w_scales), tuple(AXES), moves)  19.3 us
    ppermute x1, waiting for transfers between devices, body(): lax.ppermute(total * (1.0 / math.sqrt(count * devices(AXES))), tuple(AXES...  12.8 us
    all_to_all x2, starting transfers between devices, reduce(): lax.all_to_all(rows.reshape(devices(axes), -1, rows.shape[1]), axes, 0, 0)  12.5 us
    unnamed x25, local copies, waits for them, and re-layouts  6.84 us
    pallas_call x3, Pallas kernels, call(): pl.pallas_call(kernel, out_shape=outs, in_specs=[pl.BlockSpec(memory_spac...  5.62 us
  transfers between devices with their start and end apart: 8, of which 6 were waited for; matrix products, arithmetic and copies ran while one was open for 6% of the time, Pallas kernels for 3%

profile of v6, /device:TPU:14, one launch (start us, length us, event | category | flops | bytes accessed | tf_op | source)
XLA Modules:
  0.0 174.8 jit_solution(18103735064060416191)
XLA Ops:
  0.7 1.2 constant_dynamic-slice_fusion
  1.9 1.0 pad_maximum_fusion
  2.8 1.9 %collective-permute-start = (bf16[128,2816]{1,0:T(8,128)(2,1)S(1)}, bf16[128,2816]{1,0:T(8,128)(2,1)S(1)}, u32[]{:S(2)}, u32[]{:S(2)}) collective-permute-start(bf16[128,2816]{1,0:T(8,128)(2,1)S(1)} %pad_maximum_fusion), channel_id=1, source_target_pairs={{0,1},{1,0},{2,3},{3,2},{4,5},{5,4},{6,7},{7,6},{8,9},{9,8},{10,11... | collective-permute-start | bytes 2162696 | tf_op jit(solution)/shard_map/ppermute | solution.py:44
  4.8 0.8 dynamic_slice.7
  6.2 1.3 compare_select_fusion
  7.6 19.3 %collective-permute-start.1 = (bf16[6,512]{1,0:T(8,128)(2,1)S(1)}, bf16[6,512]{1,0:T(8,128)(2,1)S(1)}, u32[]{:S(2)}, u32[]{:S(2)}) collective-permute-start(bf16[6,512]{1,0:T(8,128)(2,1)S(1)} %multiply_convert_fusion), channel_id=1, source_target_pairs={{0,0},{1,16},{2,32},{3,48},{4,128},{5,144},{6,160},{7,176},{8,256}... | collective-permute-start | bytes 18440 | tf_op jit(solution)/shard_map/ppermute | solution.py:158
  26.9 1.3 collective-permute-done.1
  28.2 0.7 broadcast_in_dim.24
  28.9 13.9 %all-to-all-start = ((bf16[24,6,512]{2,1,0:T(8,128)(2,1)}), bf16[24,6,512]{2,1,0:T(8,128)(2,1)S(1)}, u32[]{:S(2)}, u32[]{:S(2)}) async-start(bf16[24,6,512]{2,1,0:T(8,128)(2,1)} %broadcast_in_dim.24), calls=%async_computation | async-start | bytes 393216 | tf_op jit(solution)/shard_map/all_to_all | solution.py:49
  42.9 2.3 %shard_map.69 = bf16[2304,512]{1,0:T(8,128)(2,1)} custom-call(s32[1]{0:T(128)} %bitcast.place_ref, bf16[128,4608]{1,0:T(8,128)(2,1)S(1)} %copy-done, bf16[128,512]{1,0:T(8,128)(2,1)S(1)} %copy-done.5, bf16[128,2816]{1,0:T(8,128)(2,1)S(1)} %collective-permute-done.theirs_ref), custom_call_target="tpu_custom_call" | custom-call | flops 603979776 | bytes 4718592 | tf_op jit(solution)/shard_map/pallas_call | solution.py:65
  45.1 14.4 %all-to-all-done = bf16[24,6,512]{2,1,0:T(8,128)(2,1)S(1)} async-done(((bf16[24,6,512]{2,1,0:T(8,128)(2,1)}), bf16[24,6,512]{2,1,0:T(8,128)(2,1)S(1)}, u32[]{:S(2)}, u32[]{:S(2)}) %all-to-all-start) | async-done | bytes 147488 | tf_op jit(solution)/shard_map/all_to_all | solution.py:49
  60.2 8.0 %all-to-all-start.2 = ((bf16[16,144,512]{2,1,0:T(8,128)(2,1)}), bf16[16,144,512]{2,1,0:T(8,128)(2,1)S(1)}, u32[]{:S(2)}, u32[]{:S(2)}) async-start(bf16[16,144,512]{2,1,0:T(8,128)(2,1)} %bitcast.4), calls=%async_computation.2 | async-start | bytes 4718592 | tf_op jit(solution)/shard_map/all_to_all | solution.py:54
  68.2 1.6 broadcast_in_dim.25
  69.8 26.8 %all-to-all-done.2 = bf16[16,144,512]{2,1,0:T(8,128)(2,1)S(1)} async-done(((bf16[16,144,512]{2,1,0:T(8,128)(2,1)}), bf16[16,144,512]{2,1,0:T(8,128)(2,1)S(1)}, u32[]{:S(2)}, u32[]{:S(2)}) %all-to-all-start.2) | async-done | bytes 2359328 | tf_op jit(solution)/shard_map/all_to_all | solution.py:54
  96.6 2.7 %broadcast_in_dim.26 = bf16[16,144,512]{2,1,0:T(8,128)(2,1)} broadcast(bf16[144,512]{1,0:T(8,128)(2,1)} %broadcast_in_dim.25), dimensions={1,2} | broadcast | bytes 2506752 | tf_op jit(solution)/shard_map/broadcast_in_dim | solution.py:49
  99.3 6.3 %all-to-all-start.1 = ((bf16[16,144,512]{2,1,0:T(8,128)(2,1)}), bf16[16,144,512]{2,1,0:T(8,128)(2,1)S(1)}, u32[]{:S(2)}, u32[]{:S(2)}) async-start(bf16[16,144,512]{2,1,0:T(8,128)(2,1)} %broadcast_in_dim.26), calls=%async_computation.1 | async-start | bytes 4718592 | tf_op jit(solution)/shard_map/all_to_all | solution.py:49
  105.7 2.7 %reduce_sum.21 = bf16[144,512]{1,0:T(8,128)(2,1)} reduce(bf16[16,144,512]{2,1,0:T(8,128)(2,1)} %copy-done.9, bf16[]{:T(256)} %constant.71.clone.1), dimensions={0}, to_apply=%region_0.1 | reduce | flops 1105920 | bytes 2506754 | tf_op jit(solution)/shard_map/reduce_sum | solution.py:55
  108.4 1.6 reshape.45
  110.0 23.7 %all-to-all-done.1 = bf16[16,144,512]{2,1,0:T(8,128)(2,1)S(1)} async-done(((bf16[16,144,512]{2,1,0:T(8,128)(2,1)}), bf16[16,144,512]{2,1,0:T(8,128)(2,1)S(1)}, u32[]{:S(2)}, u32[]{:S(2)}) %all-to-all-start.1) | async-done | bytes 2359328 | tf_op jit(solution)/shard_map/all_to_all | solution.py:49
  133.7 4.5 %all-to-all-start.3 = ((bf16[24,6,512]{2,1,0:T(8,128)(2,1)}), bf16[24,6,512]{2,1,0:T(8,128)(2,1)}, u32[]{:S(2)}, u32[]{:S(2)}) async-start(bf16[24,6,512]{2,1,0:T(8,128)(2,1)} %reshape.45), calls=%async_computation.3 | async-start | bytes 393216 | tf_op jit(solution)/shard_map/all_to_all | solution.py:54
  138.2 1.1 copy-done.2
  139.3 0.9 copy-done.6
  140.2 2.2 %shard_map.67 = (bf16[128,2816]{1,0:T(8,128)(2,1)}, f32[128,512]{1,0:T(8,128)S(1)}, bf16[128,2304]{1,0:T(8,128)(2,1)S(1)}) custom-call(s32[1]{0:T(128)} %bitcast.place_ref, bf16[128,4608]{1,0:T(8,128)(2,1)S(1)} %copy-done, bf16[128,512]{1,0:T(8,128)(2,1)S(1)} %copy-done.6, bf16[128,2816]{1,0:T(8,128)(2,1)S(1)} %copy-done.2, bf16[2304,512]{1,0:T(8,128)(2,1)S(1)} %bitcast.5), custom_call_target="tpu_custom_call" | custom-call | flops 1207959552 | bytes 3145728 | tf_op jit(solution)/shard_map/pallas_call | solution.py:65
  142.5 0.8 copy-done.3
  144.0 1.9 %collective-permute-start.2 = (bf16[128,2816]{1,0:T(8,128)(2,1)}, bf16[128,2816]{1,0:T(8,128)(2,1)S(1)}, u32[]{:S(2)}, u32[]{:S(2)}) collective-permute-start(bf16[128,2816]{1,0:T(8,128)(2,1)} %get-tuple-element.10), channel_id=1, source_target_pairs={{0,1},{1,0},{2,3},{3,2},{4,5},{5,4},{6,7},{7,6},{8,9},{9,8},{10,11... | collective-permute-start | bytes 2162696 | tf_op jit(solution)/shard_map/ppermute | solution.py:44
  145.9 9.4 %all-to-all-done.3 = bf16[24,6,512]{2,1,0:T(8,128)(2,1)} async-done(((bf16[24,6,512]{2,1,0:T(8,128)(2,1)}), bf16[24,6,512]{2,1,0:T(8,128)(2,1)}, u32[]{:S(2)}, u32[]{:S(2)}) %all-to-all-start.3) | async-done | bytes 147488 | tf_op jit(solution)/shard_map/all_to_all | solution.py:54
  155.2 1.0 convert_reduce_fusion
  156.2 1.9 %collective-permute-start.3 = (f32[6,512]{1,0:T(8,128)S(1)}, f32[6,512]{1,0:T(8,128)S(1)}, u32[]{:S(2)}, u32[]{:S(2)}) collective-permute-start(f32[6,512]{1,0:T(8,128)S(1)} %broadcast_multiply_fusion), channel_id=1, source_target_pairs={{0,0},{16,1},{32,2},{48,3},{128,4},{144,5},{160,6},{176,7},{256,8}... | collective-permute-start | bytes 36872 | tf_op jit(solution)/shard_map/ppermute | solution.py:165
  158.2 1.1 copy-done.4
  159.2 0.9 copy-done.8
  160.2 1.2 shard_map.68
  161.3 12.8 %collective-permute-done.3 = f32[6,512]{1,0:T(8,128)S(1)} collective-permute-done((f32[6,512]{1,0:T(8,128)S(1)}, f32[6,512]{1,0:T(8,128)S(1)}, u32[]{:S(2)}, u32[]{:S(2)}) %collective-permute-start.3) | collective-permute-done | bytes 12320 | tf_op jit(solution)/shard_map/ppermute | solution.py:165
  (25 shorter events, 2.7 us)
Async XLA Ops:
  0.6 6.9 %copy-start.11 = (bf16[6,512]{1,0:T(8,128)(2,1)S(1)}, bf16[6,512]{1,0:T(8,128)(2,1)}, u32[]{:S(2)}) copy-start(bf16[6,512]{1,0:T(8,128)(2,1)} %param.5) | copy-start | bytes 18436
  0.6 42.2 %copy-start = (bf16[128,4608]{1,0:T(8,128)(2,1)S(1)}, bf16[128,4608]{1,0:T(8,128)(2,1)}, u32[]{:S(2)}) copy-start(bf16[128,4608]{1,0:T(8,128)(2,1)} %tokens_ref.3) | copy-start | bytes 3538948
  0.7 42.2 %copy-start.5 = (bf16[128,512]{1,0:T(8,128)(2,1)S(1)}, bf16[128,512]{1,0:T(8,128)(2,1)}, u32[]{:S(2)}) copy-start(bf16[128,512]{1,0:T(8,128)(2,1)} %grad_ref.3) | copy-start | bytes 393220
  2.8 40.0 %collective-permute-start = (bf16[128,2816]{1,0:T(8,128)(2,1)S(1)}, bf16[128,2816]{1,0:T(8,128)(2,1)S(1)}, u32[]{:S(2)}, u32[]{:S(2)}) collective-permute-start(bf16[128,2816]{1,0:T(8,128)(2,1)S(1)} %pad_maximum_fusion), channel_id=1, source_target_pairs={{0,1},{1,0},{2,3},{3,2},{4,5},{5,4},{6,7},{7,6},{8,9},{9,8},{10,11... | collective-permute-start | bytes 2162696 | tf_op jit(solution)/shard_map/ppermute | solution.py:44
  7.6 20.6 %collective-permute-start.1 = (bf16[6,512]{1,0:T(8,128)(2,1)S(1)}, bf16[6,512]{1,0:T(8,128)(2,1)S(1)}, u32[]{:S(2)}, u32[]{:S(2)}) collective-permute-start(bf16[6,512]{1,0:T(8,128)(2,1)S(1)} %multiply_convert_fusion), channel_id=1, source_target_pairs={{0,0},{1,16},{2,32},{3,48},{4,128},{5,144},{6,160},{7,176},{8,256}... | collective-permute-start | bytes 18440 | tf_op jit(solution)/shard_map/ppermute | solution.py:158
  28.9 30.6 %all-to-all-start = ((bf16[24,6,512]{2,1,0:T(8,128)(2,1)}), bf16[24,6,512]{2,1,0:T(8,128)(2,1)S(1)}, u32[]{:S(2)}, u32[]{:S(2)}) async-start(bf16[24,6,512]{2,1,0:T(8,128)(2,1)} %broadcast_in_dim.24), calls=%async_computation | async-start | bytes 393216 | tf_op jit(solution)/shard_map/all_to_all | solution.py:49
  42.9 2.3 %copy-start.1 = (bf16[128,2816]{1,0:T(8,128)(2,1)}, bf16[128,2816]{1,0:T(8,128)(2,1)S(1)}, u32[]{:S(2)}) copy-start(bf16[128,2816]{1,0:T(8,128)(2,1)S(1)} %collective-permute-done.theirs_ref) | copy-start | bytes 2162692
  59.5 0.7 copy-start.10
  60.2 36.4 %all-to-all-start.2 = ((bf16[16,144,512]{2,1,0:T(8,128)(2,1)}), bf16[16,144,512]{2,1,0:T(8,128)(2,1)S(1)}, u32[]{:S(2)}, u32[]{:S(2)}) async-start(bf16[16,144,512]{2,1,0:T(8,128)(2,1)} %bitcast.4), calls=%async_computation.2 | async-start | bytes 4718592 | tf_op jit(solution)/shard_map/all_to_all | solution.py:54
  96.6 2.7 %copy-start.9 = (bf16[16,144,512]{2,1,0:T(8,128)(2,1)}, bf16[16,144,512]{2,1,0:T(8,128)(2,1)S(1)}, u32[]{:S(2)}) copy-start(bf16[16,144,512]{2,1,0:T(8,128)(2,1)S(1)} %all-to-all-done.2) | copy-start | bytes 7077892
  99.3 34.4 %all-to-all-start.1 = ((bf16[16,144,512]{2,1,0:T(8,128)(2,1)}), bf16[16,144,512]{2,1,0:T(8,128)(2,1)S(1)}, u32[]{:S(2)}, u32[]{:S(2)}) async-start(bf16[16,144,512]{2,1,0:T(8,128)(2,1)} %broadcast_in_dim.26), calls=%async_computation.1 | async-start | bytes 4718592 | tf_op jit(solution)/shard_map/all_to_all | solution.py:49
  133.7 21.5 %all-to-all-start.3 = ((bf16[24,6,512]{2,1,0:T(8,128)(2,1)}), bf16[24,6,512]{2,1,0:T(8,128)(2,1)}, u32[]{:S(2)}, u32[]{:S(2)}) async-start(bf16[24,6,512]{2,1,0:T(8,128)(2,1)} %reshape.45), calls=%async_computation.3 | async-start | bytes 393216 | tf_op jit(solution)/shard_map/all_to_all | solution.py:54
  138.2 1.1 copy-start.2
  139.3 0.9 copy-start.6
  142.5 0.8 copy-start.3
  143.3 0.7 copy-start.7
  144.0 14.2 %collective-permute-start.2 = (bf16[128,2816]{1,0:T(8,128)(2,1)}, bf16[128,2816]{1,0:T(8,128)(2,1)S(1)}, u32[]{:S(2)}, u32[]{:S(2)}) collective-permute-start(bf16[128,2816]{1,0:T(8,128)(2,1)} %get-tuple-element.10), channel_id=1, source_target_pairs={{0,1},{1,0},{2,3},{3,2},{4,5},{5,4},{6,7},{7,6},{8,9},{9,8},{10,11... | collective-permute-start | bytes 2162696 | tf_op jit(solution)/shard_map/ppermute | solution.py:44
  156.2 18.0 %collective-permute-start.3 = (f32[6,512]{1,0:T(8,128)S(1)}, f32[6,512]{1,0:T(8,128)S(1)}, u32[]{:S(2)}, u32[]{:S(2)}) collective-permute-start(f32[6,512]{1,0:T(8,128)S(1)} %broadcast_multiply_fusion), channel_id=1, source_target_pairs={{0,0},{16,1},{32,2},{48,3},{128,4},{144,5},{160,6},{176,7},{256,8}... | collective-permute-start | bytes 36872 | tf_op jit(solution)/shard_map/ppermute | solution.py:165
  158.2 1.1 copy-start.4
  159.2 0.9 copy-start.8

commit v7 on v5

--- a/solution.py
+++ b/solution.py
@@ -10,18 +10,17 @@
 BLOCK_ROWS = 4
 NZ, NY, NX, NC = 12, 8, 4, 2
 AXES = ("z", "y", "x", "c")
-PLANE = ("z", "y")
 BF16 = jnp.bfloat16
 F32 = jnp.float32
 LONG = 10**11
-PARAMS = pltpu.CompilerParams(vmem_limit_bytes=16 * 2**20)
+PARAMS = pltpu.CompilerParams(vmem_limit_bytes=24 * 2**20)
 
 
 def block_moves():
     moves = []
     for block in range(NZ * NY * NX * NC):
-        rest, y = divmod(block, NY)
-        rest, z = divmod(rest, NZ)
+        rest, z = divmod(block, NZ)
+        rest, y = divmod(rest, NY)
         c, x = divmod(rest, NX)
         moves.append((block, ((z * NY + y) * NX + x) * NC + c))
     return moves
@@ -45,26 +44,39 @@
     return lax.ppermute(array, "x", [(i, (i + step) % NX) for i in range(NX)])
 
 
+def gather(rows, axis, size):
+    out = lax.all_to_all(jnp.broadcast_to(rows[None], (size, *rows.shape)), axis, 0, 0)
+    return out.reshape(-1, rows.shape[1])
+
+
+def reduce(rows, axis, size):
+    out = lax.all_to_all(rows.reshape(size, -1, rows.shape[1]), axis, 0, 0)
+    return jnp.sum(out.astype(F32), axis=0)
+
+
 def dot(a, b, over):
     return lax.dot_general(a, b, ((over[:1], over[1:]), ((), ())), preferred_element_type=F32)
 
 
-def call(kernel, outs, scratch, flops, place, *args):
+def whole(shape):
+    return pl.BlockSpec(shape, lambda i, place: (0,) * len(shape))
+
+
+def call(kernel, outs, in_specs, scratch, flops, args):
     moved = sum(math.prod(s.shape) * s.dtype.itemsize for s in outs)
-    vmem = pl.BlockSpec(memory_space=pltpu.VMEM)
     return pl.pallas_call(
         kernel,
         out_shape=outs,
-        in_specs=[pl.BlockSpec(memory_space=pltpu.SMEM), *[vmem] * len(args)],
-        out_specs=[vmem] * len(outs),
-        scratch_shapes=scratch,
+        grid_spec=pltpu.PrefetchScalarGridSpec(
+            num_scalar_prefetch=1,
+            grid=(1,),
+            in_specs=in_specs,
+            out_specs=[whole(s.shape) for s in outs],
+            scratch_shapes=scratch,
+        ),
         compiler_params=PARAMS,
         cost_estimate=pl.CostEstimate(flops=flops, bytes_accessed=2 * moved, transcendentals=0),
-    )(place, *args)
-
-
-def core_columns(place_ref, half):
-    return pl.multiple_of(place_ref[0] * half, half)
+    )(*args)
 
 
 def partials(place, tokens, grad, theirs):
@@ -76,10 +88,10 @@
     def kernel(place_ref, tokens_ref, grad_ref, theirs_ref, *rest):
         outs, total = rest[:NX], rest[NX]
         grads = jnp.concatenate([grad_ref[...], theirs_ref[:, half:]], axis=0)
-        first = core_columns(place_ref, half)
         for k in range(0, half, chunk):
-            mine = tokens_ref[:, pl.ds(pl.multiple_of(first + k, chunk), chunk)]
-            both = jnp.concatenate([mine, theirs_ref[:, k : k + chunk]], axis=0)
+            both = jnp.concatenate(
+                [tokens_ref[:, k : k + chunk], theirs_ref[:, k : k + chunk]], axis=0
+            )
             total[k : k + chunk] = dot(both, grads, (0, 0)).astype(BF16)
         x = place_ref[1]
         for step in range(NX):
@@ -89,12 +101,14 @@
     return call(
         kernel,
         [jax.ShapeDtypeStruct((rows, cols), BF16)] * NX,
+        [
+            pl.BlockSpec((count, half), lambda i, place: (0, place[0])),
+            whole(grad.shape),
+            whole(theirs.shape),
+        ],
         [pltpu.VMEM((half, cols), BF16)],
         4 * count * half * cols,
-        place,
-        tokens,
-        grad,
-        theirs,
+        (place, tokens, grad, theirs),
     )
 
 
@@ -109,8 +123,7 @@
         for step in range(NX):
             block = lax.rem(x + NX - step, NX)
             weights[pl.ds(pl.multiple_of(block * rows, rows), rows), :] = block_refs[step][...]
-        mine = tokens_ref[:, pl.ds(core_columns(place_ref, half), half)]
-        tokens_both = jnp.concatenate([theirs_ref[:, :half], mine], axis=0)
+        tokens_both = jnp.concatenate([theirs_ref[:, :half], tokens_ref[...]], axis=0)
         part = dot(tokens_both, weights[...], (1, 0))
         for_them[:, half:] = part[:count].astype(BF16)
         part_ref[...] = part[count:]
@@ -126,13 +139,15 @@
             jax.ShapeDtypeStruct((count, cols), F32),
             jax.ShapeDtypeStruct((count, half), BF16),
         ],
+        [
+            pl.BlockSpec((count, half), lambda i, place: (0, place[0])),
+            whole(grad.shape),
+            whole(theirs.shape),
+            *[whole(b.shape) for b in blocks],
+        ],
         [pltpu.VMEM((half, cols), BF16)],
-        LONG,
-        place,
-        tokens,
-        grad,
-        theirs,
-        *blocks,
+        8 * count * half * cols,
+        (place, tokens, grad, theirs, *blocks),
     )
 
 
@@ -142,7 +157,7 @@
         out_ref[...] = sum(p[...].astype(F32) for p in part_refs).astype(BF16)
 
     out = jax.ShapeDtypeStruct(parts[0].shape, BF16)
-    return call(kernel, [out], [], LONG, place, *parts)[0]
+    return call(kernel, [out], [whole(p.shape) for p in parts], [], LONG, (place, *parts))[0]
 
 
 def assemble(place, part, columns, received):
@@ -169,12 +184,10 @@
             jax.ShapeDtypeStruct((count, cols), BF16),
             jax.ShapeDtypeStruct((count, NC * half), BF16),
         ],
+        [whole(part.shape), whole(columns.shape), whole(received.shape)],
         [],
         count * cols,
-        place,
-        part,
-        columns,
-        received,
+        (place, part, columns, received),
     )
 
 
@@ -186,27 +199,26 @@
     cols = out_grad.shape[1]
     others = lax.dynamic_slice(tokens, (0, (1 - core) * half), (tokens.shape[0], half))
     theirs = swap(jnp.concatenate([others, out_grad], axis=1))
-    rows = scaled_rows(w_values, w_scales)
+    rows = lax.ppermute(scaled_rows(w_values, w_scales), AXES, moves)
 
     parts = partials(place, tokens, out_grad, theirs)
     rows, *parts = lax.optimization_barrier((rows, *parts))
-    rows = lax.ppermute(rows, AXES, moves)
     parts = [parts[0], *(along_x(parts[step], step) for step in range(1, NX))]
 
-    rows = lax.all_to_all(jnp.broadcast_to(rows[None], (NZ * NY, *rows.shape)), PLANE, 0, 0)
-    rows = rows.reshape(-1, cols)
+    rows = gather(gather(rows, "z", NZ), "y", NY)
     total = add_up(place, parts)
     total, rows = lax.optimization_barrier((total, rows))
     blocks = [rows, *(along_x(rows, step) for step in range(1, NX))]
-    total = lax.all_to_all(total.reshape(NZ * NY, -1, cols), PLANE, 0, 0)
-    total = jnp.sum(total.astype(F32), axis=0)
+
+    total = reduce(total, "y", NY).astype(BF16)
+    for_them, part, columns = forward(place, tokens, out_grad, theirs, blocks)
+    total, for_them = lax.optimization_barrier((total, for_them))
+    received = swap(for_them)
+    total = reduce(total, "z", NZ)
     count = tokens.shape[0] * NZ * NY * NX * NC
     weight_grad = lax.ppermute(
         total * (1.0 / math.sqrt(count)), AXES, [(b, a) for a, b in moves]
     )
-
-    for_them, part, columns = forward(place, tokens, out_grad, theirs, blocks)
-    received = swap(for_them)
     projected, token_grad = assemble(place, part, columns, received)
     return projected, token_grad, weight_grad
 

time: 166 us -> 154 us (0.928)
  the two profiles are of different devices: /device:TPU:150 before, /device:TPU:92 now
where the time goes in v7:
time: 154 us; the launch traced here: 153 us
  starting transfers between devices  58 us (38%)
  waiting for transfers between devices  37.7 us (24%)
  blocking collectives  37.5 us (24%)
  Pallas kernels  9.43 us (6%)
  local copies, waits for them, and re-layouts  6.92 us (4%)
  other arithmetic  2.72 us (2%)
    all_to_all x1, blocking collectives, gather(): lax.all_to_all(jnp.broadcast_to(rows[None], (size, *rows.shape)), axis, 0...  20.8 us
    ppermute x6, starting transfers between devices, along_x(): return lax.ppermute(array, 'x', [(i, (i + step) % NX) for i in range(NX)])  19.6 us
    all_to_all x1, blocking collectives, reduce(): out = lax.all_to_all(rows.reshape(size, -1, rows.shape[1]), axis, 0, 0)  16.7 us
    ppermute x6, waiting for transfers between devices, along_x(): return lax.ppermute(array, 'x', [(i, (i + step) % NX) for i in range(NX)])  16.5 us
    ppermute x1, starting transfers between devices, body(): rows = lax.ppermute(scaled_rows(w_values, w_scales), AXES, moves)  16.1 us
    ppermute x1, waiting for transfers between devices, body(): lax.ppermute(total * (1.0 / math.sqrt(count)), AXES, [(b, a) for a, b in...  13.9 us
    pallas_call x4, Pallas kernels, call(): pl.pallas_call(kernel, out_shape=outs, grid_spec=pltpu.PrefetchScalarGrid...  9.43 us
    all_to_all x1, starting transfers between devices, gather(): lax.all_to_all(jnp.broadcast_to(rows[None], (size, *rows.shape)), axis, 0...  8.01 us
  transfers between devices with their start and end apart: 12, of which 5 were waited for; matrix products, arithmetic and copies ran while one was open for 3% of the time, Pallas kernels for 5%

profile of v7, /device:TPU:92, one launch (start us, length us, event | category | flops | bytes accessed | tf_op | source)
XLA Modules:
  0.0 153.1 jit_solution(1604161148325756680)
XLA Ops:
  0.7 1.2 constant_dynamic-slice_fusion
  1.9 1.9 %collective-permute-start = (bf16[128,2816]{1,0:T(8,128)(2,1)S(1)}, bf16[128,2816]{1,0:T(8,128)(2,1)S(1)}, u32[]{:S(2)}, u32[]{:S(2)}) collective-permute-start(bf16[128,2816]{1,0:T(8,128)(2,1)S(1)} %pad_maximum_fusion), channel_id=1, source_target_pairs={{0,1},{1,0},{2,3},{3,2},{4,5},{5,4},{6,7},{7,6},{8,9},{9,8},{10,11... | collective-permute-start | bytes 2162696 | tf_op jit(solution)/shard_map/ppermute | solution.py:40
  3.9 0.8 dynamic_slice.7
  4.7 0.7 fusion
  5.4 1.3 compare_select_fusion
  6.8 16.1 %collective-permute-start.1 = (bf16[6,512]{1,0:T(8,128)(2,1)S(1)}, bf16[6,512]{1,0:T(8,128)(2,1)S(1)}, u32[]{:S(2)}, u32[]{:S(2)}) collective-permute-start(bf16[6,512]{1,0:T(8,128)(2,1)S(1)} %multiply_convert_fusion), channel_id=1, source_target_pairs={{0,0},{1,64},{2,128},{3,192},{4,256},{5,320},{6,384},{7,448},{8,51... | collective-permute-start | bytes 18440 | tf_op jit(solution)/shard_map/ppermute | solution.py:202
  23.0 2.5 %shard_map.67 = (bf16[576,512]{1,0:T(8,128)(2,1)S(1)}, bf16[576,512]{1,0:T(8,128)(2,1)}, bf16[576,512]{1,0:T(8,128)(2,1)}, bf16[576,512]{1,0:T(8,128)(2,1)S(1)}) custom-call(s32[2]{0:T(128)S(1)} %pad_add_fusion.place_ref, bf16[128,4608]{1,0:T(8,128)(2,1)S(1)} %copy-done, bf16[128,512]{1,0:T(8,128)(2,1)S(1)} %copy-done.1, ...), custom_call_target="tpu_custom_call" | custom-call | flops 603979776 | bytes 4718592 | tf_op jit(solution)/shard_map/pallas_call | solution.py:67
  25.5 0.8 copy-done.3
  26.4 3.1 %collective-permute-start.2 = (bf16[576,512]{1,0:T(8,128)(2,1)}, bf16[576,512]{1,0:T(8,128)(2,1)}, u32[]{:S(2)}, u32[]{:S(2)}) collective-permute-start(bf16[576,512]{1,0:T(8,128)(2,1)} %get-tuple-element.26), channel_id=1, source_target_pairs={{0,2},{2,4},{4,6},{6,0},{1,3},{3,5},{5,7},{7,1},{8,10},{10,12},{12... | collective-permute-start | bytes 1769480 | tf_op jit(solution)/shard_map/ppermute | solution.py:44
  29.5 1.9 %collective-permute-start.3 = (bf16[576,512]{1,0:T(8,128)(2,1)}, bf16[576,512]{1,0:T(8,128)(2,1)}, u32[]{:S(2)}, u32[]{:S(2)}) collective-permute-start(bf16[576,512]{1,0:T(8,128)(2,1)} %get-tuple-element.27), channel_id=1, source_target_pairs={{0,4},{2,6},{4,0},{6,2},{1,5},{3,7},{5,1},{7,3},{8,12},{10,14},{12... | collective-permute-start | bytes 1769480 | tf_op jit(solution)/shard_map/ppermute | solution.py:44
  31.4 3.4 %collective-permute-start.4 = (bf16[576,512]{1,0:T(8,128)(2,1)S(1)}, bf16[576,512]{1,0:T(8,128)(2,1)}, u32[]{:S(2)}, u32[]{:S(2)}) collective-permute-start(bf16[576,512]{1,0:T(8,128)(2,1)S(1)} %get-tuple-element.28), channel_id=1, source_target_pairs={{0,6},{2,0},{4,2},{6,4},{1,7},{3,1},{5,3},{7,5},{8,14},{10,8},{12,... | collective-permute-start | bytes 1769480 | tf_op jit(solution)/shard_map/ppermute | solution.py:44
  34.8 20.8 %all_to_all.20 = bf16[12,6,512]{2,1,0:T(8,128)(2,1)S(1)} all-to-all(bf16[12,6,512]{2,1,0:T(8,128)(2,1)S(1)} %broadcast_in_dim.24), channel_id=1, replica_groups=mesh['z'=12,'y'=8,'x'=4,'c'=2] {'z'}, dimensions={0} | all-to-all | bytes 147456 | tf_op jit(solution)/shard_map/all_to_all | solution.py:48
  55.6 0.9 broadcast_in_dim.26
  56.5 8.0 %all-to-all-start.1 = ((bf16[8,72,512]{2,1,0:T(8,128)(2,1)}), bf16[8,72,512]{2,1,0:T(8,128)(2,1)S(1)}, u32[]{:S(2)}, u32[]{:S(2)}) async-start(bf16[8,72,512]{2,1,0:T(8,128)(2,1)} %broadcast_in_dim.26), calls=%async_computation.1 | async-start | bytes 1179648 | tf_op jit(solution)/shard_map/all_to_all | solution.py:48
  64.5 1.1 copy-done.4
  65.6 3.1 %shard_map.68 = bf16[576,512]{1,0:T(8,128)(2,1)} custom-call(s32[2]{0:T(128)S(1)} %pad_add_fusion.place_ref, bf16[576,512]{1,0:T(8,128)(2,1)S(1)} %copy-done.4, bf16[576,512]{1,0:T(8,128)(2,1)} %collective-permute-done.2.refs_1_, bf16[576,512]{1,0:T(8,128)(2,1)} %collective-permute-done.3.refs_2_, bf16[576,512]{1,0:T(8,128)(2,1)} %collective-permute-done.4.refs_3_), custom_call_target="tpu_custom_call" | custom-call | flops 99999997952 | bytes 1179648 | tf_op jit(solution)/shard_map/pallas_call | solution.py:67
  68.6 7.2 %all-to-all-done.1 = bf16[8,72,512]{2,1,0:T(8,128)(2,1)S(1)} async-done(((bf16[8,72,512]{2,1,0:T(8,128)(2,1)}), bf16[8,72,512]{2,1,0:T(8,128)(2,1)S(1)}, u32[]{:S(2)}, u32[]{:S(2)}) %all-to-all-start.1) | async-done | bytes 589856 | tf_op jit(solution)/shard_map/all_to_all | solution.py:48
  75.9 6.7 %all-to-all-start.2 = ((bf16[8,72,512]{2,1,0:T(8,128)(2,1)}), bf16[8,72,512]{2,1,0:T(8,128)(2,1)}, u32[]{:S(2)}, u32[]{:S(2)}) async-start(bf16[8,72,512]{2,1,0:T(8,128)(2,1)} %bitcast.5), calls=%async_computation.2 | async-start | bytes 1179648 | tf_op jit(solution)/shard_map/all_to_all | solution.py:53
  82.6 3.8 %collective-permute-start.7 = (bf16[576,512]{1,0:T(8,128)(2,1)S(1)}, bf16[576,512]{1,0:T(8,128)(2,1)S(1)}, u32[]{:S(2)}, u32[]{:S(2)}) collective-permute-start(bf16[576,512]{1,0:T(8,128)(2,1)S(1)} %bitcast.6), channel_id=1, source_target_pairs={{0,6},{2,0},{4,2},{6,4},{1,7},{3,1},{5,3},{7,5},{8,14},{10,8},{12,... | collective-permute-start | bytes 1769480 | tf_op jit(solution)/shard_map/ppermute | solution.py:44
  86.4 3.1 %collective-permute-start.6 = (bf16[576,512]{1,0:T(8,128)(2,1)S(1)}, bf16[576,512]{1,0:T(8,128)(2,1)S(1)}, u32[]{:S(2)}, u32[]{:S(2)}) collective-permute-start(bf16[576,512]{1,0:T(8,128)(2,1)S(1)} %bitcast.7), channel_id=1, source_target_pairs={{0,4},{2,6},{4,0},{6,2},{1,5},{3,7},{5,1},{7,3},{8,12},{10,14},{12... | collective-permute-start | bytes 1769480 | tf_op jit(solution)/shard_map/ppermute | solution.py:44
  89.5 4.3 %collective-permute-start.5 = (bf16[576,512]{1,0:T(8,128)(2,1)S(1)}, bf16[576,512]{1,0:T(8,128)(2,1)S(1)}, u32[]{:S(2)}, u32[]{:S(2)}) collective-permute-start(bf16[576,512]{1,0:T(8,128)(2,1)S(1)} %bitcast.8), channel_id=1, source_target_pairs={{0,2},{2,4},{4,6},{6,0},{1,3},{3,5},{5,7},{7,1},{8,10},{10,12},{12... | collective-permute-start | bytes 1769480 | tf_op jit(solution)/shard_map/ppermute | solution.py:44
  93.8 5.4 %collective-permute-done.7.rest_3_ = bf16[576,512]{1,0:T(8,128)(2,1)S(1)} collective-permute-done((bf16[576,512]{1,0:T(8,128)(2,1)S(1)}, bf16[576,512]{1,0:T(8,128)(2,1)S(1)}, u32[]{:S(2)}, u32[]{:S(2)}) %collective-permute-start.7) | collective-permute-done | bytes 589856 | tf_op jit(solution)/shard_map/ppermute | solution.py:44
  99.2 4.9 %collective-permute-done.6.rest_2_ = bf16[576,512]{1,0:T(8,128)(2,1)S(1)} collective-permute-done((bf16[576,512]{1,0:T(8,128)(2,1)S(1)}, bf16[576,512]{1,0:T(8,128)(2,1)S(1)}, u32[]{:S(2)}, u32[]{:S(2)}) %collective-permute-start.6) | collective-permute-done | bytes 589856 | tf_op jit(solution)/shard_map/ppermute | solution.py:44
  104.1 6.2 %collective-permute-done.5.rest_1_ = bf16[576,512]{1,0:T(8,128)(2,1)S(1)} collective-permute-done((bf16[576,512]{1,0:T(8,128)(2,1)S(1)}, bf16[576,512]{1,0:T(8,128)(2,1)S(1)}, u32[]{:S(2)}, u32[]{:S(2)}) %collective-permute-start.5) | collective-permute-done | bytes 589856 | tf_op jit(solution)/shard_map/ppermute | solution.py:44
  110.3 2.1 %shard_map.69 = (bf16[128,2816]{1,0:T(8,128)(2,1)S(1)}, f32[128,512]{1,0:T(8,128)S(1)}, bf16[128,2304]{1,0:T(8,128)(2,1)S(1)}) custom-call(s32[2]{0:T(128)S(1)} %pad_add_fusion.place_ref, bf16[128,4608]{1,0:T(8,128)(2,1)S(1)} %copy-done, bf16[128,512]{1,0:T(8,128)(2,1)S(1)} %copy-done.1, bf16[128,2816]{1,0:T(8,128)(2,1)S(1)} %collective-permute-done.theirs_ref, ...), custom_call_target="tpu_custom_call" | custom-call | flops 1207959552 | bytes 3145728 | tf_op jit(solution)/shard_map/pallas_call | solution.py:67
  112.4 0.8 copy-done.2
  113.3 1.1 reduce_sum.21
  114.4 1.9 %collective-permute-start.8 = (bf16[128,2816]{1,0:T(8,128)(2,1)}, bf16[128,2816]{1,0:T(8,128)(2,1)S(1)}, u32[]{:S(2)}, u32[]{:S(2)}) collective-permute-start(bf16[128,2816]{1,0:T(8,128)(2,1)} %copy-done.2), channel_id=1, source_target_pairs={{0,1},{1,0},{2,3},{3,2},{4,5},{5,4},{6,7},{7,6},{8,9},{9,8},{10,11... | collective-permute-start | bytes 2162696 | tf_op jit(solution)/shard_map/ppermute | solution.py:40
  116.4 16.7 %all_to_all.21 = bf16[12,6,512]{2,1,0:T(8,128)(2,1)S(1)} all-to-all(bf16[12,6,512]{2,1,0:T(8,128)(2,1)S(1)} %reshape.41), channel_id=1, replica_groups=mesh['z'=12,'y'=8,'x'=4,'c'=2] {'z'}, dimensions={0} | all-to-all | bytes 147456 | tf_op jit(solution)/shard_map/all_to_all | solution.py:53
  133.2 3.7 %collective-permute-start.9 = (f32[6,512]{1,0:T(8,128)S(1)}, f32[6,512]{1,0:T(8,128)S(1)}, u32[]{:S(2)}, u32[]{:S(2)}) collective-permute-start(f32[6,512]{1,0:T(8,128)S(1)} %broadcast_multiply_fusion), channel_id=1, source_target_pairs={{0,0},{64,1},{128,2},{192,3},{256,4},{320,5},{384,6},{448,7},{512,... | collective-permute-start | bytes 36872 | tf_op jit(solution)/shard_map/ppermute | solution.py:219
  136.9 13.9 %collective-permute-done.9 = f32[6,512]{1,0:T(8,128)S(1)} collective-permute-done((f32[6,512]{1,0:T(8,128)S(1)}, f32[6,512]{1,0:T(8,128)S(1)}, u32[]{:S(2)}, u32[]{:S(2)}) %collective-permute-start.9) | collective-permute-done | bytes 12320 | tf_op jit(solution)/shard_map/ppermute | solution.py:219
  150.8 1.7 %shard_map.70 = (bf16[128,512]{1,0:T(8,128)(2,1)}, bf16[128,4608]{1,0:T(8,128)(2,1)}) custom-call(s32[2]{0:T(128)S(1)} %pad_add_fusion.place_ref, f32[128,512]{1,0:T(8,128)S(1)} %get-tuple-element.31.part_ref, bf16[128,2304]{1,0:T(8,128)(2,1)S(1)} %get-tuple-element.32.columns_ref, bf16[128,2816]{1,0:T(8,128)(2,1)S(1)} %collective-permute-done.8.received_ref), custom_call_target="tpu_custom_call" | custom-call | flops 65536 | bytes 2621440 | tf_op jit(solution)/shard_map/pallas_call | solution.py:67
  (25 shorter events, 0.9 us)
Async XLA Ops:
  0.6 1.2 copy-start.1
  0.6 6.1 %copy-start.5 = (bf16[6,512]{1,0:T(8,128)(2,1)S(1)}, bf16[6,512]{1,0:T(8,128)(2,1)}, u32[]{:S(2)}) copy-start(bf16[6,512]{1,0:T(8,128)(2,1)} %param.5) | copy-start | bytes 18436
  0.7 22.4 %copy-start = (bf16[128,4608]{1,0:T(8,128)(2,1)S(1)}, bf16[128,4608]{1,0:T(8,128)(2,1)}, u32[]{:S(2)}) copy-start(bf16[128,4608]{1,0:T(8,128)(2,1)} %tokens_ref.3) | copy-start | bytes 3538948
  1.9 21.1 %collective-permute-start = (bf16[128,2816]{1,0:T(8,128)(2,1)S(1)}, bf16[128,2816]{1,0:T(8,128)(2,1)S(1)}, u32[]{:S(2)}, u32[]{:S(2)}) collective-permute-start(bf16[128,2816]{1,0:T(8,128)(2,1)S(1)} %pad_maximum_fusion), channel_id=1, source_target_pairs={{0,1},{1,0},{2,3},{3,2},{4,5},{5,4},{6,7},{7,6},{8,9},{9,8},{10,11... | collective-permute-start | bytes 2162696 | tf_op jit(solution)/shard_map/ppermute | solution.py:40
  6.8 19.6 %collective-permute-start.1 = (bf16[6,512]{1,0:T(8,128)(2,1)S(1)}, bf16[6,512]{1,0:T(8,128)(2,1)S(1)}, u32[]{:S(2)}, u32[]{:S(2)}) collective-permute-start(bf16[6,512]{1,0:T(8,128)(2,1)S(1)} %multiply_convert_fusion), channel_id=1, source_target_pairs={{0,0},{1,64},{2,128},{3,192},{4,256},{5,320},{6,384},{7,448},{8,51... | collective-permute-start | bytes 18440 | tf_op jit(solution)/shard_map/ppermute | solution.py:202
  25.5 0.8 copy-start.3
  26.4 38.1 %collective-permute-start.2 = (bf16[576,512]{1,0:T(8,128)(2,1)}, bf16[576,512]{1,0:T(8,128)(2,1)}, u32[]{:S(2)}, u32[]{:S(2)}) collective-permute-start(bf16[576,512]{1,0:T(8,128)(2,1)} %get-tuple-element.26), channel_id=1, source_target_pairs={{0,2},{2,4},{4,6},{6,0},{1,3},{3,5},{5,7},{7,1},{8,10},{10,12},{12... | collective-permute-start | bytes 1769480 | tf_op jit(solution)/shard_map/ppermute | solution.py:44
  29.5 35.0 %collective-permute-start.3 = (bf16[576,512]{1,0:T(8,128)(2,1)}, bf16[576,512]{1,0:T(8,128)(2,1)}, u32[]{:S(2)}, u32[]{:S(2)}) collective-permute-start(bf16[576,512]{1,0:T(8,128)(2,1)} %get-tuple-element.27), channel_id=1, source_target_pairs={{0,4},{2,6},{4,0},{6,2},{1,5},{3,7},{5,1},{7,3},{8,12},{10,14},{12... | collective-permute-start | bytes 1769480 | tf_op jit(solution)/shard_map/ppermute | solution.py:44
  31.4 33.1 %collective-permute-start.4 = (bf16[576,512]{1,0:T(8,128)(2,1)S(1)}, bf16[576,512]{1,0:T(8,128)(2,1)}, u32[]{:S(2)}, u32[]{:S(2)}) collective-permute-start(bf16[576,512]{1,0:T(8,128)(2,1)S(1)} %get-tuple-element.28), channel_id=1, source_target_pairs={{0,6},{2,0},{4,2},{6,4},{1,7},{3,1},{5,3},{7,5},{8,14},{10,8},{12,... | collective-permute-start | bytes 1769480 | tf_op jit(solution)/shard_map/ppermute | solution.py:44
  56.5 19.4 %all-to-all-start.1 = ((bf16[8,72,512]{2,1,0:T(8,128)(2,1)}), bf16[8,72,512]{2,1,0:T(8,128)(2,1)S(1)}, u32[]{:S(2)}, u32[]{:S(2)}) async-start(bf16[8,72,512]{2,1,0:T(8,128)(2,1)} %broadcast_in_dim.26), calls=%async_computation.1 | async-start | bytes 1179648 | tf_op jit(solution)/shard_map/all_to_all | solution.py:48
  64.5 1.1 copy-start.4
  75.9 37.4 %all-to-all-start.2 = ((bf16[8,72,512]{2,1,0:T(8,128)(2,1)}), bf16[8,72,512]{2,1,0:T(8,128)(2,1)}, u32[]{:S(2)}, u32[]{:S(2)}) async-start(bf16[8,72,512]{2,1,0:T(8,128)(2,1)} %bitcast.5), calls=%async_computation.2 | async-start | bytes 1179648 | tf_op jit(solution)/shard_map/all_to_all | solution.py:53
  82.6 16.6 %collective-permute-start.7 = (bf16[576,512]{1,0:T(8,128)(2,1)S(1)}, bf16[576,512]{1,0:T(8,128)(2,1)S(1)}, u32[]{:S(2)}, u32[]{:S(2)}) collective-permute-start(bf16[576,512]{1,0:T(8,128)(2,1)S(1)} %bitcast.6), channel_id=1, source_target_pairs={{0,6},{2,0},{4,2},{6,4},{1,7},{3,1},{5,3},{7,5},{8,14},{10,8},{12,... | collective-permute-start | bytes 1769480 | tf_op jit(solution)/shard_map/ppermute | solution.py:44
  86.4 17.7 %collective-permute-start.6 = (bf16[576,512]{1,0:T(8,128)(2,1)S(1)}, bf16[576,512]{1,0:T(8,128)(2,1)S(1)}, u32[]{:S(2)}, u32[]{:S(2)}) collective-permute-start(bf16[576,512]{1,0:T(8,128)(2,1)S(1)} %bitcast.7), channel_id=1, source_target_pairs={{0,4},{2,6},{4,0},{6,2},{1,5},{3,7},{5,1},{7,3},{8,12},{10,14},{12... | collective-permute-start | bytes 1769480 | tf_op jit(solution)/shard_map/ppermute | solution.py:44
  89.5 20.8 %collective-permute-start.5 = (bf16[576,512]{1,0:T(8,128)(2,1)S(1)}, bf16[576,512]{1,0:T(8,128)(2,1)S(1)}, u32[]{:S(2)}, u32[]{:S(2)}) collective-permute-start(bf16[576,512]{1,0:T(8,128)(2,1)S(1)} %bitcast.8), channel_id=1, source_target_pairs={{0,2},{2,4},{4,6},{6,0},{1,3},{3,5},{5,7},{7,1},{8,10},{10,12},{12... | collective-permute-start | bytes 1769480 | tf_op jit(solution)/shard_map/ppermute | solution.py:44
  112.4 0.9 copy-start.2
  114.4 36.4 %collective-permute-start.8 = (bf16[128,2816]{1,0:T(8,128)(2,1)}, bf16[128,2816]{1,0:T(8,128)(2,1)S(1)}, u32[]{:S(2)}, u32[]{:S(2)}) collective-permute-start(bf16[128,2816]{1,0:T(8,128)(2,1)} %copy-done.2), channel_id=1, source_target_pairs={{0,1},{1,0},{2,3},{3,2},{4,5},{5,4},{6,7},{7,6},{8,9},{9,8},{10,11... | collective-permute-start | bytes 2162696 | tf_op jit(solution)/shard_map/ppermute | solution.py:40
  133.2 17.6 %collective-permute-start.9 = (f32[6,512]{1,0:T(8,128)S(1)}, f32[6,512]{1,0:T(8,128)S(1)}, u32[]{:S(2)}, u32[]{:S(2)}) collective-permute-start(f32[6,512]{1,0:T(8,128)S(1)} %broadcast_multiply_fusion), channel_id=1, source_target_pairs={{0,0},{64,1},{128,2},{192,3},{256,4},{320,5},{384,6},{448,7},{512,... | collective-permute-start | bytes 36872 | tf_op jit(solution)/shard_map/ppermute | solution.py:219

commit v8 on v7

--- a/solution.py
+++ b/solution.py
@@ -201,25 +201,26 @@
     theirs = swap(jnp.concatenate([others, out_grad], axis=1))
     rows = lax.ppermute(scaled_rows(w_values, w_scales), AXES, moves)
 
+    rows = gather(rows, "z", NZ)
+    theirs, rows = lax.optimization_barrier((theirs, rows))
+
     parts = partials(place, tokens, out_grad, theirs)
     rows, *parts = lax.optimization_barrier((rows, *parts))
     parts = [parts[0], *(along_x(parts[step], step) for step in range(1, NX))]
-
-    rows = gather(gather(rows, "z", NZ), "y", NY)
+    rows = gather(rows, "y", NY)
     total = add_up(place, parts)
     total, rows = lax.optimization_barrier((total, rows))
     blocks = [rows, *(along_x(rows, step) for step in range(1, NX))]
 
     total = reduce(total, "y", NY).astype(BF16)
-    for_them, part, columns = forward(place, tokens, out_grad, theirs, blocks)
-    total, for_them = lax.optimization_barrier((total, for_them))
-    received = swap(for_them)
     total = reduce(total, "z", NZ)
+    total, *blocks = lax.optimization_barrier((total, *blocks))
     count = tokens.shape[0] * NZ * NY * NX * NC
     weight_grad = lax.ppermute(
         total * (1.0 / math.sqrt(count)), AXES, [(b, a) for a, b in moves]
     )
-    projected, token_grad = assemble(place, part, columns, received)
+    for_them, part, columns = forward(place, tokens, out_grad, theirs, blocks)
+    projected, token_grad = assemble(place, part, columns, swap(for_them))
     return projected, token_grad, weight_grad
 
 

time: 154 us -> 153 us (level)
  the two profiles are of different devices: /device:TPU:92 before, /device:TPU:67 now
where the time goes in v8:
time: 153 us
  starting transfers between devices  73.5 us (48%)
  waiting for transfers between devices  44.4 us (29%)
  blocking collectives  13.8 us (9%)
  Pallas kernels  10.7 us (7%)
  local copies, waits for them, and re-layouts  6.68 us (4%)
  other arithmetic  2.72 us (2%)
    ppermute x6, starting transfers between devices, along_x(): return lax.ppermute(array, 'x', [(i, (i + step) % NX) for i in range(NX)])  19.4 us
    ppermute x1, starting transfers between devices, body(): rows = lax.ppermute(scaled_rows(w_values, w_scales), AXES, moves)  18.3 us
    all_to_all x1, blocking collectives, reduce(): out = lax.all_to_all(rows.reshape(size, -1, rows.shape[1]), axis, 0, 0)  13.8 us
    ppermute x6, waiting for transfers between devices, along_x(): return lax.ppermute(array, 'x', [(i, (i + step) % NX) for i in range(NX)])  12.8 us
    all_to_all x2, starting transfers between devices, gather(): lax.all_to_all(jnp.broadcast_to(rows[None], (size, *rows.shape)), axis, 0...  11.8 us
    all_to_all x1, starting transfers between devices, reduce(): out = lax.all_to_all(rows.reshape(size, -1, rows.shape[1]), axis, 0, 0)  11.2 us
    all_to_all x1, waiting for transfers between devices, reduce(): out = lax.all_to_all(rows.reshape(size, -1, rows.shape[1]), axis, 0, 0)  11.2 us
    pallas_call x4, Pallas kernels, call(): pl.pallas_call(kernel, out_shape=outs, grid_spec=pltpu.PrefetchScalarGrid...  10.7 us
  transfers between devices with their start and end apart: 13, of which 5 were waited for; matrix products, arithmetic and copies ran while one was open for 4% of the time, Pallas kernels for 2%

profile of v8, /device:TPU:67, one launch (start us, length us, event | category | flops | bytes accessed | tf_op | source)
XLA Modules:
  0.0 152.6 jit_solution(11613514984684987040)
XLA Ops:
  0.7 1.2 constant_dynamic-slice_fusion
  1.9 2.7 %collective-permute-start = (bf16[128,2816]{1,0:T(8,128)(2,1)S(1)}, bf16[128,2816]{1,0:T(8,128)(2,1)S(1)}, u32[]{:S(2)}, u32[]{:S(2)}) collective-permute-start(bf16[128,2816]{1,0:T(8,128)(2,1)S(1)} %pad_maximum_fusion), channel_id=1, source_target_pairs={{0,1},{1,0},{2,3},{3,2},{4,5},{5,4},{6,7},{7,6},{8,9},{9,8},{10,11... | collective-permute-start | bytes 2162696 | tf_op jit(solution)/shard_map/ppermute | solution.py:40
  4.7 0.8 dynamic_slice.7
  5.4 0.7 fusion
  6.1 1.3 compare_select_fusion
  7.5 18.3 %collective-permute-start.1 = (bf16[6,512]{1,0:T(8,128)(2,1)S(1)}, bf16[6,512]{1,0:T(8,128)(2,1)S(1)}, u32[]{:S(2)}, u32[]{:S(2)}) collective-permute-start(bf16[6,512]{1,0:T(8,128)(2,1)S(1)} %multiply_convert_fusion), channel_id=1, source_target_pairs={{0,0},{1,64},{2,128},{3,192},{4,256},{5,320},{6,384},{7,448},{8,51... | collective-permute-start | bytes 18440 | tf_op jit(solution)/shard_map/ppermute | solution.py:202
  25.8 1.9 %collective-permute-done.1 = bf16[6,512]{1,0:T(8,128)(2,1)S(1)} collective-permute-done((bf16[6,512]{1,0:T(8,128)(2,1)S(1)}, bf16[6,512]{1,0:T(8,128)(2,1)S(1)}, u32[]{:S(2)}, u32[]{:S(2)}) %collective-permute-start.1) | collective-permute-done | bytes 6176 | tf_op jit(solution)/shard_map/ppermute | solution.py:202
  27.8 0.6 broadcast_in_dim.23
  28.4 5.6 %all-to-all-start = ((bf16[12,6,512]{2,1,0:T(8,128)(2,1)}), bf16[12,6,512]{2,1,0:T(8,128)(2,1)S(1)}, u32[]{:S(2)}, u32[]{:S(2)}) async-start(bf16[12,6,512]{2,1,0:T(8,128)(2,1)} %broadcast_in_dim.23), calls=%async_computation | async-start | bytes 196608 | tf_op jit(solution)/shard_map/all_to_all | solution.py:48
  34.1 9.3 %all-to-all-done = bf16[12,6,512]{2,1,0:T(8,128)(2,1)S(1)} async-done(((bf16[12,6,512]{2,1,0:T(8,128)(2,1)}), bf16[12,6,512]{2,1,0:T(8,128)(2,1)S(1)}, u32[]{:S(2)}, u32[]{:S(2)}) %all-to-all-start) | async-done | bytes 73760 | tf_op jit(solution)/shard_map/all_to_all | solution.py:48
  43.4 2.5 %shard_map.67 = (bf16[576,512]{1,0:T(8,128)(2,1)S(1)}, bf16[576,512]{1,0:T(8,128)(2,1)}, bf16[576,512]{1,0:T(8,128)(2,1)}, bf16[576,512]{1,0:T(8,128)(2,1)S(1)}) custom-call(s32[2]{0:T(128)S(1)} %pad_add_fusion.place_ref, bf16[128,4608]{1,0:T(8,128)(2,1)S(1)} %copy-done, bf16[128,512]{1,0:T(8,128)(2,1)S(1)} %copy-done.1, ...), custom_call_target="tpu_custom_call" | custom-call | flops 603979776 | bytes 4718592 | tf_op jit(solution)/shard_map/pallas_call | solution.py:67
  45.9 0.8 copy-done.2
  46.8 1.9 %collective-permute-start.2 = (bf16[576,512]{1,0:T(8,128)(2,1)}, bf16[576,512]{1,0:T(8,128)(2,1)}, u32[]{:S(2)}, u32[]{:S(2)}) collective-permute-start(bf16[576,512]{1,0:T(8,128)(2,1)} %get-tuple-element.33), channel_id=1, source_target_pairs={{0,2},{2,4},{4,6},{6,0},{1,3},{3,5},{5,7},{7,1},{8,10},{10,12},{12... | collective-permute-start | bytes 1769480 | tf_op jit(solution)/shard_map/ppermute | solution.py:44
  48.7 5.3 %collective-permute-start.3 = (bf16[576,512]{1,0:T(8,128)(2,1)}, bf16[576,512]{1,0:T(8,128)(2,1)}, u32[]{:S(2)}, u32[]{:S(2)}) collective-permute-start(bf16[576,512]{1,0:T(8,128)(2,1)} %get-tuple-element.34), channel_id=1, source_target_pairs={{0,4},{2,6},{4,0},{6,2},{1,5},{3,7},{5,1},{7,3},{8,12},{10,14},{12... | collective-permute-start | bytes 1769480 | tf_op jit(solution)/shard_map/ppermute | solution.py:44
  54.0 4.0 %collective-permute-start.4 = (bf16[576,512]{1,0:T(8,128)(2,1)S(1)}, bf16[576,512]{1,0:T(8,128)(2,1)}, u32[]{:S(2)}, u32[]{:S(2)}) collective-permute-start(bf16[576,512]{1,0:T(8,128)(2,1)S(1)} %get-tuple-element.35), channel_id=1, source_target_pairs={{0,6},{2,0},{4,2},{6,4},{1,7},{3,1},{5,3},{7,5},{8,14},{10,8},{12,... | collective-permute-start | bytes 1769480 | tf_op jit(solution)/shard_map/ppermute | solution.py:44
  57.9 0.9 broadcast_in_dim.24
  58.8 6.2 %all-to-all-start.1 = ((bf16[8,72,512]{2,1,0:T(8,128)(2,1)}), bf16[8,72,512]{2,1,0:T(8,128)(2,1)S(1)}, u32[]{:S(2)}, u32[]{:S(2)}) async-start(bf16[8,72,512]{2,1,0:T(8,128)(2,1)} %broadcast_in_dim.24), calls=%async_computation.1 | async-start | bytes 1179648 | tf_op jit(solution)/shard_map/all_to_all | solution.py:48
  65.1 12.8 %collective-permute-done.4.refs_3_ = bf16[576,512]{1,0:T(8,128)(2,1)} collective-permute-done((bf16[576,512]{1,0:T(8,128)(2,1)S(1)}, bf16[576,512]{1,0:T(8,128)(2,1)}, u32[]{:S(2)}, u32[]{:S(2)}) %collective-permute-start.4) | collective-permute-done | bytes 589856 | tf_op jit(solution)/shard_map/ppermute | solution.py:44
  77.8 1.1 copy-done.3
  78.9 3.1 %shard_map.68 = bf16[576,512]{1,0:T(8,128)(2,1)} custom-call(s32[2]{0:T(128)S(1)} %pad_add_fusion.place_ref, bf16[576,512]{1,0:T(8,128)(2,1)S(1)} %copy-done.3, bf16[576,512]{1,0:T(8,128)(2,1)} %collective-permute-done.2.refs_1_, bf16[576,512]{1,0:T(8,128)(2,1)} %collective-permute-done.3.refs_2_, bf16[576,512]{1,0:T(8,128)(2,1)} %collective-permute-done.4.refs_3_), custom_call_target="tpu_custom_call" | custom-call | flops 99999997952 | bytes 1179648 | tf_op jit(solution)/shard_map/pallas_call | solution.py:67
  82.0 11.2 %all-to-all-start.2 = ((bf16[8,72,512]{2,1,0:T(8,128)(2,1)}), bf16[8,72,512]{2,1,0:T(8,128)(2,1)}, u32[]{:S(2)}, u32[]{:S(2)}) async-start(bf16[8,72,512]{2,1,0:T(8,128)(2,1)} %bitcast.5), calls=%async_computation.2 | async-start | bytes 1179648 | tf_op jit(solution)/shard_map/all_to_all | solution.py:53
  93.2 1.9 %collective-permute-start.7 = (bf16[576,512]{1,0:T(8,128)(2,1)S(1)}, bf16[576,512]{1,0:T(8,128)(2,1)S(1)}, u32[]{:S(2)}, u32[]{:S(2)}) collective-permute-start(bf16[576,512]{1,0:T(8,128)(2,1)S(1)} %bitcast.6), channel_id=1, source_target_pairs={{0,6},{2,0},{4,2},{6,4},{1,7},{3,1},{5,3},{7,5},{8,14},{10,8},{12,... | collective-permute-start | bytes 1769480 | tf_op jit(solution)/shard_map/ppermute | solution.py:44
  95.1 2.4 %collective-permute-start.6 = (bf16[576,512]{1,0:T(8,128)(2,1)S(1)}, bf16[576,512]{1,0:T(8,128)(2,1)}, u32[]{:S(2)}, u32[]{:S(2)}) collective-permute-start(bf16[576,512]{1,0:T(8,128)(2,1)S(1)} %bitcast.7), channel_id=1, source_target_pairs={{0,4},{2,6},{4,0},{6,2},{1,5},{3,7},{5,1},{7,3},{8,12},{10,14},{12... | collective-permute-start | bytes 1769480 | tf_op jit(solution)/shard_map/ppermute | solution.py:44
  97.5 4.0 %collective-permute-start.5 = (bf16[576,512]{1,0:T(8,128)(2,1)S(1)}, bf16[576,512]{1,0:T(8,128)(2,1)}, u32[]{:S(2)}, u32[]{:S(2)}) collective-permute-start(bf16[576,512]{1,0:T(8,128)(2,1)S(1)} %bitcast.8), channel_id=1, source_target_pairs={{0,2},{2,4},{4,6},{6,0},{1,3},{3,5},{5,7},{7,1},{8,10},{10,12},{12... | collective-permute-start | bytes 1769480 | tf_op jit(solution)/shard_map/ppermute | solution.py:44
  101.5 11.2 %all-to-all-done.2 = bf16[8,72,512]{2,1,0:T(8,128)(2,1)} async-done(((bf16[8,72,512]{2,1,0:T(8,128)(2,1)}), bf16[8,72,512]{2,1,0:T(8,128)(2,1)}, u32[]{:S(2)}, u32[]{:S(2)}) %all-to-all-start.2) | async-done | bytes 589856 | tf_op jit(solution)/shard_map/all_to_all | solution.py:53
  112.6 1.1 reduce_sum.21
  113.8 13.8 %all_to_all.20 = bf16[12,6,512]{2,1,0:T(8,128)(2,1)S(1)} all-to-all(bf16[12,6,512]{2,1,0:T(8,128)(2,1)S(1)} %reshape.45), channel_id=1, replica_groups=mesh['z'=12,'y'=8,'x'=4,'c'=2] {'z'}, dimensions={0} | all-to-all | bytes 147456 | tf_op jit(solution)/shard_map/all_to_all | solution.py:53
  127.7 3.4 %shard_map.69 = (bf16[128,2816]{1,0:T(8,128)(2,1)S(1)}, f32[128,512]{1,0:T(8,128)S(1)}, bf16[128,2304]{1,0:T(8,128)(2,1)S(1)}) custom-call(s32[2]{0:T(128)S(1)} %pad_add_fusion.place_ref, bf16[128,4608]{1,0:T(8,128)(2,1)S(1)} %copy-done, bf16[128,512]{1,0:T(8,128)(2,1)S(1)} %copy-done.1, bf16[128,2816]{1,0:T(8,128)(2,1)S(1)} %collective-permute-done.theirs_ref, ...), custom_call_target="tpu_custom_call" | custom-call | flops 1207959552 | bytes 3145728 | tf_op jit(solution)/shard_map/pallas_call | solution.py:67
  131.0 3.1 %collective-permute-start.8 = (bf16[128,2816]{1,0:T(8,128)(2,1)S(1)}, bf16[128,2816]{1,0:T(8,128)(2,1)S(1)}, u32[]{:S(2)}, u32[]{:S(2)}) collective-permute-start(bf16[128,2816]{1,0:T(8,128)(2,1)S(1)} %get-tuple-element.45), channel_id=1, source_target_pairs={{0,1},{1,0},{2,3},{3,2},{4,5},{5,4},{6,7},{7,6},{8,9},{9,8},{10,11... | collective-permute-start | bytes 2162696 | tf_op jit(solution)/shard_map/ppermute | solution.py:40
  134.1 6.9 %collective-permute-start.9 = (f32[6,512]{1,0:T(8,128)S(1)}, f32[6,512]{1,0:T(8,128)S(1)}, u32[]{:S(2)}, u32[]{:S(2)}) collective-permute-start(f32[6,512]{1,0:T(8,128)S(1)} %broadcast_multiply_fusion), channel_id=1, source_target_pairs={{0,0},{64,1},{128,2},{192,3},{256,4},{320,5},{384,6},{448,7},{512,... | collective-permute-start | bytes 36872 | tf_op jit(solution)/shard_map/ppermute | solution.py:219
  141.1 9.3 %collective-permute-done.9 = f32[6,512]{1,0:T(8,128)S(1)} collective-permute-done((f32[6,512]{1,0:T(8,128)S(1)}, f32[6,512]{1,0:T(8,128)S(1)}, u32[]{:S(2)}, u32[]{:S(2)}) %collective-permute-start.9) | collective-permute-done | bytes 12320 | tf_op jit(solution)/shard_map/ppermute | solution.py:219
  150.3 1.7 %shard_map.70 = (bf16[128,512]{1,0:T(8,128)(2,1)}, bf16[128,4608]{1,0:T(8,128)(2,1)}) custom-call(s32[2]{0:T(128)S(1)} %pad_add_fusion.place_ref, f32[128,512]{1,0:T(8,128)S(1)} %get-tuple-element.43.part_ref, bf16[128,2304]{1,0:T(8,128)(2,1)S(1)} %get-tuple-element.44.columns_ref, bf16[128,2816]{1,0:T(8,128)(2,1)S(1)} %collective-permute-done.8.received_ref), custom_call_target="tpu_custom_call" | custom-call | flops 65536 | bytes 2621440 | tf_op jit(solution)/shard_map/pallas_call | solution.py:67
  (24 shorter events, 0.9 us)
Async XLA Ops:
  0.6 1.2 copy-start.1
  0.6 6.8 %copy-start.4 = (bf16[6,512]{1,0:T(8,128)(2,1)S(1)}, bf16[6,512]{1,0:T(8,128)(2,1)}, u32[]{:S(2)}) copy-start(bf16[6,512]{1,0:T(8,128)(2,1)} %param.5) | copy-start | bytes 18436
  1.8 41.5 %copy-start = (bf16[128,4608]{1,0:T(8,128)(2,1)S(1)}, bf16[128,4608]{1,0:T(8,128)(2,1)}, u32[]{:S(2)}) copy-start(bf16[128,4608]{1,0:T(8,128)(2,1)} %tokens_ref.3) | copy-start | bytes 3538948
  1.9 41.5 %collective-permute-start = (bf16[128,2816]{1,0:T(8,128)(2,1)S(1)}, bf16[128,2816]{1,0:T(8,128)(2,1)S(1)}, u32[]{:S(2)}, u32[]{:S(2)}) collective-permute-start(bf16[128,2816]{1,0:T(8,128)(2,1)S(1)} %pad_maximum_fusion), channel_id=1, source_target_pairs={{0,1},{1,0},{2,3},{3,2},{4,5},{5,4},{6,7},{7,6},{8,9},{9,8},{10,11... | collective-permute-start | bytes 2162696 | tf_op jit(solution)/shard_map/ppermute | solution.py:40
  7.5 20.2 %collective-permute-start.1 = (bf16[6,512]{1,0:T(8,128)(2,1)S(1)}, bf16[6,512]{1,0:T(8,128)(2,1)S(1)}, u32[]{:S(2)}, u32[]{:S(2)}) collective-permute-start(bf16[6,512]{1,0:T(8,128)(2,1)S(1)} %multiply_convert_fusion), channel_id=1, source_target_pairs={{0,0},{1,64},{2,128},{3,192},{4,256},{5,320},{6,384},{7,448},{8,51... | collective-permute-start | bytes 18440 | tf_op jit(solution)/shard_map/ppermute | solution.py:202
  28.4 14.9 %all-to-all-start = ((bf16[12,6,512]{2,1,0:T(8,128)(2,1)}), bf16[12,6,512]{2,1,0:T(8,128)(2,1)S(1)}, u32[]{:S(2)}, u32[]{:S(2)}) async-start(bf16[12,6,512]{2,1,0:T(8,128)(2,1)} %broadcast_in_dim.23), calls=%async_computation | async-start | bytes 196608 | tf_op jit(solution)/shard_map/all_to_all | solution.py:48
  45.9 0.8 copy-start.2
  46.8 18.3 %collective-permute-start.2 = (bf16[576,512]{1,0:T(8,128)(2,1)}, bf16[576,512]{1,0:T(8,128)(2,1)}, u32[]{:S(2)}, u32[]{:S(2)}) collective-permute-start(bf16[576,512]{1,0:T(8,128)(2,1)} %get-tuple-element.33), channel_id=1, source_target_pairs={{0,2},{2,4},{4,6},{6,0},{1,3},{3,5},{5,7},{7,1},{8,10},{10,12},{12... | collective-permute-start | bytes 1769480 | tf_op jit(solution)/shard_map/ppermute | solution.py:44
  48.7 16.4 %collective-permute-start.3 = (bf16[576,512]{1,0:T(8,128)(2,1)}, bf16[576,512]{1,0:T(8,128)(2,1)}, u32[]{:S(2)}, u32[]{:S(2)}) collective-permute-start(bf16[576,512]{1,0:T(8,128)(2,1)} %get-tuple-element.34), channel_id=1, source_target_pairs={{0,4},{2,6},{4,0},{6,2},{1,5},{3,7},{5,1},{7,3},{8,12},{10,14},{12... | collective-permute-start | bytes 1769480 | tf_op jit(solution)/shard_map/ppermute | solution.py:44
  54.0 23.9 %collective-permute-start.4 = (bf16[576,512]{1,0:T(8,128)(2,1)S(1)}, bf16[576,512]{1,0:T(8,128)(2,1)}, u32[]{:S(2)}, u32[]{:S(2)}) collective-permute-start(bf16[576,512]{1,0:T(8,128)(2,1)S(1)} %get-tuple-element.35), channel_id=1, source_target_pairs={{0,6},{2,0},{4,2},{6,4},{1,7},{3,1},{5,3},{7,5},{8,14},{10,8},{12,... | collective-permute-start | bytes 1769480 | tf_op jit(solution)/shard_map/ppermute | solution.py:44
  58.8 23.2 %all-to-all-start.1 = ((bf16[8,72,512]{2,1,0:T(8,128)(2,1)}), bf16[8,72,512]{2,1,0:T(8,128)(2,1)S(1)}, u32[]{:S(2)}, u32[]{:S(2)}) async-start(bf16[8,72,512]{2,1,0:T(8,128)(2,1)} %broadcast_in_dim.24), calls=%async_computation.1 | async-start | bytes 1179648 | tf_op jit(solution)/shard_map/all_to_all | solution.py:48
  77.8 1.1 copy-start.3
  82.0 30.7 %all-to-all-start.2 = ((bf16[8,72,512]{2,1,0:T(8,128)(2,1)}), bf16[8,72,512]{2,1,0:T(8,128)(2,1)}, u32[]{:S(2)}, u32[]{:S(2)}) async-start(bf16[8,72,512]{2,1,0:T(8,128)(2,1)} %bitcast.5), calls=%async_computation.2 | async-start | bytes 1179648 | tf_op jit(solution)/shard_map/all_to_all | solution.py:53
  93.2 34.5 %collective-permute-start.7 = (bf16[576,512]{1,0:T(8,128)(2,1)S(1)}, bf16[576,512]{1,0:T(8,128)(2,1)S(1)}, u32[]{:S(2)}, u32[]{:S(2)}) collective-permute-start(bf16[576,512]{1,0:T(8,128)(2,1)S(1)} %bitcast.6), channel_id=1, source_target_pairs={{0,6},{2,0},{4,2},{6,4},{1,7},{3,1},{5,3},{7,5},{8,14},{10,8},{12,... | collective-permute-start | bytes 1769480 | tf_op jit(solution)/shard_map/ppermute | solution.py:44
  95.1 32.6 %collective-permute-start.6 = (bf16[576,512]{1,0:T(8,128)(2,1)S(1)}, bf16[576,512]{1,0:T(8,128)(2,1)}, u32[]{:S(2)}, u32[]{:S(2)}) collective-permute-start(bf16[576,512]{1,0:T(8,128)(2,1)S(1)} %bitcast.7), channel_id=1, source_target_pairs={{0,4},{2,6},{4,0},{6,2},{1,5},{3,7},{5,1},{7,3},{8,12},{10,14},{12... | collective-permute-start | bytes 1769480 | tf_op jit(solution)/shard_map/ppermute | solution.py:44
  97.5 30.2 %collective-permute-start.5 = (bf16[576,512]{1,0:T(8,128)(2,1)S(1)}, bf16[576,512]{1,0:T(8,128)(2,1)}, u32[]{:S(2)}, u32[]{:S(2)}) collective-permute-start(bf16[576,512]{1,0:T(8,128)(2,1)S(1)} %bitcast.8), channel_id=1, source_target_pairs={{0,2},{2,4},{4,6},{6,0},{1,3},{3,5},{5,7},{7,1},{8,10},{10,12},{12... | collective-permute-start | bytes 1769480 | tf_op jit(solution)/shard_map/ppermute | solution.py:44
  131.0 19.3 %collective-permute-start.8 = (bf16[128,2816]{1,0:T(8,128)(2,1)S(1)}, bf16[128,2816]{1,0:T(8,128)(2,1)S(1)}, u32[]{:S(2)}, u32[]{:S(2)}) collective-permute-start(bf16[128,2816]{1,0:T(8,128)(2,1)S(1)} %get-tuple-element.45), channel_id=1, source_target_pairs={{0,1},{1,0},{2,3},{3,2},{4,5},{5,4},{6,7},{7,6},{8,9},{9,8},{10,11... | collective-permute-start | bytes 2162696 | tf_op jit(solution)/shard_map/ppermute | solution.py:40
  134.1 16.2 %collective-permute-start.9 = (f32[6,512]{1,0:T(8,128)S(1)}, f32[6,512]{1,0:T(8,128)S(1)}, u32[]{:S(2)}, u32[]{:S(2)}) collective-permute-start(f32[6,512]{1,0:T(8,128)S(1)} %broadcast_multiply_fusion), channel_id=1, source_target_pairs={{0,0},{64,1},{128,2},{192,3},{256,4},{320,5},{384,6},{448,7},{512,... | collective-permute-start | bytes 36872 | tf_op jit(solution)/shard_map/ppermute | solution.py:219

commit v9 on v8

v9 whole, which is shorter than its diff:
```python
import math

import ml_dtypes
import numpy as np
import jax
import jax.numpy as jnp
from jax import lax
from jax.experimental import pallas as pl
from jax.experimental.pallas import tpu as pltpu
from jax.sharding import Mesh, PartitionSpec as P

BLOCK_ROWS = 4
NZ, NY, NX, NC = 12, 8, 4, 2
AXES = ("z", "y", "x", "c")
BF16 = jnp.bfloat16
F32 = jnp.float32
LONG = 10**11
PARAMS = pltpu.CompilerParams(vmem_limit_bytes=24 * 2**20)


PLANES = 2


def column_order(rows):
    size = PLANES * NY * NX * NC * rows
    places = np.arange(size).reshape(PLANES, NY, NX, NC, rows).transpose(3, 2, 0, 1, 4)
    order = np.zeros((size, size), ml_dtypes.bfloat16)
    order[places.reshape(-1), np.arange(size)] = 1
    return order


def scaled_rows(w_values, w_scales):
    rows = w_values.shape[0]
    first = lax.axis_index(AXES) * rows
    start = first // BLOCK_ROWS
    pair = lax.dynamic_slice(w_scales, (start,), (2,))
    block = (first + lax.iota(jnp.int32, rows)) // BLOCK_ROWS - start
    scale = jnp.where(block == 0, pair[0], pair[1])
    return (w_values.astype(F32) * scale[:, None]).astype(BF16)


def swap(array):
    return lax.ppermute(array, "c", [(0, 1), (1, 0)])


def along_x(array, step):
    return lax.ppermute(array, "x", [(i, (i + step) % NX) for i in range(NX)])


def gather(rows, axis, size):
    out = lax.all_to_all(jnp.broadcast_to(rows[None], (size, *rows.shape)), axis, 0, 0)
    return out.reshape(-1, rows.shape[1])


def reduce(rows, axis, size):
    out = lax.all_to_all(rows.reshape(size, -1, rows.shape[1]), axis, 0, 0)
    return jnp.sum(out.astype(F32), axis=0)


def dot(a, b, over):
    return lax.dot_general(a, b, ((over[:1], over[1:]), ((), ())), preferred_element_type=F32)


def whole(shape):
    return pl.BlockSpec(shape, lambda i, place: (0,) * len(shape))


def call(kernel, outs, in_specs, scratch, flops, args):
    moved = sum(math.prod(s.shape) * s.dtype.itemsize for s in outs)
    return pl.pallas_call(
        kernel,
        out_shape=outs,
        grid_spec=pltpu.PrefetchScalarGridSpec(
            num_scalar_prefetch=1,
            grid=(1,),
            in_specs=in_specs,
            out_specs=[whole(s.shape) for s in outs],
            scratch_shapes=scratch,
        ),
        compiler_params=PARAMS,
        cost_estimate=pl.CostEstimate(flops=flops, bytes_accessed=2 * moved, transcendentals=0),
    )(*args)


def sort_columns(place, tokens, grad, order):
    count, cols = grad.shape
    half = tokens.shape[1] // NC
    window = order.shape[0]
    part = window // NC

    def kernel(place_ref, tokens_ref, grad_ref, order_ref, mine_ref, send_ref):
        first = place_ref[0] == 0
        for k in range(tokens.shape[1] // window):
            both = dot(tokens_ref[:, k * window : (k + 1) * window], order_ref[...], (1, 0))
            low, high = both[:, :part], both[:, part:]
            at = slice(k * part, (k + 1) * part)
            mine_ref[:, at] = jnp.where(first, low, high).astype(BF16)
            send_ref[:, at] = jnp.where(first, high, low).astype(BF16)
        send_ref[:, half:] = grad_ref[...]

    return call(
        kernel,
        [
            jax.ShapeDtypeStruct((count, half), BF16),
            jax.ShapeDtypeStruct((count, half + cols), BF16),
        ],
        [whole(tokens.shape), whole(grad.shape), whole(order.shape)],
        [],
        2 * tokens.size * window,
        (place, tokens, grad, order),
    )


def x_rows(window, block, part):
    return pl.multiple_of(window * part * NX + block * part, part)


def partials(place, mine, grad, theirs, part):
    count, half = mine.shape
    cols = grad.shape[1]
    rows = half // NX
    chunk = 256

    def kernel(place_ref, mine_ref, grad_ref, theirs_ref, *rest):
        outs, total = rest[:NX], rest[NX]
        grads = jnp.concatenate([grad_ref[...], theirs_ref[:, half:]], axis=0)
        for k in range(0, half, chunk):
            both = jnp.concatenate(
                [mine_ref[:, k : k + chunk], theirs_ref[:, k : k + chunk]], axis=0
            )
            total[k : k + chunk] = dot(both, grads, (0, 0)).astype(BF16)
        x = place_ref[1]
        for step in range(NX):
            block = lax.rem(x + step, NX)
            for k in range(rows // part):
                outs[step][k * part : (k + 1) * part] = total[
                    pl.ds(x_rows(k, block, part), part), :
                ]

    return call(
        kernel,
        [jax.ShapeDtypeStruct((rows, cols), BF16)] * NX,
        [whole(mine.shape), whole(grad.shape), whole(theirs.shape)],
        [pltpu.VMEM((half, cols), BF16)],
        4 * count * half * cols,
        (place, mine, grad, theirs),
    )


def forward(place, mine, grad, theirs, blocks, part_rows):
    rows, cols = blocks[0].shape
    half = rows * NX
    count = mine.shape[0]

    def kernel(place_ref, mine_ref, grad_ref, theirs_ref, *rest):
        block_refs, (for_them, part_ref, columns_ref, weights) = rest[:NX], rest[NX:]
        x = place_ref[1]
        for step in range(NX):
            block = lax.rem(x + NX - step, NX)
            for k in range(rows // part_rows):
                weights[pl.ds(x_rows(k, block, part_rows), part_rows), :] = block_refs[step][
                    k * part_rows : (k + 1) * part_rows
                ]
        tokens_both = jnp.concatenate([theirs_ref[:, :half], mine_ref[...]], axis=0)
        part = dot(tokens_both, weights[...], (1, 0))
        for_them[:, half:] = part[:count].astype(BF16)
        part_ref[...] = part[count:]
        grads = jnp.concatenate([theirs_ref[:, half:], grad_ref[...]], axis=0)
        columns = dot(grads, weights[...], (1, 1)).astype(BF16)
        for_them[:, :half] = columns[:count]
        columns_ref[...] = columns[count:]

    return call(
        kernel,
        [
            jax.ShapeDtypeStruct((count, half + cols), BF16),
            jax.ShapeDtypeStruct((count, cols), F32),
            jax.ShapeDtypeStruct((count, half), BF16),
        ],
        [
            whole(mine.shape),
            whole(grad.shape),
            whole(theirs.shape),
            *[whole(b.shape) for b in blocks],
        ],
        [pltpu.VMEM((half, cols), BF16)],
        8 * count * half * cols,
        (place, mine, grad, theirs, *blocks),
    )


def add_up(place, parts):
    def kernel(place_ref, *refs):
        *part_refs, out_ref = refs
        out_ref[...] = sum(p[...].astype(F32) for p in part_refs).astype(BF16)

    out = jax.ShapeDtypeStruct(parts[0].shape, BF16)
    return call(kernel, [out], [whole(p.shape) for p in parts], [], LONG, (place, *parts))[0]


def assemble(place, part, columns, received, order):
    count, half = columns.shape
    cols = part.shape[1]
    window = order.shape[0]
    width = window // NC

    def kernel(place_ref, part_ref, columns_ref, received_ref, order_ref, projected_ref, out_ref):
        projected_ref[...] = (part_ref[...] + received_ref[:, half:].astype(F32)).astype(BF16)

        def put(low_ref, high_ref):
            for k in range(half // width):
                at = slice(k * width, (k + 1) * width)
                both = jnp.concatenate([low_ref[:, at], high_ref[:, at]], axis=1)
                out_ref[:, k * window : (k + 1) * window] = dot(
                    both, order_ref[...], (1, 1)
                ).astype(BF16)

        @pl.when(place_ref[0] == 0)
        def _():
            put(columns_ref, received_ref)

        @pl.when(place_ref[0] == 1)
        def _():
            put(received_ref, columns_ref)

    return call(
        kernel,
        [
            jax.ShapeDtypeStruct((count, cols), BF16),
            jax.ShapeDtypeStruct((count, NC * half), BF16),
        ],
        [whole(part.shape), whole(columns.shape), whole(received.shape), whole(order.shape)],
        [],
        2 * NC * count * half * window,
        (place, part, columns, received, order),
    )


def body(tokens, w_values, w_scales, out_grad):
    core, x = lax.axis_index("c"), lax.axis_index("x")
    place = jnp.stack([core, x]).astype(jnp.int32)
    order = jnp.asarray(column_order(w_values.shape[0]))
    part_rows = order.shape[0] // (NC * NX)
    mine, send = sort_columns(place, tokens, out_grad, order)
    theirs = swap(send)
    rows = gather(scaled_rows(w_values, w_scales), "y", NY)
    theirs, rows = lax.optimization_barrier((theirs, rows))

    parts = partials(place, mine, out_grad, theirs, part_rows)
    rows, *parts = lax.optimization_barrier((rows, *parts))
    parts = [parts[0], *(along_x(parts[step], step) for step in range(1, NX))]
    rows = gather(rows, "z", NZ)
    total = add_up(place, parts)
    total, rows = lax.optimization_barrier((total, rows))
    blocks = [rows, *(along_x(rows, step) for step in range(1, NX))]

    total = reduce(total, "z", NZ).astype(BF16)
    total = reduce(total, "y", NY)
    total, *blocks = lax.optimization_barrier((total, *blocks))
    count = tokens.shape[0] * NZ * NY * NX * NC
    weight_grad = total * (1.0 / math.sqrt(count))
    for_them, part, columns = forward(place, mine, out_grad, theirs, blocks, part_rows)
    projected, token_grad = assemble(place, part, columns, swap(for_them), order)
    return projected, token_grad, weight_grad


def solution(mesh):
    split = Mesh(mesh.devices.reshape(NZ, NY, NX, NC), AXES)
    by_rows = P(AXES, None)
    return jax.shard_map(
        body,
        mesh=split,
        in_specs=(by_rows, by_rows, P(), by_rows),
        out_specs=(by_rows, by_rows, by_rows),
        check_vma=False,
    )
```

time: 153 us -> 135 us (0.88)
  the two profiles are of different devices: /device:TPU:67 before, /device:TPU:1 now
where the time goes in v9:
time: 135 us; the launch traced here: 134 us
  starting transfers between devices  53.5 us (40%)
  waiting for transfers between devices  35.6 us (26%)
  blocking collectives  19.3 us (14%)
  Pallas kernels  13 us (10%)
  local copies, waits for them, and re-layouts  8.78 us (7%)
  other arithmetic  3.23 us (2%)
    ppermute x2, starting transfers between devices, swap(): return lax.ppermute(array, 'c', [(0, 1), (1, 0)])  18.5 us
    ppermute x6, starting transfers between devices, along_x(): return lax.ppermute(array, 'x', [(i, (i + step) % NX) for i in range(NX)])  16.2 us
    all_to_all x1, waiting for transfers between devices, reduce(): out = lax.all_to_all(rows.reshape(size, -1, rows.shape[1]), axis, 0, 0)  15.6 us
    pallas_call x5, Pallas kernels, call(): pl.pallas_call(kernel, out_shape=outs, grid_spec=pltpu.PrefetchScalarGrid...  13 us
    all_to_all x1, starting transfers between devices, gather(): lax.all_to_all(jnp.broadcast_to(rows[None], (size, *rows.shape)), axis, 0...  12 us
    ppermute x6, waiting for transfers between devices, along_x(): return lax.ppermute(array, 'x', [(i, (i + step) % NX) for i in range(NX)])  11.1 us
    all_to_all x1, blocking collectives, gather(): lax.all_to_all(jnp.broadcast_to(rows[None], (size, *rows.shape)), axis, 0...  9.73 us
    all_to_all x1, blocking collectives, reduce(): out = lax.all_to_all(rows.reshape(size, -1, rows.shape[1]), axis, 0, 0)  9.6 us
  transfers between devices with their start and end apart: 10, of which 5 were waited for; matrix products, arithmetic and copies ran while one was open for 4% of the time, Pallas kernels for 2%

profile of v9, /device:TPU:1, one launch (start us, length us, event | category | flops | bytes accessed | tf_op | source)
XLA Modules:
  0.0 134.3 jit_solution(1231268604362544615)
XLA Ops:
  0.7 1.3 copy-done
  2.0 0.9 copy-done.1
  2.9 1.3 copy-done.3
  4.2 1.6 %shard_map.76 = (bf16[128,2304]{1,0:T(8,128)(2,1)S(1)}, bf16[128,2816]{1,0:T(8,128)(2,1)S(1)}) custom-call(s32[2]{0:T(128)S(1)} %pad_add_fusion.place_ref, bf16[128,4608]{1,0:T(8,128)(2,1)S(1)} %copy-done, bf16[128,512]{1,0:T(8,128)(2,1)S(1)} %copy-done.1, bf16[768,768]{1,0:T(8,128)(2,1)S(1)} %copy-done.3), custom_call_target="tpu_custom_call" | custom-call | flops 905969664 | bytes 2621440 | tf_op jit(solution)/shard_map/pallas_call | solution.py:70
  5.8 12.4 %collective-permute-start = (bf16[128,2816]{1,0:T(8,128)(2,1)S(1)}, bf16[128,2816]{1,0:T(8,128)(2,1)S(1)}, u32[]{:S(2)}, u32[]{:S(2)}) collective-permute-start(bf16[128,2816]{1,0:T(8,128)(2,1)S(1)} %get-tuple-element.29), channel_id=1, source_target_pairs={{0,1},{1,0},{2,3},{3,2},{4,5},{5,4},{6,7},{7,6},{8,9},{9,8},{10,11... | collective-permute-start | bytes 2162696 | tf_op jit(solution)/shard_map/ppermute | solution.py:43
  18.3 0.8 dynamic_slice.3
  19.7 1.3 compare_select_fusion
  21.1 9.7 %all_to_all.20 = bf16[8,6,512]{2,1,0:T(8,128)(2,1)S(1)} all-to-all(bf16[8,6,512]{2,1,0:T(8,128)(2,1)S(1)} %broadcast_in_dim.23), channel_id=1, replica_groups=mesh['z'=12,'y'=8,'x'=4,'c'=2] {'y'}, dimensions={0} | all-to-all | bytes 98304 | tf_op jit(solution)/shard_map/all_to_all | solution.py:51
  30.8 2.3 %shard_map.77 = (bf16[576,512]{1,0:T(8,128)(2,1)S(1)}, bf16[576,512]{1,0:T(8,128)(2,1)}, bf16[576,512]{1,0:T(8,128)(2,1)S(1)}, bf16[576,512]{1,0:T(8,128)(2,1)S(1)}) custom-call(s32[2]{0:T(128)S(1)} %pad_add_fusion.place_ref, bf16[128,2304]{1,0:T(8,128)(2,1)S(1)} %get-tuple-element.28.mine_ref, bf16[128,512]{1,0:T(8,128)(2,1)S(1)} %copy-done.2, ...), custom_call_target="tpu_custom_call" | custom-call | flops 603979776 | bytes 4718592 | tf_op jit(solution)/shard_map/pallas_call | solution.py:70
  33.2 0.8 copy-done.7
  34.0 1.9 %collective-permute-start.1 = (bf16[576,512]{1,0:T(8,128)(2,1)}, bf16[576,512]{1,0:T(8,128)(2,1)S(1)}, u32[]{:S(2)}, u32[]{:S(2)}) collective-permute-start(bf16[576,512]{1,0:T(8,128)(2,1)} %get-tuple-element.37), channel_id=1, source_target_pairs={{0,2},{2,4},{4,6},{6,0},{1,3},{3,5},{5,7},{7,1},{8,10},{10,12},{12... | collective-permute-start | bytes 1769480 | tf_op jit(solution)/shard_map/ppermute | solution.py:47
  35.9 1.9 %collective-permute-start.2 = (bf16[576,512]{1,0:T(8,128)(2,1)S(1)}, bf16[576,512]{1,0:T(8,128)(2,1)}, u32[]{:S(2)}, u32[]{:S(2)}) collective-permute-start(bf16[576,512]{1,0:T(8,128)(2,1)S(1)} %get-tuple-element.38), channel_id=1, source_target_pairs={{0,4},{2,6},{4,0},{6,2},{1,5},{3,7},{5,1},{7,3},{8,12},{10,14},{12... | collective-permute-start | bytes 1769480 | tf_op jit(solution)/shard_map/ppermute | solution.py:47
  37.8 4.6 %collective-permute-start.3 = (bf16[576,512]{1,0:T(8,128)(2,1)S(1)}, bf16[576,512]{1,0:T(8,128)(2,1)}, u32[]{:S(2)}, u32[]{:S(2)}) collective-permute-start(bf16[576,512]{1,0:T(8,128)(2,1)S(1)} %get-tuple-element.39), channel_id=1, source_target_pairs={{0,6},{2,0},{4,2},{6,4},{1,7},{3,1},{5,3},{7,5},{8,14},{10,8},{12,... | collective-permute-start | bytes 1769480 | tf_op jit(solution)/shard_map/ppermute | solution.py:47
  42.4 0.9 broadcast_in_dim.24
  43.3 12.0 %all-to-all-start.1 = ((bf16[12,48,512]{2,1,0:T(8,128)(2,1)}), bf16[12,48,512]{2,1,0:T(8,128)(2,1)S(1)}, u32[]{:S(2)}, u32[]{:S(2)}) async-start(bf16[12,48,512]{2,1,0:T(8,128)(2,1)} %broadcast_in_dim.24), calls=%async_computation.1 | async-start | bytes 1179648 | tf_op jit(solution)/shard_map/all_to_all | solution.py:51
  55.3 8.2 %collective-permute-done.1.refs_1_ = bf16[576,512]{1,0:T(8,128)(2,1)S(1)} collective-permute-done((bf16[576,512]{1,0:T(8,128)(2,1)}, bf16[576,512]{1,0:T(8,128)(2,1)S(1)}, u32[]{:S(2)}, u32[]{:S(2)}) %collective-permute-start.1) | collective-permute-done | bytes 589856 | tf_op jit(solution)/shard_map/ppermute | solution.py:47
  63.5 2.9 %collective-permute-done.3.refs_3_ = bf16[576,512]{1,0:T(8,128)(2,1)} collective-permute-done((bf16[576,512]{1,0:T(8,128)(2,1)S(1)}, bf16[576,512]{1,0:T(8,128)(2,1)}, u32[]{:S(2)}, u32[]{:S(2)}) %collective-permute-start.3) | collective-permute-done | bytes 589856 | tf_op jit(solution)/shard_map/ppermute | solution.py:47
  66.5 1.1 copy-done.8
  67.5 2.9 %shard_map.78 = bf16[576,512]{1,0:T(8,128)(2,1)} custom-call(s32[2]{0:T(128)S(1)} %pad_add_fusion.place_ref, bf16[576,512]{1,0:T(8,128)(2,1)S(1)} %copy-done.8, bf16[576,512]{1,0:T(8,128)(2,1)S(1)} %collective-permute-done.1.refs_1_, bf16[576,512]{1,0:T(8,128)(2,1)} %collective-permute-done.2.refs_2_, bf16[576,512]{1,0:T(8,128)(2,1)} %collective-permute-done.3.refs_3_), custom_call_target="tpu_custom_call" | custom-call | flops 99999997952 | bytes 1179648 | tf_op jit(solution)/shard_map/pallas_call | solution.py:70
  70.4 7.7 %all-to-all-done.1 = bf16[12,48,512]{2,1,0:T(8,128)(2,1)S(1)} async-done(((bf16[12,48,512]{2,1,0:T(8,128)(2,1)}), bf16[12,48,512]{2,1,0:T(8,128)(2,1)S(1)}, u32[]{:S(2)}, u32[]{:S(2)}) %all-to-all-start.1) | async-done | bytes 589856 | tf_op jit(solution)/shard_map/all_to_all | solution.py:51
  78.1 6.7 %all-to-all-start.2 = ((bf16[12,48,512]{2,1,0:T(8,128)(2,1)}), bf16[12,48,512]{2,1,0:T(8,128)(2,1)}, u32[]{:S(2)}, u32[]{:S(2)}) async-start(bf16[12,48,512]{2,1,0:T(8,128)(2,1)} %bitcast.5), calls=%async_computation.2 | async-start | bytes 1179648 | tf_op jit(solution)/shard_map/all_to_all | solution.py:56
  84.8 1.9 %collective-permute-start.6 = (bf16[576,512]{1,0:T(8,128)(2,1)S(1)}, bf16[576,512]{1,0:T(8,128)(2,1)S(1)}, u32[]{:S(2)}, u32[]{:S(2)}) collective-permute-start(bf16[576,512]{1,0:T(8,128)(2,1)S(1)} %bitcast.6), channel_id=1, source_target_pairs={{0,6},{2,0},{4,2},{6,4},{1,7},{3,1},{5,3},{7,5},{8,14},{10,8},{12,... | collective-permute-start | bytes 1769480 | tf_op jit(solution)/shard_map/ppermute | solution.py:47
  86.8 4.0 %collective-permute-start.5 = (bf16[576,512]{1,0:T(8,128)(2,1)S(1)}, bf16[576,512]{1,0:T(8,128)(2,1)S(1)}, u32[]{:S(2)}, u32[]{:S(2)}) collective-permute-start(bf16[576,512]{1,0:T(8,128)(2,1)S(1)} %bitcast.7), channel_id=1, source_target_pairs={{0,4},{2,6},{4,0},{6,2},{1,5},{3,7},{5,1},{7,3},{8,12},{10,14},{12... | collective-permute-start | bytes 1769480 | tf_op jit(solution)/shard_map/ppermute | solution.py:47
  90.8 1.9 %collective-permute-start.4 = (bf16[576,512]{1,0:T(8,128)(2,1)S(1)}, bf16[576,512]{1,0:T(8,128)(2,1)S(1)}, u32[]{:S(2)}, u32[]{:S(2)}) collective-permute-start(bf16[576,512]{1,0:T(8,128)(2,1)S(1)} %bitcast.8), channel_id=1, source_target_pairs={{0,2},{2,4},{4,6},{6,0},{1,3},{3,5},{5,7},{7,1},{8,10},{10,12},{12... | collective-permute-start | bytes 1769480 | tf_op jit(solution)/shard_map/ppermute | solution.py:47
  92.7 15.6 %all-to-all-done.2 = bf16[12,48,512]{2,1,0:T(8,128)(2,1)} async-done(((bf16[12,48,512]{2,1,0:T(8,128)(2,1)}), bf16[12,48,512]{2,1,0:T(8,128)(2,1)}, u32[]{:S(2)}, u32[]{:S(2)}) %all-to-all-start.2) | async-done | bytes 589856 | tf_op jit(solution)/shard_map/all_to_all | solution.py:56
  108.3 1.2 reduce_sum.21
  109.5 9.6 %all_to_all.21 = bf16[8,6,512]{2,1,0:T(8,128)(2,1)S(1)} all-to-all(bf16[8,6,512]{2,1,0:T(8,128)(2,1)S(1)} %reshape.45), channel_id=1, replica_groups=mesh['z'=12,'y'=8,'x'=4,'c'=2] {'y'}, dimensions={0} | all-to-all | bytes 98304 | tf_op jit(solution)/shard_map/all_to_all | solution.py:56
  119.2 1.1 copy-done.6
  120.3 2.1 %shard_map.79 = (bf16[128,2816]{1,0:T(8,128)(2,1)S(1)}, f32[128,512]{1,0:T(8,128)S(1)}, bf16[128,2304]{1,0:T(8,128)(2,1)S(1)}) custom-call(s32[2]{0:T(128)S(1)} %pad_add_fusion.place_ref, bf16[128,2304]{1,0:T(8,128)(2,1)S(1)} %copy-done.6, bf16[128,512]{1,0:T(8,128)(2,1)S(1)} %copy-done.2, bf16[128,2816]{1,0:T(8,128)(2,1)S(1)} %collective-permute-done.theirs_ref, ...), custom_call_target="tpu_custom_call" | custom-call | flops 1207959552 | bytes 3145728 | tf_op jit(solution)/shard_map/pallas_call | solution.py:70
  122.4 6.1 %collective-permute-start.7 = (bf16[128,2816]{1,0:T(8,128)(2,1)S(1)}, bf16[128,2816]{1,0:T(8,128)(2,1)S(1)}, u32[]{:S(2)}, u32[]{:S(2)}) collective-permute-start(bf16[128,2816]{1,0:T(8,128)(2,1)S(1)} %get-tuple-element.49), channel_id=1, source_target_pairs={{0,1},{1,0},{2,3},{3,2},{4,5},{5,4},{6,7},{7,6},{8,9},{9,8},{10,11... | collective-permute-start | bytes 2162696 | tf_op jit(solution)/shard_map/ppermute | solution.py:43
  129.1 1.2 collective-permute-done.7.received_ref
  130.3 4.0 %shard_map.80 = (bf16[128,512]{1,0:T(8,128)(2,1)}, bf16[128,4608]{1,0:T(8,128)(2,1)}) custom-call(s32[2]{0:T(128)S(1)} %pad_add_fusion.place_ref, f32[128,512]{1,0:T(8,128)S(1)} %get-tuple-element.47.part_ref, bf16[128,2304]{1,0:T(8,128)(2,1)S(1)} %get-tuple-element.48.columns_ref, bf16[128,2816]{1,0:T(8,128)(2,1)S(1)} %collective-permute-done.7.received_ref, ...), custom_call_target="tpu_custom_call" | custom-call | flops 905969664 | bytes 2621440 | tf_op jit(solution)/shard_map/pallas_call | solution.py:70
  (27 shorter events, 1.5 us)
Async XLA Ops:
  0.7 1.3 copy-start
  2.0 0.9 copy-start.1
  2.9 1.3 copy-start.3
  4.2 16.8 %copy-start.9 = (bf16[6,512]{1,0:T(8,128)(2,1)S(1)}, bf16[6,512]{1,0:T(8,128)(2,1)}, u32[]{:S(2)}) copy-start(bf16[6,512]{1,0:T(8,128)(2,1)} %param.6) | copy-start | bytes 18436
  4.2 26.7 %copy-start.2 = (bf16[128,512]{1,0:T(8,128)(2,1)S(1)}, bf16[128,512]{1,0:T(8,128)(2,1)}, u32[]{:S(2)}) copy-start(bf16[128,512]{1,0:T(8,128)(2,1)} %grad_ref.5) | copy-start | bytes 393220
  5.8 27.4 %copy-start.5 = (bf16[128,2304]{1,0:T(8,128)(2,1)}, bf16[128,2304]{1,0:T(8,128)(2,1)S(1)}, u32[]{:S(2)}) copy-start(bf16[128,2304]{1,0:T(8,128)(2,1)S(1)} %get-tuple-element.28.mine_ref) | copy-start | bytes 1769476
  5.8 25.0 %collective-permute-start = (bf16[128,2816]{1,0:T(8,128)(2,1)S(1)}, bf16[128,2816]{1,0:T(8,128)(2,1)S(1)}, u32[]{:S(2)}, u32[]{:S(2)}) collective-permute-start(bf16[128,2816]{1,0:T(8,128)(2,1)S(1)} %get-tuple-element.29), channel_id=1, source_target_pairs={{0,1},{1,0},{2,3},{3,2},{4,5},{5,4},{6,7},{7,6},{8,9},{9,8},{10,11... | collective-permute-start | bytes 2162696 | tf_op jit(solution)/shard_map/ppermute | solution.py:43
  33.2 0.8 copy-start.7
  34.0 29.5 %collective-permute-start.1 = (bf16[576,512]{1,0:T(8,128)(2,1)}, bf16[576,512]{1,0:T(8,128)(2,1)S(1)}, u32[]{:S(2)}, u32[]{:S(2)}) collective-permute-start(bf16[576,512]{1,0:T(8,128)(2,1)} %get-tuple-element.37), channel_id=1, source_target_pairs={{0,2},{2,4},{4,6},{6,0},{1,3},{3,5},{5,7},{7,1},{8,10},{10,12},{12... | collective-permute-start | bytes 1769480 | tf_op jit(solution)/shard_map/ppermute | solution.py:47
  35.9 27.6 %collective-permute-start.2 = (bf16[576,512]{1,0:T(8,128)(2,1)S(1)}, bf16[576,512]{1,0:T(8,128)(2,1)}, u32[]{:S(2)}, u32[]{:S(2)}) collective-permute-start(bf16[576,512]{1,0:T(8,128)(2,1)S(1)} %get-tuple-element.38), channel_id=1, source_target_pairs={{0,4},{2,6},{4,0},{6,2},{1,5},{3,7},{5,1},{7,3},{8,12},{10,14},{12... | collective-permute-start | bytes 1769480 | tf_op jit(solution)/shard_map/ppermute | solution.py:47
  37.8 28.6 %collective-permute-start.3 = (bf16[576,512]{1,0:T(8,128)(2,1)S(1)}, bf16[576,512]{1,0:T(8,128)(2,1)}, u32[]{:S(2)}, u32[]{:S(2)}) collective-permute-start(bf16[576,512]{1,0:T(8,128)(2,1)S(1)} %get-tuple-element.39), channel_id=1, source_target_pairs={{0,6},{2,0},{4,2},{6,4},{1,7},{3,1},{5,3},{7,5},{8,14},{10,8},{12,... | collective-permute-start | bytes 1769480 | tf_op jit(solution)/shard_map/ppermute | solution.py:47
  43.3 34.8 %all-to-all-start.1 = ((bf16[12,48,512]{2,1,0:T(8,128)(2,1)}), bf16[12,48,512]{2,1,0:T(8,128)(2,1)S(1)}, u32[]{:S(2)}, u32[]{:S(2)}) async-start(bf16[12,48,512]{2,1,0:T(8,128)(2,1)} %broadcast_in_dim.24), calls=%async_computation.1 | async-start | bytes 1179648 | tf_op jit(solution)/shard_map/all_to_all | solution.py:51
  66.5 1.1 copy-start.8
  78.1 30.2 %all-to-all-start.2 = ((bf16[12,48,512]{2,1,0:T(8,128)(2,1)}), bf16[12,48,512]{2,1,0:T(8,128)(2,1)}, u32[]{:S(2)}, u32[]{:S(2)}) async-start(bf16[12,48,512]{2,1,0:T(8,128)(2,1)} %bitcast.5), calls=%async_computation.2 | async-start | bytes 1179648 | tf_op jit(solution)/shard_map/all_to_all | solution.py:56
  84.8 34.3 %collective-permute-start.6 = (bf16[576,512]{1,0:T(8,128)(2,1)S(1)}, bf16[576,512]{1,0:T(8,128)(2,1)S(1)}, u32[]{:S(2)}, u32[]{:S(2)}) collective-permute-start(bf16[576,512]{1,0:T(8,128)(2,1)S(1)} %bitcast.6), channel_id=1, source_target_pairs={{0,6},{2,0},{4,2},{6,4},{1,7},{3,1},{5,3},{7,5},{8,14},{10,8},{12,... | collective-permute-start | bytes 1769480 | tf_op jit(solution)/shard_map/ppermute | solution.py:47
  86.8 32.4 %collective-permute-start.5 = (bf16[576,512]{1,0:T(8,128)(2,1)S(1)}, bf16[576,512]{1,0:T(8,128)(2,1)S(1)}, u32[]{:S(2)}, u32[]{:S(2)}) collective-permute-start(bf16[576,512]{1,0:T(8,128)(2,1)S(1)} %bitcast.7), channel_id=1, source_target_pairs={{0,4},{2,6},{4,0},{6,2},{1,5},{3,7},{5,1},{7,3},{8,12},{10,14},{12... | collective-permute-start | bytes 1769480 | tf_op jit(solution)/shard_map/ppermute | solution.py:47
  90.8 28.4 %collective-permute-start.4 = (bf16[576,512]{1,0:T(8,128)(2,1)S(1)}, bf16[576,512]{1,0:T(8,128)(2,1)S(1)}, u32[]{:S(2)}, u32[]{:S(2)}) collective-permute-start(bf16[576,512]{1,0:T(8,128)(2,1)S(1)} %bitcast.8), channel_id=1, source_target_pairs={{0,2},{2,4},{4,6},{6,0},{1,3},{3,5},{5,7},{7,1},{8,10},{10,12},{12... | collective-permute-start | bytes 1769480 | tf_op jit(solution)/shard_map/ppermute | solution.py:47
  119.1 11.2 %copy-start.4 = (bf16[768,768]{1,0:T(8,128)(2,1)S(1)}, bf16[768,768]{1,0:T(8,128)(2,1)}, u32[]{:S(2)}) copy-start(bf16[768,768]{1,0:T(8,128)(2,1)} %constant.61.clone.order_ref) | copy-start | bytes 3538948
  119.2 1.2 copy-start.6
  122.4 7.9 %collective-permute-start.7 = (bf16[128,2816]{1,0:T(8,128)(2,1)S(1)}, bf16[128,2816]{1,0:T(8,128)(2,1)S(1)}, u32[]{:S(2)}, u32[]{:S(2)}) collective-permute-start(bf16[128,2816]{1,0:T(8,128)(2,1)S(1)} %get-tuple-element.49), channel_id=1, source_target_pairs={{0,1},{1,0},{2,3},{3,2},{4,5},{5,4},{6,7},{7,6},{8,9},{9,8},{10,11... | collective-permute-start | bytes 2162696 | tf_op jit(solution)/shard_map/ppermute | solution.py:43

commit v10 on v9

--- a/solution.py
+++ b/solution.py
@@ -189,15 +189,6 @@
     )
 
 
-def add_up(place, parts):
-    def kernel(place_ref, *refs):
-        *part_refs, out_ref = refs
-        out_ref[...] = sum(p[...].astype(F32) for p in part_refs).astype(BF16)
-
-    out = jax.ShapeDtypeStruct(parts[0].shape, BF16)
-    return call(kernel, [out], [whole(p.shape) for p in parts], [], LONG, (place, *parts))[0]
-
-
 def assemble(place, part, columns, received, order):
     count, half = columns.shape
     cols = part.shape[1]
@@ -231,7 +222,7 @@
         ],
         [whole(part.shape), whole(columns.shape), whole(received.shape), whole(order.shape)],
         [],
-        2 * NC * count * half * window,
+        LONG,
         (place, part, columns, received, order),
     )
 
@@ -250,17 +241,20 @@
     rows, *parts = lax.optimization_barrier((rows, *parts))
     parts = [parts[0], *(along_x(parts[step], step) for step in range(1, NX))]
     rows = gather(rows, "z", NZ)
-    total = add_up(place, parts)
+    total = sum(p.astype(F32) for p in parts).astype(BF16)
     total, rows = lax.optimization_barrier((total, rows))
     blocks = [rows, *(along_x(rows, step) for step in range(1, NX))]
 
     total = reduce(total, "z", NZ).astype(BF16)
-    total = reduce(total, "y", NY)
-    total, *blocks = lax.optimization_barrier((total, *blocks))
+    for_them, part, columns = forward(place, mine, out_grad, theirs, blocks, part_rows)
+    total, for_them = lax.optimization_barrier((total, for_them))
+    received = swap(for_them)
+    total = lax.all_to_all(total.reshape(NY, -1, total.shape[1]), "y", 0, 0)
+    projected, token_grad = assemble(place, part, columns, received, order)
+    total, projected, token_grad = lax.optimization_barrier((total, projected, token_grad))
+    total = jnp.sum(total.astype(F32), axis=0)
     count = tokens.shape[0] * NZ * NY * NX * NC
     weight_grad = total * (1.0 / math.sqrt(count))
-    for_them, part, columns = forward(place, mine, out_grad, theirs, blocks, part_rows)
-    projected, token_grad = assemble(place, part, columns, swap(for_them), order)
     return projected, token_grad, weight_grad
 
 

time: 135 us -> 145 us (1.074)
  waiting for transfers between devices: 35.6 us -> 48.7 us
  blocking collectives: 19.3 us -> 9.73 us
  starting transfers between devices: 53.5 us -> 58.5 us
  Pallas kernels: 13 us -> 9.28 us
  local copies, waits for them, and re-layouts: 8.78 us -> 12.2 us
    ppermute x6, waiting for transfers between devices: 11.1 us -> 47.8 us  [along_x(): return lax.ppermute(array, 'x', [(i, (i + step) % NX) for i in range(NX)])]
    all_to_all x1, waiting for transfers between devices: 15.6 us -> 0.01 us  [reduce(): out = lax.all_to_all(rows.reshape(size, -1, rows.shape[1]), axis, 0, 0)]
    all_to_all x1 -> x0, blocking collectives: 9.6 us -> none  [reduce(): out = lax.all_to_all(rows.reshape(size, -1, rows.shape[1]), axis, 0, 0)]
    all_to_all x1, waiting for transfers between devices: 7.7 us -> 0.01 us  [gather(): lax.all_to_all(jnp.broadcast_to(rows[None], (size, *rows.shape)), axis, 0...]
    ppermute x6, starting transfers between devices: 16.2 us -> 21.2 us  [along_x(): return lax.ppermute(array, 'x', [(i, (i + step) % NX) for i in range(NX)])]
    pallas_call x5 -> x4, Pallas kernels: 13 us -> 9.28 us  [call(): pl.pallas_call(kernel, out_shape=outs, grid_spec=pltpu.PrefetchScalarGrid...]
    ppermute x2, starting transfers between devices: 18.5 us -> 14.8 us  [swap(): return lax.ppermute(array, 'c', [(0, 1), (1, 0)])]
    all_to_all x0 -> x1, starting transfers between devices: none -> 3.35 us  [body(): total = lax.all_to_all(total.reshape(NY, -1, total.shape[1]), 'y', 0, 0)]
  transfers between devices with their start and end apart: 10 -> 11, of which waited for: 5 -> 7; matrix products, arithmetic and copies ran while one was open for 4% -> 3% of each run, Pallas kernels for 2% -> 4%
where the time goes in v10:
time: 145 us; the launch traced here: 144 us
  starting transfers between devices  58.5 us (40%)
  waiting for transfers between devices  48.7 us (34%)
  local copies, waits for them, and re-layouts  12.2 us (8%)
  blocking collectives  9.73 us (7%)
  Pallas kernels  9.28 us (6%)
  other arithmetic  4.37 us (3%)
    ppermute x6, waiting for transfers between devices, along_x(): return lax.ppermute(array, 'x', [(i, (i + step) % NX) for i in range(NX)])  47.8 us
    ppermute x6, starting transfers between devices, along_x(): return lax.ppermute(array, 'x', [(i, (i + step) % NX) for i in range(NX)])  21.2 us
    ppermute x2, starting transfers between devices, swap(): return lax.ppermute(array, 'c', [(0, 1), (1, 0)])  14.8 us
    all_to_all x1, starting transfers between devices, gather(): lax.all_to_all(jnp.broadcast_to(rows[None], (size, *rows.shape)), axis, 0...  9.88 us
    all_to_all x1, blocking collectives, gather(): lax.all_to_all(jnp.broadcast_to(rows[None], (size, *rows.shape)), axis, 0...  9.73 us
    unnamed x24, local copies, waits for them, and re-layouts  9.29 us
    pallas_call x4, Pallas kernels, call(): pl.pallas_call(kernel, out_shape=outs, grid_spec=pltpu.PrefetchScalarGrid...  9.28 us
    all_to_all x1, starting transfers between devices, reduce(): out = lax.all_to_all(rows.reshape(size, -1, rows.shape[1]), axis, 0, 0)  9.19 us
  transfers between devices with their start and end apart: 11, of which 7 were waited for; matrix products, arithmetic and copies ran while one was open for 3% of the time, Pallas kernels for 4%

profile of v10, /device:TPU:1, one launch (start us, length us, event | category | flops | bytes accessed | tf_op | source)
XLA Modules:
  0.0 143.7 jit_solution(12434240224370178635)
XLA Ops:
  0.7 1.3 copy-done
  2.0 0.9 copy-done.2
  2.9 1.3 copy-done.4
  4.2 1.6 %shard_map.76 = (bf16[128,2304]{1,0:T(8,128)(2,1)S(1)}, bf16[128,2816]{1,0:T(8,128)(2,1)S(1)}) custom-call(s32[2]{0:T(128)S(1)} %pad_add_fusion.place_ref, bf16[128,4608]{1,0:T(8,128)(2,1)S(1)} %copy-done, bf16[128,512]{1,0:T(8,128)(2,1)S(1)} %copy-done.2, bf16[768,768]{1,0:T(8,128)(2,1)S(1)} %copy-done.4), custom_call_target="tpu_custom_call" | custom-call | flops 905969664 | bytes 2621440 | tf_op jit(solution)/shard_map/pallas_call | solution.py:70
  6.6 12.4 %collective-permute-start = (bf16[128,2816]{1,0:T(8,128)(2,1)S(1)}, bf16[128,2816]{1,0:T(8,128)(2,1)S(1)}, u32[]{:S(2)}, u32[]{:S(2)}) collective-permute-start(bf16[128,2816]{1,0:T(8,128)(2,1)S(1)} %get-tuple-element.28), channel_id=1, source_target_pairs={{0,1},{1,0},{2,3},{3,2},{4,5},{5,4},{6,7},{7,6},{8,9},{9,8},{10,11... | collective-permute-start | bytes 2162696 | tf_op jit(solution)/shard_map/ppermute | solution.py:43
  20.4 1.3 compare_select_fusion
  21.8 9.7 %all_to_all.20 = bf16[8,6,512]{2,1,0:T(8,128)(2,1)S(1)} all-to-all(bf16[8,6,512]{2,1,0:T(8,128)(2,1)S(1)} %broadcast_in_dim.23), channel_id=1, replica_groups=mesh['z'=12,'y'=8,'x'=4,'c'=2] {'y'}, dimensions={0} | all-to-all | bytes 98304 | tf_op jit(solution)/shard_map/all_to_all | solution.py:51
  31.6 1.1 copy-done.7
  32.7 1.5 %shard_map.77 = (bf16[576,512]{1,0:T(8,128)(2,1)S(1)}, bf16[576,512]{1,0:T(8,128)(2,1)S(1)}, bf16[576,512]{1,0:T(8,128)(2,1)S(1)}, bf16[576,512]{1,0:T(8,128)(2,1)S(1)}) custom-call(s32[2]{0:T(128)S(1)} %pad_add_fusion.place_ref, bf16[128,2304]{1,0:T(8,128)(2,1)S(1)} %copy-done.7, bf16[128,512]{1,0:T(8,128)(2,1)S(1)} %copy-done.3, ...), custom_call_target="tpu_custom_call" | custom-call | flops 603979776 | bytes 4718592 | tf_op jit(solution)/shard_map/pallas_call | solution.py:70
  35.9 9.9 %all-to-all-start.1 = ((bf16[12,48,512]{2,1,0:T(8,128)(2,1)}), bf16[12,48,512]{2,1,0:T(8,128)(2,1)S(1)}, u32[]{:S(2)}, u32[]{:S(2)}) async-start(bf16[12,48,512]{2,1,0:T(8,128)(2,1)} %broadcast_in_dim.24), calls=%async_computation.1 | async-start | bytes 1179648 | tf_op jit(solution)/shard_map/all_to_all | solution.py:51
  45.8 3.1 %collective-permute-start.1 = (bf16[576,512]{1,0:T(8,128)(2,1)}, bf16[576,512]{1,0:T(8,128)(2,1)S(1)}, u32[]{:S(2)}, u32[]{:S(2)}) collective-permute-start(bf16[576,512]{1,0:T(8,128)(2,1)} %copy-done.1), channel_id=1, source_target_pairs={{0,2},{2,4},{4,6},{6,0},{1,3},{3,5},{5,7},{7,1},{8,10},{10,12},{12... | collective-permute-start | bytes 1769480 | tf_op jit(solution)/shard_map/ppermute | solution.py:47
  49.0 4.4 %collective-permute-start.2 = (bf16[576,512]{1,0:T(8,128)(2,1)S(1)}, bf16[576,512]{1,0:T(8,128)(2,1)S(1)}, u32[]{:S(2)}, u32[]{:S(2)}) collective-permute-start(bf16[576,512]{1,0:T(8,128)(2,1)S(1)} %get-tuple-element.38), channel_id=1, source_target_pairs={{0,4},{2,6},{4,0},{6,2},{1,5},{3,7},{5,1},{7,3},{8,12},{10,14},{12... | collective-permute-start | bytes 1769480 | tf_op jit(solution)/shard_map/ppermute | solution.py:47
  53.3 3.1 %collective-permute-start.3 = (bf16[576,512]{1,0:T(8,128)(2,1)S(1)}, bf16[576,512]{1,0:T(8,128)(2,1)S(1)}, u32[]{:S(2)}, u32[]{:S(2)}) collective-permute-start(bf16[576,512]{1,0:T(8,128)(2,1)S(1)} %get-tuple-element.39), channel_id=1, source_target_pairs={{0,6},{2,0},{4,2},{6,4},{1,7},{3,1},{5,3},{7,5},{8,14},{10,8},{12,... | collective-permute-start | bytes 1769480 | tf_op jit(solution)/shard_map/ppermute | solution.py:47
  56.4 5.7 %collective-permute-done.1 = bf16[576,512]{1,0:T(8,128)(2,1)S(1)} collective-permute-done((bf16[576,512]{1,0:T(8,128)(2,1)}, bf16[576,512]{1,0:T(8,128)(2,1)S(1)}, u32[]{:S(2)}, u32[]{:S(2)}) %collective-permute-start.1) | collective-permute-done | bytes 589856 | tf_op jit(solution)/shard_map/ppermute | solution.py:47
  62.1 13.6 %collective-permute-done.2 = bf16[576,512]{1,0:T(8,128)(2,1)S(1)} collective-permute-done((bf16[576,512]{1,0:T(8,128)(2,1)S(1)}, bf16[576,512]{1,0:T(8,128)(2,1)S(1)}, u32[]{:S(2)}, u32[]{:S(2)}) %collective-permute-start.2) | collective-permute-done | bytes 589856 | tf_op jit(solution)/shard_map/ppermute | solution.py:47
  75.8 2.5 %collective-permute-done.3 = bf16[576,512]{1,0:T(8,128)(2,1)S(1)} collective-permute-done((bf16[576,512]{1,0:T(8,128)(2,1)S(1)}, bf16[576,512]{1,0:T(8,128)(2,1)S(1)}, u32[]{:S(2)}, u32[]{:S(2)}) %collective-permute-start.3) | collective-permute-done | bytes 589856 | tf_op jit(solution)/shard_map/ppermute | solution.py:47
  78.3 1.1 add_convert_fusion
  79.4 9.2 %all-to-all-start.2 = ((bf16[12,48,512]{2,1,0:T(8,128)(2,1)}), bf16[12,48,512]{2,1,0:T(8,128)(2,1)}, u32[]{:S(2)}, u32[]{:S(2)}) async-start(bf16[12,48,512]{2,1,0:T(8,128)(2,1)} %bitcast.5), calls=%async_computation.2 | async-start | bytes 1179648 | tf_op jit(solution)/shard_map/all_to_all | solution.py:56
  88.6 5.3 %collective-permute-start.6 = (bf16[576,512]{1,0:T(8,128)(2,1)S(1)}, bf16[576,512]{1,0:T(8,128)(2,1)S(1)}, u32[]{:S(2)}, u32[]{:S(2)}) collective-permute-start(bf16[576,512]{1,0:T(8,128)(2,1)S(1)} %bitcast.6), channel_id=1, source_target_pairs={{0,6},{2,0},{4,2},{6,4},{1,7},{3,1},{5,3},{7,5},{8,14},{10,8},{12,... | collective-permute-start | bytes 1769480 | tf_op jit(solution)/shard_map/ppermute | solution.py:47
  94.0 3.4 %collective-permute-start.5 = (bf16[576,512]{1,0:T(8,128)(2,1)S(1)}, bf16[576,512]{1,0:T(8,128)(2,1)S(1)}, u32[]{:S(2)}, u32[]{:S(2)}) collective-permute-start(bf16[576,512]{1,0:T(8,128)(2,1)S(1)} %bitcast.7), channel_id=1, source_target_pairs={{0,4},{2,6},{4,0},{6,2},{1,5},{3,7},{5,1},{7,3},{8,12},{10,14},{12... | collective-permute-start | bytes 1769480 | tf_op jit(solution)/shard_map/ppermute | solution.py:47
  97.4 1.9 %collective-permute-start.4 = (bf16[576,512]{1,0:T(8,128)(2,1)S(1)}, bf16[576,512]{1,0:T(8,128)(2,1)S(1)}, u32[]{:S(2)}, u32[]{:S(2)}) collective-permute-start(bf16[576,512]{1,0:T(8,128)(2,1)S(1)} %bitcast.8), channel_id=1, source_target_pairs={{0,2},{2,4},{4,6},{6,0},{1,3},{3,5},{5,7},{7,1},{8,10},{10,12},{12... | collective-permute-start | bytes 1769480 | tf_op jit(solution)/shard_map/ppermute | solution.py:47
  99.3 7.4 %collective-permute-done.6.rest_3_ = bf16[576,512]{1,0:T(8,128)(2,1)S(1)} collective-permute-done((bf16[576,512]{1,0:T(8,128)(2,1)S(1)}, bf16[576,512]{1,0:T(8,128)(2,1)S(1)}, u32[]{:S(2)}, u32[]{:S(2)}) %collective-permute-start.6) | collective-permute-done | bytes 589856 | tf_op jit(solution)/shard_map/ppermute | solution.py:47
  106.7 4.5 %collective-permute-done.5.rest_2_ = bf16[576,512]{1,0:T(8,128)(2,1)S(1)} collective-permute-done((bf16[576,512]{1,0:T(8,128)(2,1)S(1)}, bf16[576,512]{1,0:T(8,128)(2,1)S(1)}, u32[]{:S(2)}, u32[]{:S(2)}) %collective-permute-start.5) | collective-permute-done | bytes 589856 | tf_op jit(solution)/shard_map/ppermute | solution.py:47
  111.3 14.0 %collective-permute-done.4.rest_1_ = bf16[576,512]{1,0:T(8,128)(2,1)S(1)} collective-permute-done((bf16[576,512]{1,0:T(8,128)(2,1)S(1)}, bf16[576,512]{1,0:T(8,128)(2,1)S(1)}, u32[]{:S(2)}, u32[]{:S(2)}) %collective-permute-start.4) | collective-permute-done | bytes 589856 | tf_op jit(solution)/shard_map/ppermute | solution.py:47
  125.3 2.1 %shard_map.78 = (bf16[128,2816]{1,0:T(8,128)(2,1)S(1)}, f32[128,512]{1,0:T(8,128)S(1)}, bf16[128,2304]{1,0:T(8,128)(2,1)S(1)}) custom-call(s32[2]{0:T(128)S(1)} %pad_add_fusion.place_ref, bf16[128,2304]{1,0:T(8,128)(2,1)S(1)} %copy-done.8, bf16[128,512]{1,0:T(8,128)(2,1)S(1)} %copy-done.3, bf16[128,2816]{1,0:T(8,128)(2,1)S(1)} %collective-permute-done.theirs_ref, ...), custom_call_target="tpu_custom_call" | custom-call | flops 1207959552 | bytes 3145728 | tf_op jit(solution)/shard_map/pallas_call | solution.py:70
  128.2 1.2 reduce_sum.21
  129.4 2.4 %collective-permute-start.7 = (bf16[128,2816]{1,0:T(8,128)(2,1)S(1)}, bf16[128,2816]{1,0:T(8,128)(2,1)S(1)}, u32[]{:S(2)}, u32[]{:S(2)}) collective-permute-start(bf16[128,2816]{1,0:T(8,128)(2,1)S(1)} %get-tuple-element.47), channel_id=1, source_target_pairs={{0,1},{1,0},{2,3},{3,2},{4,5},{5,4},{6,7},{7,6},{8,9},{9,8},{10,11... | collective-permute-start | bytes 2162696 | tf_op jit(solution)/shard_map/ppermute | solution.py:43
  132.4 3.3 %all-to-all-start.3 = ((bf16[8,6,512]{2,1,0:T(8,128)(2,1)}), bf16[8,6,512]{2,1,0:T(8,128)(2,1)S(1)}, u32[]{:S(2)}, u32[]{:S(2)}) async-start(bf16[8,6,512]{2,1,0:T(8,128)(2,1)} %reshape.45), calls=%async_computation.3 | async-start | bytes 131072 | tf_op jit(solution)/shard_map/all_to_all | solution.py:252
  135.8 1.3 copy-done.5
  137.1 1.1 copy-done.10
  138.1 4.0 %shard_map.79 = (bf16[128,512]{1,0:T(8,128)(2,1)}, bf16[128,4608]{1,0:T(8,128)(2,1)}) custom-call(s32[2]{0:T(128)S(1)} %pad_add_fusion.place_ref, f32[128,512]{1,0:T(8,128)S(1)} %get-tuple-element.45.part_ref, bf16[128,2304]{1,0:T(8,128)(2,1)S(1)} %copy-done.10, bf16[128,2816]{1,0:T(8,128)(2,1)S(1)} %collective-permute-done.7.received_ref, ...), custom_call_target="tpu_custom_call" | custom-call | flops 99999997952 | bytes 2621440 | tf_op jit(solution)/shard_map/pallas_call | solution.py:70
  142.1 0.9 all-to-all-done.3
  (32 shorter events, 6.2 us)
Async XLA Ops:
  0.7 1.3 copy-start
  2.0 0.9 copy-start.2
  2.9 1.3 copy-start.4
  4.2 17.6 %copy-start.11 = (bf16[6,512]{1,0:T(8,128)(2,1)S(1)}, bf16[6,512]{1,0:T(8,128)(2,1)}, u32[]{:S(2)}) copy-start(bf16[6,512]{1,0:T(8,128)(2,1)} %param.6) | copy-start | bytes 18436
  4.2 27.5 %copy-start.3 = (bf16[128,512]{1,0:T(8,128)(2,1)S(1)}, bf16[128,512]{1,0:T(8,128)(2,1)}, u32[]{:S(2)}) copy-start(bf16[128,512]{1,0:T(8,128)(2,1)} %grad_ref.5) | copy-start | bytes 393220
  5.8 0.8 copy-start.6
  6.6 25.0 %collective-permute-start = (bf16[128,2816]{1,0:T(8,128)(2,1)S(1)}, bf16[128,2816]{1,0:T(8,128)(2,1)S(1)}, u32[]{:S(2)}, u32[]{:S(2)}) collective-permute-start(bf16[128,2816]{1,0:T(8,128)(2,1)S(1)} %get-tuple-element.28), channel_id=1, source_target_pairs={{0,1},{1,0},{2,3},{3,2},{4,5},{5,4},{6,7},{7,6},{8,9},{9,8},{10,11... | collective-permute-start | bytes 2162696 | tf_op jit(solution)/shard_map/ppermute | solution.py:43
  31.6 1.1 copy-start.7
  34.2 0.8 copy-start.1
  35.9 43.5 %all-to-all-start.1 = ((bf16[12,48,512]{2,1,0:T(8,128)(2,1)}), bf16[12,48,512]{2,1,0:T(8,128)(2,1)S(1)}, u32[]{:S(2)}, u32[]{:S(2)}) async-start(bf16[12,48,512]{2,1,0:T(8,128)(2,1)} %broadcast_in_dim.24), calls=%async_computation.1 | async-start | bytes 1179648 | tf_op jit(solution)/shard_map/all_to_all | solution.py:51
  45.8 16.3 %collective-permute-start.1 = (bf16[576,512]{1,0:T(8,128)(2,1)}, bf16[576,512]{1,0:T(8,128)(2,1)S(1)}, u32[]{:S(2)}, u32[]{:S(2)}) collective-permute-start(bf16[576,512]{1,0:T(8,128)(2,1)} %copy-done.1), channel_id=1, source_target_pairs={{0,2},{2,4},{4,6},{6,0},{1,3},{3,5},{5,7},{7,1},{8,10},{10,12},{12... | collective-permute-start | bytes 1769480 | tf_op jit(solution)/shard_map/ppermute | solution.py:47
  49.0 26.8 %collective-permute-start.2 = (bf16[576,512]{1,0:T(8,128)(2,1)S(1)}, bf16[576,512]{1,0:T(8,128)(2,1)S(1)}, u32[]{:S(2)}, u32[]{:S(2)}) collective-permute-start(bf16[576,512]{1,0:T(8,128)(2,1)S(1)} %get-tuple-element.38), channel_id=1, source_target_pairs={{0,4},{2,6},{4,0},{6,2},{1,5},{3,7},{5,1},{7,3},{8,12},{10,14},{12... | collective-permute-start | bytes 1769480 | tf_op jit(solution)/shard_map/ppermute | solution.py:47
  53.3 25.0 %collective-permute-start.3 = (bf16[576,512]{1,0:T(8,128)(2,1)S(1)}, bf16[576,512]{1,0:T(8,128)(2,1)S(1)}, u32[]{:S(2)}, u32[]{:S(2)}) collective-permute-start(bf16[576,512]{1,0:T(8,128)(2,1)S(1)} %get-tuple-element.39), channel_id=1, source_target_pairs={{0,6},{2,0},{4,2},{6,4},{1,7},{3,1},{5,3},{7,5},{8,14},{10,8},{12,... | collective-permute-start | bytes 1769480 | tf_op jit(solution)/shard_map/ppermute | solution.py:47
  79.4 45.8 %copy-start.8 = (bf16[128,2304]{1,0:T(8,128)(2,1)S(1)}, bf16[128,2304]{1,0:T(8,128)(2,1)}, u32[]{:S(2)}) copy-start(bf16[128,2304]{1,0:T(8,128)(2,1)} %copy-done.6) | copy-start | bytes 1769476
  79.4 48.8 %all-to-all-start.2 = ((bf16[12,48,512]{2,1,0:T(8,128)(2,1)}), bf16[12,48,512]{2,1,0:T(8,128)(2,1)}, u32[]{:S(2)}, u32[]{:S(2)}) async-start(bf16[12,48,512]{2,1,0:T(8,128)(2,1)} %bitcast.5), calls=%async_computation.2 | async-start | bytes 1179648 | tf_op jit(solution)/shard_map/all_to_all | solution.py:56
  88.6 18.1 %collective-permute-start.6 = (bf16[576,512]{1,0:T(8,128)(2,1)S(1)}, bf16[576,512]{1,0:T(8,128)(2,1)S(1)}, u32[]{:S(2)}, u32[]{:S(2)}) collective-permute-start(bf16[576,512]{1,0:T(8,128)(2,1)S(1)} %bitcast.6), channel_id=1, source_target_pairs={{0,6},{2,0},{4,2},{6,4},{1,7},{3,1},{5,3},{7,5},{8,14},{10,8},{12,... | collective-permute-start | bytes 1769480 | tf_op jit(solution)/shard_map/ppermute | solution.py:47
  94.0 17.3 %collective-permute-start.5 = (bf16[576,512]{1,0:T(8,128)(2,1)S(1)}, bf16[576,512]{1,0:T(8,128)(2,1)S(1)}, u32[]{:S(2)}, u32[]{:S(2)}) collective-permute-start(bf16[576,512]{1,0:T(8,128)(2,1)S(1)} %bitcast.7), channel_id=1, source_target_pairs={{0,4},{2,6},{4,0},{6,2},{1,5},{3,7},{5,1},{7,3},{8,12},{10,14},{12... | collective-permute-start | bytes 1769480 | tf_op jit(solution)/shard_map/ppermute | solution.py:47
  97.4 27.8 %collective-permute-start.4 = (bf16[576,512]{1,0:T(8,128)(2,1)S(1)}, bf16[576,512]{1,0:T(8,128)(2,1)S(1)}, u32[]{:S(2)}, u32[]{:S(2)}) collective-permute-start(bf16[576,512]{1,0:T(8,128)(2,1)S(1)} %bitcast.8), channel_id=1, source_target_pairs={{0,2},{2,4},{4,6},{6,0},{1,3},{3,5},{5,7},{7,1},{8,10},{10,12},{12... | collective-permute-start | bytes 1769480 | tf_op jit(solution)/shard_map/ppermute | solution.py:47
  127.4 0.8 copy-start.9
  129.4 6.4 %collective-permute-start.7 = (bf16[128,2816]{1,0:T(8,128)(2,1)S(1)}, bf16[128,2816]{1,0:T(8,128)(2,1)S(1)}, u32[]{:S(2)}, u32[]{:S(2)}) collective-permute-start(bf16[128,2816]{1,0:T(8,128)(2,1)S(1)} %get-tuple-element.47), channel_id=1, source_target_pairs={{0,1},{1,0},{2,3},{3,2},{4,5},{5,4},{6,7},{7,6},{8,9},{9,8},{10,11... | collective-permute-start | bytes 2162696 | tf_op jit(solution)/shard_map/ppermute | solution.py:43
  132.4 10.6 %all-to-all-start.3 = ((bf16[8,6,512]{2,1,0:T(8,128)(2,1)}), bf16[8,6,512]{2,1,0:T(8,128)(2,1)S(1)}, u32[]{:S(2)}, u32[]{:S(2)}) async-start(bf16[8,6,512]{2,1,0:T(8,128)(2,1)} %reshape.45), calls=%async_computation.3 | async-start | bytes 131072 | tf_op jit(solution)/shard_map/all_to_all | solution.py:252
  135.8 1.3 copy-start.5
  137.0 1.1 copy-start.10

commit v11 on v9

--- a/solution.py
+++ b/solution.py
@@ -27,16 +27,6 @@
     order = np.zeros((size, size), ml_dtypes.bfloat16)
     order[places.reshape(-1), np.arange(size)] = 1
     return order
-
-
-def scaled_rows(w_values, w_scales):
-    rows = w_values.shape[0]
-    first = lax.axis_index(AXES) * rows
-    start = first // BLOCK_ROWS
-    pair = lax.dynamic_slice(w_scales, (start,), (2,))
-    block = (first + lax.iota(jnp.int32, rows)) // BLOCK_ROWS - start
-    scale = jnp.where(block == 0, pair[0], pair[1])
-    return (w_values.astype(F32) * scale[:, None]).astype(BF16)
 
 
 def swap(array):
@@ -82,33 +72,84 @@
     )(*args)
 
 
-def sort_columns(place, tokens, grad, order):
+def sort_columns(place, tokens, grad, order, w_values, w_scales):
     count, cols = grad.shape
     half = tokens.shape[1] // NC
     window = order.shape[0]
     part = window // NC
-
-    def kernel(place_ref, tokens_ref, grad_ref, order_ref, mine_ref, send_ref):
+    windows = tokens.shape[1] // window
+    rows = w_values.shape[0]
+
+    def kernel(
+        place_ref,
+        scales_ref,
+        tokens_ref,
+        order_ref,
+        grad_ref,
+        values_ref,
+        mine_ref,
+        send_ref,
+        rows_ref,
+        tokens_here,
+        order_here,
+        sems,
+        order_sem,
+    ):
+        fetch_order = pltpu.make_async_copy(order_ref, order_here, order_sem)
+        fetch_order.start()
+        fetches = [
+            pltpu.make_async_copy(
+                tokens_ref.at[:, pl.ds(k * window, window)], tokens_here.at[k], sems.at[k]
+            )
+            for k in range(windows)
+        ]
+        for fetch in fetches:
+            fetch.start()
+
+        first_row = place_ref[2] * rows
+        start = lax.div(first_row, BLOCK_ROWS)
+        row = first_row + lax.broadcasted_iota(jnp.int32, (rows, cols), 0)
+        scale = jnp.where(
+            row < (start + 1) * BLOCK_ROWS, scales_ref[start], scales_ref[start + 1]
+        )
+        scaled = (values_ref[...].astype(F32) * scale).astype(BF16)
+        for k in range(NY):
+            rows_ref[k] = scaled
+        send_ref[:, half:] = grad_ref[...]
+
+        fetch_order.wait()
         first = place_ref[0] == 0
-        for k in range(tokens.shape[1] // window):
-            both = dot(tokens_ref[:, k * window : (k + 1) * window], order_ref[...], (1, 0))
+        for k, fetch in enumerate(fetches):
+            fetch.wait()
+            both = dot(tokens_here[k], order_here[...], (1, 0))
             low, high = both[:, :part], both[:, part:]
             at = slice(k * part, (k + 1) * part)
             mine_ref[:, at] = jnp.where(first, low, high).astype(BF16)
             send_ref[:, at] = jnp.where(first, high, low).astype(BF16)
-        send_ref[:, half:] = grad_ref[...]
-
-    return call(
-        kernel,
-        [
+
+    smem = pl.BlockSpec(memory_space=pltpu.SMEM)
+    vmem = pl.BlockSpec(memory_space=pltpu.VMEM)
+    hbm = pl.BlockSpec(memory_space=pltpu.HBM)
+    return pl.pallas_call(
+        kernel,
+        out_shape=[
             jax.ShapeDtypeStruct((count, half), BF16),
             jax.ShapeDtypeStruct((count, half + cols), BF16),
-        ],
-        [whole(tokens.shape), whole(grad.shape), whole(order.shape)],
-        [],
-        2 * tokens.size * window,
-        (place, tokens, grad, order),
-    )
+            jax.ShapeDtypeStruct((NY, rows, cols), BF16),
+        ],
+        in_specs=[smem, smem, hbm, hbm, vmem, vmem],
+        out_specs=[vmem] * 3,
+        scratch_shapes=[
+            pltpu.VMEM((windows, count, window), BF16),
+            pltpu.VMEM(order.shape, BF16),
+            pltpu.SemaphoreType.DMA((windows,)),
+            pltpu.SemaphoreType.DMA,
+        ],
+        compiler_params=PARAMS,
+        cost_estimate=pl.CostEstimate(
+            flops=2 * tokens.size * window, bytes_accessed=6 * tokens.size, transcendentals=0
+        ),
+    )(place, w_scales, tokens, order, grad, w_values)
 
 
 def x_rows(window, block, part):
@@ -203,47 +244,67 @@
     cols = part.shape[1]
     window = order.shape[0]
     width = window // NC
-
-    def kernel(place_ref, part_ref, columns_ref, received_ref, order_ref, projected_ref, out_ref):
+    windows = half // width
+
+    def kernel(
+        place_ref,
+        part_ref,
+        columns_ref,
+        received_ref,
+        order_ref,
+        projected_ref,
+        out_ref,
+        out_here,
+        sems,
+    ):
+        def leave(k):
+            return pltpu.make_async_copy(
+                out_here.at[k], out_ref.at[:, pl.ds(k * window, window)], sems.at[k]
+            )
+
+        first = place_ref[0] == 0
+        for k in range(windows):
+            at = slice(k * width, (k + 1) * width)
+            own, other = columns_ref[:, at].astype(F32), received_ref[:, at].astype(F32)
+            both = jnp.concatenate(
+                [jnp.where(first, own, other), jnp.where(first, other, own)], axis=1
+            )
+            out_here[k] = dot(both.astype(BF16), order_ref[...], (1, 1)).astype(BF16)
+            leave(k).start()
         projected_ref[...] = (part_ref[...] + received_ref[:, half:].astype(F32)).astype(BF16)
-
-        def put(low_ref, high_ref):
-            for k in range(half // width):
-                at = slice(k * width, (k + 1) * width)
-                both = jnp.concatenate([low_ref[:, at], high_ref[:, at]], axis=1)
-                out_ref[:, k * window : (k + 1) * window] = dot(
-                    both, order_ref[...], (1, 1)
-                ).astype(BF16)
-
-        @pl.when(place_ref[0] == 0)
-        def _():
-            put(columns_ref, received_ref)
-
-        @pl.when(place_ref[0] == 1)
-        def _():
-            put(received_ref, columns_ref)
-
-    return call(
-        kernel,
-        [
+        for k in range(windows):
+            leave(k).wait()
+
+    vmem = pl.BlockSpec(memory_space=pltpu.VMEM)
+    return pl.pallas_call(
+        kernel,
+        out_shape=[
             jax.ShapeDtypeStruct((count, cols), BF16),
             jax.ShapeDtypeStruct((count, NC * half), BF16),
         ],
-        [whole(part.shape), whole(columns.shape), whole(received.shape), whole(order.shape)],
-        [],
-        2 * NC * count * half * window,
-        (place, part, columns, received, order),
-    )
+        in_specs=[pl.BlockSpec(memory_space=pltpu.SMEM), *[vmem] * 4],
+        out_specs=[vmem, pl.BlockSpec(memory_space=pltpu.HBM)],
+        scratch_shapes=[
+            pltpu.VMEM((windows, count, window), BF16),
+            pltpu.SemaphoreType.DMA((windows,)),
+        ],
+        compiler_params=PARAMS,
+        cost_estimate=pl.CostEstimate(
+            flops=2 * NC * count * half * window,
+            bytes_accessed=8 * count * half,
+            transcendentals=0,
+        ),
+    )(place, part, columns, received, order)
 
 
 def body(tokens, w_values, w_scales, out_grad):
     core, x = lax.axis_index("c"), lax.axis_index("x")
-    place = jnp.stack([core, x]).astype(jnp.int32)
+    place = jnp.stack([core, x, lax.axis_index(AXES)]).astype(jnp.int32)
     order = jnp.asarray(column_order(w_values.shape[0]))
     part_rows = order.shape[0] // (NC * NX)
-    mine, send = sort_columns(place, tokens, out_grad, order)
+    mine, send, rows = sort_columns(place, tokens, out_grad, order, w_values, w_scales)
     theirs = swap(send)
-    rows = gather(scaled_rows(w_values, w_scales), "y", NY)
+    rows = lax.all_to_all(rows, "y", 0, 0).reshape(-1, out_grad.shape[1])
     theirs, rows = lax.optimization_barrier((theirs, rows))
 
     parts = partials(place, mine, out_grad, theirs, part_rows)

time: 135 us -> 136 us (level)
  Pallas kernels: 13 us -> 15 us
  other arithmetic: 3.23 us -> 1.86 us
    pallas_call x0 -> x2, Pallas kernels: none -> 7.66 us  [the longest x1 4.35 us: assemble(): pl.pallas_call(kernel, out_shape=[jax.ShapeDtypeStruct((count, cols), BF1...]
    pallas_call x5 -> x3, Pallas kernels: 13 us -> 7.37 us  [call(): pl.pallas_call(kernel, out_shape=outs, grid_spec=pltpu.PrefetchScalarGrid...]
    unnamed x20 -> x22, local copies, waits for them, and re-layouts: 6.5 us -> 7.89 us
  transfers between devices with their start and end apart: 10 -> 10, of which waited for: 5 -> 5; matrix products, arithmetic and copies ran while one was open for 4% -> 2% of each run, Pallas kernels for 2% -> 2%
where the time goes in v11:
time: 136 us; the launch traced here: 135 us
  starting transfers between devices  53.5 us (39%)
  waiting for transfers between devices  35.6 us (26%)
  blocking collectives  19.3 us (14%)
  Pallas kernels  15 us (11%)
  local copies, waits for them, and re-layouts  8.81 us (6%)
  other arithmetic  1.86 us (1%)
    ppermute x2, starting transfers between devices, swap(): return lax.ppermute(array, 'c', [(0, 1), (1, 0)])  18.5 us
    ppermute x6, starting transfers between devices, along_x(): return lax.ppermute(array, 'x', [(i, (i + step) % NX) for i in range(NX)])  16.2 us
    all_to_all x1, waiting for transfers between devices, reduce(): out = lax.all_to_all(rows.reshape(size, -1, rows.shape[1]), axis, 0, 0)  15.6 us
    all_to_all x1, starting transfers between devices, gather(): lax.all_to_all(jnp.broadcast_to(rows[None], (size, *rows.shape)), axis, 0...  12 us
    ppermute x6, waiting for transfers between devices, along_x(): return lax.ppermute(array, 'x', [(i, (i + step) % NX) for i in range(NX)])  11.1 us
    all_to_all x1, blocking collectives, body(): rows = lax.all_to_all(rows, 'y', 0, 0).reshape(-1, out_grad.shape[1])  9.74 us
    all_to_all x1, blocking collectives, reduce(): out = lax.all_to_all(rows.reshape(size, -1, rows.shape[1]), axis, 0, 0)  9.6 us
    unnamed x22, local copies, waits for them, and re-layouts  7.89 us
  transfers between devices with their start and end apart: 10, of which 5 were waited for; matrix products, arithmetic and copies ran while one was open for 2% of the time, Pallas kernels for 2%

profile of v11, /device:TPU:1, one launch (start us, length us, event | category | flops | bytes accessed | tf_op | source)
XLA Modules:
  0.0 135.0 jit_solution(1979151068168221550)
XLA Ops:
  0.7 1.3 copy-done
  2.0 0.9 copy-done.1
  2.9 0.7 copy-done.3
  3.6 0.7 copy-done.4
  4.3 1.3 copy-done.5
  5.6 3.3 %shard_map.76 = (bf16[128,2304]{1,0:T(8,128)(2,1)S(1)}, bf16[128,2816]{1,0:T(8,128)(2,1)S(1)}, bf16[8,6,512]{2,1,0:T(8,128)(2,1)S(1)}) custom-call(s32[3]{0:T(128)S(1)} %pad_add_fusion.place_ref, f32[1152]{0:T(1024)S(1)} %copy-done.3, bf16[128,4608]{1,0:T(8,128)(2,1)S(1)} %copy-done, bf16[768,768]{1,0:T(8,128)(2,1)S(1)} %copy-done.5, ...), custom_call_target="tpu_custom_call" | custom-call | flops 905969664 | bytes 3538944 | tf_op jit(solution)/shard_map/pallas_call | solution.py:133
  8.9 12.4 %collective-permute-start = (bf16[128,2816]{1,0:T(8,128)(2,1)S(1)}, bf16[128,2816]{1,0:T(8,128)(2,1)S(1)}, u32[]{:S(2)}, u32[]{:S(2)}) collective-permute-start(bf16[128,2816]{1,0:T(8,128)(2,1)S(1)} %get-tuple-element.30), channel_id=1, source_target_pairs={{0,1},{1,0},{2,3},{3,2},{4,5},{5,4},{6,7},{7,6},{8,9},{9,8},{10,11... | collective-permute-start | bytes 2162696 | tf_op jit(solution)/shard_map/ppermute | solution.py:33
  21.3 9.7 %all_to_all.20 = bf16[8,6,512]{2,1,0:T(8,128)(2,1)S(1)} all-to-all(bf16[8,6,512]{2,1,0:T(8,128)(2,1)S(1)} %get-tuple-element.31), channel_id=1, replica_groups=mesh['z'=12,'y'=8,'x'=4,'c'=2] {'y'}, dimensions={0} | all-to-all | bytes 98304 | tf_op jit(solution)/shard_map/all_to_all | solution.py:307
  31.1 2.3 %shard_map.77 = (bf16[576,512]{1,0:T(8,128)(2,1)S(1)}, bf16[576,512]{1,0:T(8,128)(2,1)}, bf16[576,512]{1,0:T(8,128)(2,1)S(1)}, bf16[576,512]{1,0:T(8,128)(2,1)S(1)}) custom-call(s32[3]{0:T(128)S(1)} %pad_add_fusion.place_ref, bf16[128,2304]{1,0:T(8,128)(2,1)S(1)} %get-tuple-element.29.mine_ref, bf16[128,512]{1,0:T(8,128)(2,1)S(1)} %copy-done.2, ...), custom_call_target="tpu_custom_call" | custom-call | flops 603979776 | bytes 4718592 | tf_op jit(solution)/shard_map/pallas_call | solution.py:60
  33.5 0.8 copy-done.9
  34.3 1.9 %collective-permute-start.1 = (bf16[576,512]{1,0:T(8,128)(2,1)}, bf16[576,512]{1,0:T(8,128)(2,1)S(1)}, u32[]{:S(2)}, u32[]{:S(2)}) collective-permute-start(bf16[576,512]{1,0:T(8,128)(2,1)} %get-tuple-element.39), channel_id=1, source_target_pairs={{0,2},{2,4},{4,6},{6,0},{1,3},{3,5},{5,7},{7,1},{8,10},{10,12},{12... | collective-permute-start | bytes 1769480 | tf_op jit(solution)/shard_map/ppermute | solution.py:37
  36.2 1.9 %collective-permute-start.2 = (bf16[576,512]{1,0:T(8,128)(2,1)S(1)}, bf16[576,512]{1,0:T(8,128)(2,1)}, u32[]{:S(2)}, u32[]{:S(2)}) collective-permute-start(bf16[576,512]{1,0:T(8,128)(2,1)S(1)} %get-tuple-element.40), channel_id=1, source_target_pairs={{0,4},{2,6},{4,0},{6,2},{1,5},{3,7},{5,1},{7,3},{8,12},{10,14},{12... | collective-permute-start | bytes 1769480 | tf_op jit(solution)/shard_map/ppermute | solution.py:37
  38.1 4.6 %collective-permute-start.3 = (bf16[576,512]{1,0:T(8,128)(2,1)S(1)}, bf16[576,512]{1,0:T(8,128)(2,1)}, u32[]{:S(2)}, u32[]{:S(2)}) collective-permute-start(bf16[576,512]{1,0:T(8,128)(2,1)S(1)} %get-tuple-element.41), channel_id=1, source_target_pairs={{0,6},{2,0},{4,2},{6,4},{1,7},{3,1},{5,3},{7,5},{8,14},{10,8},{12,... | collective-permute-start | bytes 1769480 | tf_op jit(solution)/shard_map/ppermute | solution.py:37
  42.7 0.9 broadcast_in_dim.2
  43.6 12.0 %all-to-all-start.1 = ((bf16[12,48,512]{2,1,0:T(8,128)(2,1)}), bf16[12,48,512]{2,1,0:T(8,128)(2,1)S(1)}, u32[]{:S(2)}, u32[]{:S(2)}) async-start(bf16[12,48,512]{2,1,0:T(8,128)(2,1)} %broadcast_in_dim.2), calls=%async_computation.1 | async-start | bytes 1179648 | tf_op jit(solution)/shard_map/all_to_all | solution.py:41
  55.6 8.2 %collective-permute-done.1.refs_1_ = bf16[576,512]{1,0:T(8,128)(2,1)S(1)} collective-permute-done((bf16[576,512]{1,0:T(8,128)(2,1)}, bf16[576,512]{1,0:T(8,128)(2,1)S(1)}, u32[]{:S(2)}, u32[]{:S(2)}) %collective-permute-start.1) | collective-permute-done | bytes 589856 | tf_op jit(solution)/shard_map/ppermute | solution.py:37
  63.8 2.9 %collective-permute-done.3.refs_3_ = bf16[576,512]{1,0:T(8,128)(2,1)} collective-permute-done((bf16[576,512]{1,0:T(8,128)(2,1)S(1)}, bf16[576,512]{1,0:T(8,128)(2,1)}, u32[]{:S(2)}, u32[]{:S(2)}) %collective-permute-start.3) | collective-permute-done | bytes 589856 | tf_op jit(solution)/shard_map/ppermute | solution.py:37
  66.7 1.1 copy-done.10
  67.8 2.9 %shard_map.78 = bf16[576,512]{1,0:T(8,128)(2,1)} custom-call(s32[3]{0:T(128)S(1)} %pad_add_fusion.place_ref, bf16[576,512]{1,0:T(8,128)(2,1)S(1)} %copy-done.10, bf16[576,512]{1,0:T(8,128)(2,1)S(1)} %collective-permute-done.1.refs_1_, bf16[576,512]{1,0:T(8,128)(2,1)} %collective-permute-done.2.refs_2_, bf16[576,512]{1,0:T(8,128)(2,1)} %collective-permute-done.3.refs_3_), custom_call_target="tpu_custom_call" | custom-call | flops 99999997952 | bytes 1179648 | tf_op jit(solution)/shard_map/pallas_call | solution.py:60
  70.7 7.7 %all-to-all-done.1 = bf16[12,48,512]{2,1,0:T(8,128)(2,1)S(1)} async-done(((bf16[12,48,512]{2,1,0:T(8,128)(2,1)}), bf16[12,48,512]{2,1,0:T(8,128)(2,1)S(1)}, u32[]{:S(2)}, u32[]{:S(2)}) %all-to-all-start.1) | async-done | bytes 589856 | tf_op jit(solution)/shard_map/all_to_all | solution.py:41
  78.4 6.7 %all-to-all-start.2 = ((bf16[12,48,512]{2,1,0:T(8,128)(2,1)}), bf16[12,48,512]{2,1,0:T(8,128)(2,1)}, u32[]{:S(2)}, u32[]{:S(2)}) async-start(bf16[12,48,512]{2,1,0:T(8,128)(2,1)} %bitcast.4), calls=%async_computation.2 | async-start | bytes 1179648 | tf_op jit(solution)/shard_map/all_to_all | solution.py:46
  85.1 1.9 %collective-permute-start.6 = (bf16[576,512]{1,0:T(8,128)(2,1)S(1)}, bf16[576,512]{1,0:T(8,128)(2,1)S(1)}, u32[]{:S(2)}, u32[]{:S(2)}) collective-permute-start(bf16[576,512]{1,0:T(8,128)(2,1)S(1)} %bitcast.5), channel_id=1, source_target_pairs={{0,6},{2,0},{4,2},{6,4},{1,7},{3,1},{5,3},{7,5},{8,14},{10,8},{12,... | collective-permute-start | bytes 1769480 | tf_op jit(solution)/shard_map/ppermute | solution.py:37
  87.0 4.0 %collective-permute-start.5 = (bf16[576,512]{1,0:T(8,128)(2,1)S(1)}, bf16[576,512]{1,0:T(8,128)(2,1)S(1)}, u32[]{:S(2)}, u32[]{:S(2)}) collective-permute-start(bf16[576,512]{1,0:T(8,128)(2,1)S(1)} %bitcast.6), channel_id=1, source_target_pairs={{0,4},{2,6},{4,0},{6,2},{1,5},{3,7},{5,1},{7,3},{8,12},{10,14},{12... | collective-permute-start | bytes 1769480 | tf_op jit(solution)/shard_map/ppermute | solution.py:37
  91.1 1.9 %collective-permute-start.4 = (bf16[576,512]{1,0:T(8,128)(2,1)S(1)}, bf16[576,512]{1,0:T(8,128)(2,1)S(1)}, u32[]{:S(2)}, u32[]{:S(2)}) collective-permute-start(bf16[576,512]{1,0:T(8,128)(2,1)S(1)} %bitcast.7), channel_id=1, source_target_pairs={{0,2},{2,4},{4,6},{6,0},{1,3},{3,5},{5,7},{7,1},{8,10},{10,12},{12... | collective-permute-start | bytes 1769480 | tf_op jit(solution)/shard_map/ppermute | solution.py:37
  93.0 15.6 %all-to-all-done.2 = bf16[12,48,512]{2,1,0:T(8,128)(2,1)} async-done(((bf16[12,48,512]{2,1,0:T(8,128)(2,1)}), bf16[12,48,512]{2,1,0:T(8,128)(2,1)}, u32[]{:S(2)}, u32[]{:S(2)}) %all-to-all-start.2) | async-done | bytes 589856 | tf_op jit(solution)/shard_map/all_to_all | solution.py:46
  108.6 1.2 reduce_sum.21
  109.8 9.6 %all_to_all.21 = bf16[8,6,512]{2,1,0:T(8,128)(2,1)S(1)} all-to-all(bf16[8,6,512]{2,1,0:T(8,128)(2,1)S(1)} %reshape.22), channel_id=1, replica_groups=mesh['z'=12,'y'=8,'x'=4,'c'=2] {'y'}, dimensions={0} | all-to-all | bytes 98304 | tf_op jit(solution)/shard_map/all_to_all | solution.py:46
  119.5 1.1 copy-done.8
  120.6 2.1 %shard_map.79 = (bf16[128,2816]{1,0:T(8,128)(2,1)S(1)}, f32[128,512]{1,0:T(8,128)S(1)}, bf16[128,2304]{1,0:T(8,128)(2,1)S(1)}) custom-call(s32[3]{0:T(128)S(1)} %pad_add_fusion.place_ref, bf16[128,2304]{1,0:T(8,128)(2,1)S(1)} %copy-done.8, bf16[128,512]{1,0:T(8,128)(2,1)S(1)} %copy-done.2, bf16[128,2816]{1,0:T(8,128)(2,1)S(1)} %collective-permute-done.theirs_ref, ...), custom_call_target="tpu_custom_call" | custom-call | flops 1207959552 | bytes 3145728 | tf_op jit(solution)/shard_map/pallas_call | solution.py:60
  122.7 6.1 %collective-permute-start.7 = (bf16[128,2816]{1,0:T(8,128)(2,1)S(1)}, bf16[128,2816]{1,0:T(8,128)(2,1)S(1)}, u32[]{:S(2)}, u32[]{:S(2)}) collective-permute-start(bf16[128,2816]{1,0:T(8,128)(2,1)S(1)} %get-tuple-element.51), channel_id=1, source_target_pairs={{0,1},{1,0},{2,3},{3,2},{4,5},{5,4},{6,7},{7,6},{8,9},{9,8},{10,11... | collective-permute-start | bytes 2162696 | tf_op jit(solution)/shard_map/ppermute | solution.py:33
  129.4 1.2 collective-permute-done.7.received_ref
  130.6 4.4 %shard_map.80 = (bf16[128,512]{1,0:T(8,128)(2,1)}, bf16[128,4608]{1,0:T(8,128)(2,1)}) custom-call(s32[3]{0:T(128)S(1)} %pad_add_fusion.place_ref, f32[128,512]{1,0:T(8,128)S(1)} %get-tuple-element.49.part_ref, bf16[128,2304]{1,0:T(8,128)(2,1)S(1)} %get-tuple-element.50.columns_ref, bf16[128,2816]{1,0:T(8,128)(2,1)S(1)} %collective-permute-done.7.received_ref, ...), custom_call_target="tpu_custom_call" | custom-call | flops 905969664 | bytes 2359296 | tf_op jit(solution)/shard_map/pallas_call | solution.py:279
  (24 shorter events, 0.8 us)
Async XLA Ops:
  0.7 1.3 copy-start
  2.0 0.9 copy-start.1
  2.9 0.7 copy-start.3
  3.6 0.7 copy-start.4
  4.3 1.3 copy-start.5
  5.6 25.5 %copy-start.2 = (bf16[128,512]{1,0:T(8,128)(2,1)S(1)}, bf16[128,512]{1,0:T(8,128)(2,1)}, u32[]{:S(2)}) copy-start(bf16[128,512]{1,0:T(8,128)(2,1)} %grad_ref.5) | copy-start | bytes 393220
  8.9 24.6 %copy-start.7 = (bf16[128,2304]{1,0:T(8,128)(2,1)}, bf16[128,2304]{1,0:T(8,128)(2,1)S(1)}, u32[]{:S(2)}) copy-start(bf16[128,2304]{1,0:T(8,128)(2,1)S(1)} %get-tuple-element.29.mine_ref) | copy-start | bytes 1769476
  8.9 22.2 %collective-permute-start = (bf16[128,2816]{1,0:T(8,128)(2,1)S(1)}, bf16[128,2816]{1,0:T(8,128)(2,1)S(1)}, u32[]{:S(2)}, u32[]{:S(2)}) collective-permute-start(bf16[128,2816]{1,0:T(8,128)(2,1)S(1)} %get-tuple-element.30), channel_id=1, source_target_pairs={{0,1},{1,0},{2,3},{3,2},{4,5},{5,4},{6,7},{7,6},{8,9},{9,8},{10,11... | collective-permute-start | bytes 2162696 | tf_op jit(solution)/shard_map/ppermute | solution.py:33
  33.5 0.8 copy-start.9
  34.3 29.5 %collective-permute-start.1 = (bf16[576,512]{1,0:T(8,128)(2,1)}, bf16[576,512]{1,0:T(8,128)(2,1)S(1)}, u32[]{:S(2)}, u32[]{:S(2)}) collective-permute-start(bf16[576,512]{1,0:T(8,128)(2,1)} %get-tuple-element.39), channel_id=1, source_target_pairs={{0,2},{2,4},{4,6},{6,0},{1,3},{3,5},{5,7},{7,1},{8,10},{10,12},{12... | collective-permute-start | bytes 1769480 | tf_op jit(solution)/shard_map/ppermute | solution.py:37
  36.2 27.6 %collective-permute-start.2 = (bf16[576,512]{1,0:T(8,128)(2,1)S(1)}, bf16[576,512]{1,0:T(8,128)(2,1)}, u32[]{:S(2)}, u32[]{:S(2)}) collective-permute-start(bf16[576,512]{1,0:T(8,128)(2,1)S(1)} %get-tuple-element.40), channel_id=1, source_target_pairs={{0,4},{2,6},{4,0},{6,2},{1,5},{3,7},{5,1},{7,3},{8,12},{10,14},{12... | collective-permute-start | bytes 1769480 | tf_op jit(solution)/shard_map/ppermute | solution.py:37
  38.1 28.6 %collective-permute-start.3 = (bf16[576,512]{1,0:T(8,128)(2,1)S(1)}, bf16[576,512]{1,0:T(8,128)(2,1)}, u32[]{:S(2)}, u32[]{:S(2)}) collective-permute-start(bf16[576,512]{1,0:T(8,128)(2,1)S(1)} %get-tuple-element.41), channel_id=1, source_target_pairs={{0,6},{2,0},{4,2},{6,4},{1,7},{3,1},{5,3},{7,5},{8,14},{10,8},{12,... | collective-permute-start | bytes 1769480 | tf_op jit(solution)/shard_map/ppermute | solution.py:37
  43.6 34.8 %all-to-all-start.1 = ((bf16[12,48,512]{2,1,0:T(8,128)(2,1)}), bf16[12,48,512]{2,1,0:T(8,128)(2,1)S(1)}, u32[]{:S(2)}, u32[]{:S(2)}) async-start(bf16[12,48,512]{2,1,0:T(8,128)(2,1)} %broadcast_in_dim.2), calls=%async_computation.1 | async-start | bytes 1179648 | tf_op jit(solution)/shard_map/all_to_all | solution.py:41
  66.7 1.1 copy-start.10
  78.4 30.2 %all-to-all-start.2 = ((bf16[12,48,512]{2,1,0:T(8,128)(2,1)}), bf16[12,48,512]{2,1,0:T(8,128)(2,1)}, u32[]{:S(2)}, u32[]{:S(2)}) async-start(bf16[12,48,512]{2,1,0:T(8,128)(2,1)} %bitcast.4), calls=%async_computation.2 | async-start | bytes 1179648 | tf_op jit(solution)/shard_map/all_to_all | solution.py:46
  85.1 34.3 %collective-permute-start.6 = (bf16[576,512]{1,0:T(8,128)(2,1)S(1)}, bf16[576,512]{1,0:T(8,128)(2,1)S(1)}, u32[]{:S(2)}, u32[]{:S(2)}) collective-permute-start(bf16[576,512]{1,0:T(8,128)(2,1)S(1)} %bitcast.5), channel_id=1, source_target_pairs={{0,6},{2,0},{4,2},{6,4},{1,7},{3,1},{5,3},{7,5},{8,14},{10,8},{12,... | collective-permute-start | bytes 1769480 | tf_op jit(solution)/shard_map/ppermute | solution.py:37
  87.0 32.4 %collective-permute-start.5 = (bf16[576,512]{1,0:T(8,128)(2,1)S(1)}, bf16[576,512]{1,0:T(8,128)(2,1)S(1)}, u32[]{:S(2)}, u32[]{:S(2)}) collective-permute-start(bf16[576,512]{1,0:T(8,128)(2,1)S(1)} %bitcast.6), channel_id=1, source_target_pairs={{0,4},{2,6},{4,0},{6,2},{1,5},{3,7},{5,1},{7,3},{8,12},{10,14},{12... | collective-permute-start | bytes 1769480 | tf_op jit(solution)/shard_map/ppermute | solution.py:37
  91.1 28.4 %collective-permute-start.4 = (bf16[576,512]{1,0:T(8,128)(2,1)S(1)}, bf16[576,512]{1,0:T(8,128)(2,1)S(1)}, u32[]{:S(2)}, u32[]{:S(2)}) collective-permute-start(bf16[576,512]{1,0:T(8,128)(2,1)S(1)} %bitcast.7), channel_id=1, source_target_pairs={{0,2},{2,4},{4,6},{6,0},{1,3},{3,5},{5,7},{7,1},{8,10},{10,12},{12... | collective-permute-start | bytes 1769480 | tf_op jit(solution)/shard_map/ppermute | solution.py:37
  119.4 11.2 %copy-start.6 = (bf16[768,768]{1,0:T(8,128)(2,1)S(1)}, bf16[768,768]{1,0:T(8,128)(2,1)}, u32[]{:S(2)}) copy-start(bf16[768,768]{1,0:T(8,128)(2,1)} %constant.31.clone.order_ref) | copy-start | bytes 3538948
  119.4 1.2 copy-start.8
  122.7 7.9 %collective-permute-start.7 = (bf16[128,2816]{1,0:T(8,128)(2,1)S(1)}, bf16[128,2816]{1,0:T(8,128)(2,1)S(1)}, u32[]{:S(2)}, u32[]{:S(2)}) collective-permute-start(bf16[128,2816]{1,0:T(8,128)(2,1)S(1)} %get-tuple-element.51), channel_id=1, source_target_pairs={{0,1},{1,0},{2,3},{3,2},{4,5},{5,4},{6,7},{7,6},{8,9},{9,8},{10,11... | collective-permute-start | bytes 2162696 | tf_op jit(solution)/shard_map/ppermute | solution.py:33

commit v12 on v11

--- a/solution.py
+++ b/solution.py
@@ -90,22 +90,7 @@
         mine_ref,
         send_ref,
         rows_ref,
-        tokens_here,
-        order_here,
-        sems,
-        order_sem,
     ):
-        fetch_order = pltpu.make_async_copy(order_ref, order_here, order_sem)
-        fetch_order.start()
-        fetches = [
-            pltpu.make_async_copy(
-                tokens_ref.at[:, pl.ds(k * window, window)], tokens_here.at[k], sems.at[k]
-            )
-            for k in range(windows)
-        ]
-        for fetch in fetches:
-            fetch.start()
-
         first_row = place_ref[2] * rows
         start = lax.div(first_row, BLOCK_ROWS)
         row = first_row + lax.broadcasted_iota(jnp.int32, (rows, cols), 0)
@@ -117,19 +102,17 @@
             rows_ref[k] = scaled
         send_ref[:, half:] = grad_ref[...]
 
-        fetch_order.wait()
-        first = place_ref[0] == 0
-        for k, fetch in enumerate(fetches):
-            fetch.wait()
-            both = dot(tokens_here[k], order_here[...], (1, 0))
-            low, high = both[:, :part], both[:, part:]
-            at = slice(k * part, (k + 1) * part)
-            mine_ref[:, at] = jnp.where(first, low, high).astype(BF16)
-            send_ref[:, at] = jnp.where(first, high, low).astype(BF16)
+        stacked = jnp.concatenate(
+            [tokens_ref[:, k * window : (k + 1) * window] for k in range(windows)], axis=0
+        )
+        for core, out_ref in ((place_ref[0], mine_ref), (1 - place_ref[0], send_ref)):
+            columns = order_ref[:, pl.ds(pl.multiple_of(core * part, part), part)]
+            chosen = dot(stacked, columns, (1, 0)).astype(BF16)
+            for k in range(windows):
+                out_ref[:, k * part : (k + 1) * part] = chosen[k * count : (k + 1) * count]
 
     smem = pl.BlockSpec(memory_space=pltpu.SMEM)
     vmem = pl.BlockSpec(memory_space=pltpu.VMEM)
-    hbm = pl.BlockSpec(memory_space=pltpu.HBM)
     return pl.pallas_call(
         kernel,
         out_shape=[
@@ -137,14 +120,8 @@
             jax.ShapeDtypeStruct((count, half + cols), BF16),
             jax.ShapeDtypeStruct((NY, rows, cols), BF16),
         ],
-        in_specs=[smem, smem, hbm, hbm, vmem, vmem],
+        in_specs=[smem, smem, *[vmem] * 4],
         out_specs=[vmem] * 3,
-        scratch_shapes=[
-            pltpu.VMEM((windows, count, window), BF16),
-            pltpu.VMEM(order.shape, BF16),
-            pltpu.SemaphoreType.DMA((windows,)),
-            pltpu.SemaphoreType.DMA,
-        ],
         compiler_params=PARAMS,
         cost_estimate=pl.CostEstimate(
             flops=2 * tokens.size * window, bytes_accessed=6 * tokens.size, transcendentals=0
@@ -262,14 +239,16 @@
                 out_here.at[k], out_ref.at[:, pl.ds(k * window, window)], sems.at[k]
             )
 
-        first = place_ref[0] == 0
+        total = None
+        for core, side_ref in ((place_ref[0], columns_ref), (1 - place_ref[0], received_ref)):
+            stacked = jnp.concatenate(
+                [side_ref[:, k * width : (k + 1) * width] for k in range(windows)], axis=0
+            )
+            order_half = order_ref[:, pl.ds(pl.multiple_of(core * width, width), width)]
+            product = dot(stacked, order_half, (1, 1))
+            total = product if total is None else total + product
         for k in range(windows):
-            at = slice(k * width, (k + 1) * width)
-            own, other = columns_ref[:, at].astype(F32), received_ref[:, at].astype(F32)
-            both = jnp.concatenate(
-                [jnp.where(first, own, other), jnp.where(first, other, own)], axis=1
-            )
-            out_here[k] = dot(both.astype(BF16), order_ref[...], (1, 1)).astype(BF16)
+            out_here[k] = total[k * count : (k + 1) * count].astype(BF16)
             leave(k).start()
         projected_ref[...] = (part_ref[...] + received_ref[:, half:].astype(F32)).astype(BF16)
         for k in range(windows):

time: 136 us -> 134 us (0.985)
  Pallas kernels: 15 us -> 13 us
where the time goes in v12:
time: 134 us; the launch traced here: 133 us
  starting transfers between devices  53.5 us (40%)
  waiting for transfers between devices  35.6 us (27%)
  blocking collectives  19.3 us (14%)
  Pallas kernels  13 us (10%)
  local copies, waits for them, and re-layouts  8.81 us (7%)
  other arithmetic  1.86 us (1%)
    ppermute x2, starting transfers between devices, swap(): return lax.ppermute(array, 'c', [(0, 1), (1, 0)])  18.5 us
    ppermute x6, starting transfers between devices, along_x(): return lax.ppermute(array, 'x', [(i, (i + step) % NX) for i in range(NX)])  16.3 us
    all_to_all x1, waiting for transfers between devices, reduce(): out = lax.all_to_all(rows.reshape(size, -1, rows.shape[1]), axis, 0, 0)  15.6 us
    all_to_all x1, starting transfers between devices, gather(): lax.all_to_all(jnp.broadcast_to(rows[None], (size, *rows.shape)), axis, 0...  12 us
    ppermute x6, waiting for transfers between devices, along_x(): return lax.ppermute(array, 'x', [(i, (i + step) % NX) for i in range(NX)])  11.1 us
    all_to_all x1, blocking collectives, body(): rows = lax.all_to_all(rows, 'y', 0, 0).reshape(-1, out_grad.shape[1])  9.74 us
    all_to_all x1, blocking collectives, reduce(): out = lax.all_to_all(rows.reshape(size, -1, rows.shape[1]), axis, 0, 0)  9.6 us
    unnamed x22, local copies, waits for them, and re-layouts  7.89 us
  transfers between devices with their start and end apart: 10, of which 5 were waited for; matrix products, arithmetic and copies ran while one was open for 2% of the time, Pallas kernels for 2%

profile of v12, /device:TPU:1, one launch (start us, length us, event | category | flops | bytes accessed | tf_op | source)
XLA Modules:
  0.0 133.0 jit_solution(6670415015269616279)
XLA Ops:
  0.7 1.3 copy-done
  2.0 0.9 copy-done.1
  2.9 0.7 copy-done.3
  3.6 0.7 copy-done.4
  4.3 1.3 copy-done.5
  5.6 2.0 %shard_map.76 = (bf16[128,2304]{1,0:T(8,128)(2,1)S(1)}, bf16[128,2816]{1,0:T(8,128)(2,1)S(1)}, bf16[8,6,512]{2,1,0:T(8,128)(2,1)S(1)}) custom-call(s32[3]{0:T(128)S(1)} %pad_add_fusion.place_ref, f32[1152]{0:T(1024)S(1)} %copy-done.3, bf16[128,4608]{1,0:T(8,128)(2,1)S(1)} %copy-done, bf16[768,768]{1,0:T(8,128)(2,1)S(1)} %copy-done.5, ...), custom_call_target="tpu_custom_call" | custom-call | flops 905969664 | bytes 3538944 | tf_op jit(solution)/shard_map/pallas_call | solution.py:116
  7.6 12.4 %collective-permute-start = (bf16[128,2816]{1,0:T(8,128)(2,1)S(1)}, bf16[128,2816]{1,0:T(8,128)(2,1)S(1)}, u32[]{:S(2)}, u32[]{:S(2)}) collective-permute-start(bf16[128,2816]{1,0:T(8,128)(2,1)S(1)} %get-tuple-element.30), channel_id=1, source_target_pairs={{0,1},{1,0},{2,3},{3,2},{4,5},{5,4},{6,7},{7,6},{8,9},{9,8},{10,11... | collective-permute-start | bytes 2162696 | tf_op jit(solution)/shard_map/ppermute | solution.py:33
  20.0 9.7 %all_to_all.20 = bf16[8,6,512]{2,1,0:T(8,128)(2,1)S(1)} all-to-all(bf16[8,6,512]{2,1,0:T(8,128)(2,1)S(1)} %get-tuple-element.31), channel_id=1, replica_groups=mesh['z'=12,'y'=8,'x'=4,'c'=2] {'y'}, dimensions={0} | all-to-all | bytes 98304 | tf_op jit(solution)/shard_map/all_to_all | solution.py:286
  29.8 2.3 %shard_map.77 = (bf16[576,512]{1,0:T(8,128)(2,1)S(1)}, bf16[576,512]{1,0:T(8,128)(2,1)}, bf16[576,512]{1,0:T(8,128)(2,1)S(1)}, bf16[576,512]{1,0:T(8,128)(2,1)S(1)}) custom-call(s32[3]{0:T(128)S(1)} %pad_add_fusion.place_ref, bf16[128,2304]{1,0:T(8,128)(2,1)S(1)} %get-tuple-element.29.mine_ref, bf16[128,512]{1,0:T(8,128)(2,1)S(1)} %copy-done.2, ...), custom_call_target="tpu_custom_call" | custom-call | flops 603979776 | bytes 4718592 | tf_op jit(solution)/shard_map/pallas_call | solution.py:60
  32.2 0.8 copy-done.9
  33.0 1.9 %collective-permute-start.1 = (bf16[576,512]{1,0:T(8,128)(2,1)}, bf16[576,512]{1,0:T(8,128)(2,1)S(1)}, u32[]{:S(2)}, u32[]{:S(2)}) collective-permute-start(bf16[576,512]{1,0:T(8,128)(2,1)} %get-tuple-element.39), channel_id=1, source_target_pairs={{0,2},{2,4},{4,6},{6,0},{1,3},{3,5},{5,7},{7,1},{8,10},{10,12},{12... | collective-permute-start | bytes 1769480 | tf_op jit(solution)/shard_map/ppermute | solution.py:37
  34.9 1.9 %collective-permute-start.2 = (bf16[576,512]{1,0:T(8,128)(2,1)S(1)}, bf16[576,512]{1,0:T(8,128)(2,1)}, u32[]{:S(2)}, u32[]{:S(2)}) collective-permute-start(bf16[576,512]{1,0:T(8,128)(2,1)S(1)} %get-tuple-element.40), channel_id=1, source_target_pairs={{0,4},{2,6},{4,0},{6,2},{1,5},{3,7},{5,1},{7,3},{8,12},{10,14},{12... | collective-permute-start | bytes 1769480 | tf_op jit(solution)/shard_map/ppermute | solution.py:37
  36.8 4.6 %collective-permute-start.3 = (bf16[576,512]{1,0:T(8,128)(2,1)S(1)}, bf16[576,512]{1,0:T(8,128)(2,1)}, u32[]{:S(2)}, u32[]{:S(2)}) collective-permute-start(bf16[576,512]{1,0:T(8,128)(2,1)S(1)} %get-tuple-element.41), channel_id=1, source_target_pairs={{0,6},{2,0},{4,2},{6,4},{1,7},{3,1},{5,3},{7,5},{8,14},{10,8},{12,... | collective-permute-start | bytes 1769480 | tf_op jit(solution)/shard_map/ppermute | solution.py:37
  41.4 0.9 broadcast_in_dim.2
  42.3 12.0 %all-to-all-start.1 = ((bf16[12,48,512]{2,1,0:T(8,128)(2,1)}), bf16[12,48,512]{2,1,0:T(8,128)(2,1)S(1)}, u32[]{:S(2)}, u32[]{:S(2)}) async-start(bf16[12,48,512]{2,1,0:T(8,128)(2,1)} %broadcast_in_dim.2), calls=%async_computation.1 | async-start | bytes 1179648 | tf_op jit(solution)/shard_map/all_to_all | solution.py:41
  54.3 8.2 %collective-permute-done.1.refs_1_ = bf16[576,512]{1,0:T(8,128)(2,1)S(1)} collective-permute-done((bf16[576,512]{1,0:T(8,128)(2,1)}, bf16[576,512]{1,0:T(8,128)(2,1)S(1)}, u32[]{:S(2)}, u32[]{:S(2)}) %collective-permute-start.1) | collective-permute-done | bytes 589856 | tf_op jit(solution)/shard_map/ppermute | solution.py:37
  62.5 2.9 %collective-permute-done.3.refs_3_ = bf16[576,512]{1,0:T(8,128)(2,1)} collective-permute-done((bf16[576,512]{1,0:T(8,128)(2,1)S(1)}, bf16[576,512]{1,0:T(8,128)(2,1)}, u32[]{:S(2)}, u32[]{:S(2)}) %collective-permute-start.3) | collective-permute-done | bytes 589856 | tf_op jit(solution)/shard_map/ppermute | solution.py:37
  65.4 1.1 copy-done.10
  66.5 2.9 %shard_map.78 = bf16[576,512]{1,0:T(8,128)(2,1)} custom-call(s32[3]{0:T(128)S(1)} %pad_add_fusion.place_ref, bf16[576,512]{1,0:T(8,128)(2,1)S(1)} %copy-done.10, bf16[576,512]{1,0:T(8,128)(2,1)S(1)} %collective-permute-done.1.refs_1_, bf16[576,512]{1,0:T(8,128)(2,1)} %collective-permute-done.2.refs_2_, bf16[576,512]{1,0:T(8,128)(2,1)} %collective-permute-done.3.refs_3_), custom_call_target="tpu_custom_call" | custom-call | flops 99999997952 | bytes 1179648 | tf_op jit(solution)/shard_map/pallas_call | solution.py:60
  69.4 7.7 %all-to-all-done.1 = bf16[12,48,512]{2,1,0:T(8,128)(2,1)S(1)} async-done(((bf16[12,48,512]{2,1,0:T(8,128)(2,1)}), bf16[12,48,512]{2,1,0:T(8,128)(2,1)S(1)}, u32[]{:S(2)}, u32[]{:S(2)}) %all-to-all-start.1) | async-done | bytes 589856 | tf_op jit(solution)/shard_map/all_to_all | solution.py:41
  77.1 6.7 %all-to-all-start.2 = ((bf16[12,48,512]{2,1,0:T(8,128)(2,1)}), bf16[12,48,512]{2,1,0:T(8,128)(2,1)}, u32[]{:S(2)}, u32[]{:S(2)}) async-start(bf16[12,48,512]{2,1,0:T(8,128)(2,1)} %bitcast.4), calls=%async_computation.2 | async-start | bytes 1179648 | tf_op jit(solution)/shard_map/all_to_all | solution.py:46
  83.8 1.9 %collective-permute-start.6 = (bf16[576,512]{1,0:T(8,128)(2,1)S(1)}, bf16[576,512]{1,0:T(8,128)(2,1)S(1)}, u32[]{:S(2)}, u32[]{:S(2)}) collective-permute-start(bf16[576,512]{1,0:T(8,128)(2,1)S(1)} %bitcast.5), channel_id=1, source_target_pairs={{0,6},{2,0},{4,2},{6,4},{1,7},{3,1},{5,3},{7,5},{8,14},{10,8},{12,... | collective-permute-start | bytes 1769480 | tf_op jit(solution)/shard_map/ppermute | solution.py:37
  85.7 4.0 %collective-permute-start.5 = (bf16[576,512]{1,0:T(8,128)(2,1)S(1)}, bf16[576,512]{1,0:T(8,128)(2,1)S(1)}, u32[]{:S(2)}, u32[]{:S(2)}) collective-permute-start(bf16[576,512]{1,0:T(8,128)(2,1)S(1)} %bitcast.6), channel_id=1, source_target_pairs={{0,4},{2,6},{4,0},{6,2},{1,5},{3,7},{5,1},{7,3},{8,12},{10,14},{12... | collective-permute-start | bytes 1769480 | tf_op jit(solution)/shard_map/ppermute | solution.py:37
  89.8 1.9 %collective-permute-start.4 = (bf16[576,512]{1,0:T(8,128)(2,1)S(1)}, bf16[576,512]{1,0:T(8,128)(2,1)S(1)}, u32[]{:S(2)}, u32[]{:S(2)}) collective-permute-start(bf16[576,512]{1,0:T(8,128)(2,1)S(1)} %bitcast.7), channel_id=1, source_target_pairs={{0,2},{2,4},{4,6},{6,0},{1,3},{3,5},{5,7},{7,1},{8,10},{10,12},{12... | collective-permute-start | bytes 1769480 | tf_op jit(solution)/shard_map/ppermute | solution.py:37
  91.7 15.6 %all-to-all-done.2 = bf16[12,48,512]{2,1,0:T(8,128)(2,1)} async-done(((bf16[12,48,512]{2,1,0:T(8,128)(2,1)}), bf16[12,48,512]{2,1,0:T(8,128)(2,1)}, u32[]{:S(2)}, u32[]{:S(2)}) %all-to-all-start.2) | async-done | bytes 589856 | tf_op jit(solution)/shard_map/all_to_all | solution.py:46
  107.3 1.2 reduce_sum.21
  108.5 9.6 %all_to_all.21 = bf16[8,6,512]{2,1,0:T(8,128)(2,1)S(1)} all-to-all(bf16[8,6,512]{2,1,0:T(8,128)(2,1)S(1)} %reshape.22), channel_id=1, replica_groups=mesh['z'=12,'y'=8,'x'=4,'c'=2] {'y'}, dimensions={0} | all-to-all | bytes 98304 | tf_op jit(solution)/shard_map/all_to_all | solution.py:46
  118.2 1.1 copy-done.8
  119.3 2.1 %shard_map.79 = (bf16[128,2816]{1,0:T(8,128)(2,1)S(1)}, f32[128,512]{1,0:T(8,128)S(1)}, bf16[128,2304]{1,0:T(8,128)(2,1)S(1)}) custom-call(s32[3]{0:T(128)S(1)} %pad_add_fusion.place_ref, bf16[128,2304]{1,0:T(8,128)(2,1)S(1)} %copy-done.8, bf16[128,512]{1,0:T(8,128)(2,1)S(1)} %copy-done.2, bf16[128,2816]{1,0:T(8,128)(2,1)S(1)} %collective-permute-done.theirs_ref, ...), custom_call_target="tpu_custom_call" | custom-call | flops 1207959552 | bytes 3145728 | tf_op jit(solution)/shard_map/pallas_call | solution.py:60
  121.4 6.1 %collective-permute-start.7 = (bf16[128,2816]{1,0:T(8,128)(2,1)S(1)}, bf16[128,2816]{1,0:T(8,128)(2,1)S(1)}, u32[]{:S(2)}, u32[]{:S(2)}) collective-permute-start(bf16[128,2816]{1,0:T(8,128)(2,1)S(1)} %get-tuple-element.51), channel_id=1, source_target_pairs={{0,1},{1,0},{2,3},{3,2},{4,5},{5,4},{6,7},{7,6},{8,9},{9,8},{10,11... | collective-permute-start | bytes 2162696 | tf_op jit(solution)/shard_map/ppermute | solution.py:33
  128.1 1.2 collective-permute-done.7.received_ref
  129.3 3.6 %shard_map.80 = (bf16[128,512]{1,0:T(8,128)(2,1)}, bf16[128,4608]{1,0:T(8,128)(2,1)}) custom-call(s32[3]{0:T(128)S(1)} %pad_add_fusion.place_ref, f32[128,512]{1,0:T(8,128)S(1)} %get-tuple-element.49.part_ref, bf16[128,2304]{1,0:T(8,128)(2,1)S(1)} %get-tuple-element.50.columns_ref, bf16[128,2816]{1,0:T(8,128)(2,1)S(1)} %collective-permute-done.7.received_ref, ...), custom_call_target="tpu_custom_call" | custom-call | flops 905969664 | bytes 2359296 | tf_op jit(solution)/shard_map/pallas_call | solution.py:258
  (24 shorter events, 0.8 us)
Async XLA Ops:
  0.7 1.3 copy-start
  2.0 0.9 copy-start.1
  2.9 0.7 copy-start.3
  3.6 0.7 copy-start.4
  4.3 1.3 copy-start.5
  5.6 24.2 %copy-start.2 = (bf16[128,512]{1,0:T(8,128)(2,1)S(1)}, bf16[128,512]{1,0:T(8,128)(2,1)}, u32[]{:S(2)}) copy-start(bf16[128,512]{1,0:T(8,128)(2,1)} %grad_ref.5) | copy-start | bytes 393220
  7.6 24.6 %copy-start.7 = (bf16[128,2304]{1,0:T(8,128)(2,1)}, bf16[128,2304]{1,0:T(8,128)(2,1)S(1)}, u32[]{:S(2)}) copy-start(bf16[128,2304]{1,0:T(8,128)(2,1)S(1)} %get-tuple-element.29.mine_ref) | copy-start | bytes 1769476
  7.6 22.2 %collective-permute-start = (bf16[128,2816]{1,0:T(8,128)(2,1)S(1)}, bf16[128,2816]{1,0:T(8,128)(2,1)S(1)}, u32[]{:S(2)}, u32[]{:S(2)}) collective-permute-start(bf16[128,2816]{1,0:T(8,128)(2,1)S(1)} %get-tuple-element.30), channel_id=1, source_target_pairs={{0,1},{1,0},{2,3},{3,2},{4,5},{5,4},{6,7},{7,6},{8,9},{9,8},{10,11... | collective-permute-start | bytes 2162696 | tf_op jit(solution)/shard_map/ppermute | solution.py:33
  32.2 0.8 copy-start.9
  33.0 29.5 %collective-permute-start.1 = (bf16[576,512]{1,0:T(8,128)(2,1)}, bf16[576,512]{1,0:T(8,128)(2,1)S(1)}, u32[]{:S(2)}, u32[]{:S(2)}) collective-permute-start(bf16[576,512]{1,0:T(8,128)(2,1)} %get-tuple-element.39), channel_id=1, source_target_pairs={{0,2},{2,4},{4,6},{6,0},{1,3},{3,5},{5,7},{7,1},{8,10},{10,12},{12... | collective-permute-start | bytes 1769480 | tf_op jit(solution)/shard_map/ppermute | solution.py:37
  34.9 27.6 %collective-permute-start.2 = (bf16[576,512]{1,0:T(8,128)(2,1)S(1)}, bf16[576,512]{1,0:T(8,128)(2,1)}, u32[]{:S(2)}, u32[]{:S(2)}) collective-permute-start(bf16[576,512]{1,0:T(8,128)(2,1)S(1)} %get-tuple-element.40), channel_id=1, source_target_pairs={{0,4},{2,6},{4,0},{6,2},{1,5},{3,7},{5,1},{7,3},{8,12},{10,14},{12... | collective-permute-start | bytes 1769480 | tf_op jit(solution)/shard_map/ppermute | solution.py:37
  36.8 28.6 %collective-permute-start.3 = (bf16[576,512]{1,0:T(8,128)(2,1)S(1)}, bf16[576,512]{1,0:T(8,128)(2,1)}, u32[]{:S(2)}, u32[]{:S(2)}) collective-permute-start(bf16[576,512]{1,0:T(8,128)(2,1)S(1)} %get-tuple-element.41), channel_id=1, source_target_pairs={{0,6},{2,0},{4,2},{6,4},{1,7},{3,1},{5,3},{7,5},{8,14},{10,8},{12,... | collective-permute-start | bytes 1769480 | tf_op jit(solution)/shard_map/ppermute | solution.py:37
  42.3 34.8 %all-to-all-start.1 = ((bf16[12,48,512]{2,1,0:T(8,128)(2,1)}), bf16[12,48,512]{2,1,0:T(8,128)(2,1)S(1)}, u32[]{:S(2)}, u32[]{:S(2)}) async-start(bf16[12,48,512]{2,1,0:T(8,128)(2,1)} %broadcast_in_dim.2), calls=%async_computation.1 | async-start | bytes 1179648 | tf_op jit(solution)/shard_map/all_to_all | solution.py:41
  65.4 1.1 copy-start.10
  77.1 30.2 %all-to-all-start.2 = ((bf16[12,48,512]{2,1,0:T(8,128)(2,1)}), bf16[12,48,512]{2,1,0:T(8,128)(2,1)}, u32[]{:S(2)}, u32[]{:S(2)}) async-start(bf16[12,48,512]{2,1,0:T(8,128)(2,1)} %bitcast.4), calls=%async_computation.2 | async-start | bytes 1179648 | tf_op jit(solution)/shard_map/all_to_all | solution.py:46
  83.8 34.3 %collective-permute-start.6 = (bf16[576,512]{1,0:T(8,128)(2,1)S(1)}, bf16[576,512]{1,0:T(8,128)(2,1)S(1)}, u32[]{:S(2)}, u32[]{:S(2)}) collective-permute-start(bf16[576,512]{1,0:T(8,128)(2,1)S(1)} %bitcast.5), channel_id=1, source_target_pairs={{0,6},{2,0},{4,2},{6,4},{1,7},{3,1},{5,3},{7,5},{8,14},{10,8},{12,... | collective-permute-start | bytes 1769480 | tf_op jit(solution)/shard_map/ppermute | solution.py:37
  85.7 32.4 %collective-permute-start.5 = (bf16[576,512]{1,0:T(8,128)(2,1)S(1)}, bf16[576,512]{1,0:T(8,128)(2,1)S(1)}, u32[]{:S(2)}, u32[]{:S(2)}) collective-permute-start(bf16[576,512]{1,0:T(8,128)(2,1)S(1)} %bitcast.6), channel_id=1, source_target_pairs={{0,4},{2,6},{4,0},{6,2},{1,5},{3,7},{5,1},{7,3},{8,12},{10,14},{12... | collective-permute-start | bytes 1769480 | tf_op jit(solution)/shard_map/ppermute | solution.py:37
  89.8 28.4 %collective-permute-start.4 = (bf16[576,512]{1,0:T(8,128)(2,1)S(1)}, bf16[576,512]{1,0:T(8,128)(2,1)S(1)}, u32[]{:S(2)}, u32[]{:S(2)}) collective-permute-start(bf16[576,512]{1,0:T(8,128)(2,1)S(1)} %bitcast.7), channel_id=1, source_target_pairs={{0,2},{2,4},{4,6},{6,0},{1,3},{3,5},{5,7},{7,1},{8,10},{10,12},{12... | collective-permute-start | bytes 1769480 | tf_op jit(solution)/shard_map/ppermute | solution.py:37
  118.1 11.2 %copy-start.6 = (bf16[768,768]{1,0:T(8,128)(2,1)S(1)}, bf16[768,768]{1,0:T(8,128)(2,1)}, u32[]{:S(2)}) copy-start(bf16[768,768]{1,0:T(8,128)(2,1)} %constant.31.clone.order_ref) | copy-start | bytes 3538948
  118.1 1.2 copy-start.8
  121.4 7.9 %collective-permute-start.7 = (bf16[128,2816]{1,0:T(8,128)(2,1)S(1)}, bf16[128,2816]{1,0:T(8,128)(2,1)S(1)}, u32[]{:S(2)}, u32[]{:S(2)}) collective-permute-start(bf16[128,2816]{1,0:T(8,128)(2,1)S(1)} %get-tuple-element.51), channel_id=1, source_target_pairs={{0,1},{1,0},{2,3},{3,2},{4,5},{5,4},{6,7},{7,6},{8,9},{9,8},{10,11... | collective-permute-start | bytes 2162696 | tf_op jit(solution)/shard_map/ppermute | solution.py:33

commit v13 on v12

--- a/solution.py
+++ b/solution.py
@@ -90,7 +90,20 @@
         mine_ref,
         send_ref,
         rows_ref,
+        tokens_here,
+        order_here,
+        sems,
+        order_sem,
     ):
+        fetches = [pltpu.make_async_copy(order_ref, order_here, order_sem)]
+        for k in range(windows):
+            at = pl.ds(k * window, window)
+            fetches.append(
+                pltpu.make_async_copy(tokens_ref.at[:, at], tokens_here.at[k], sems.at[k])
+            )
+        for fetch in fetches:
+            fetch.start()
+
         first_row = place_ref[2] * rows
         start = lax.div(first_row, BLOCK_ROWS)
         row = first_row + lax.broadcasted_iota(jnp.int32, (rows, cols), 0)
@@ -102,16 +115,17 @@
             rows_ref[k] = scaled
         send_ref[:, half:] = grad_ref[...]
 
-        stacked = jnp.concatenate(
-            [tokens_ref[:, k * window : (k + 1) * window] for k in range(windows)], axis=0
-        )
+        for fetch in fetches:
+            fetch.wait()
+        stacked = tokens_here[...].reshape(windows * count, window)
         for core, out_ref in ((place_ref[0], mine_ref), (1 - place_ref[0], send_ref)):
-            columns = order_ref[:, pl.ds(pl.multiple_of(core * part, part), part)]
+            columns = order_here[:, pl.ds(pl.multiple_of(core * part, part), part)]
             chosen = dot(stacked, columns, (1, 0)).astype(BF16)
             for k in range(windows):
                 out_ref[:, k * part : (k + 1) * part] = chosen[k * count : (k + 1) * count]
 
     smem = pl.BlockSpec(memory_space=pltpu.SMEM)
+    hbm = pl.BlockSpec(memory_space=pltpu.HBM)
     vmem = pl.BlockSpec(memory_space=pltpu.VMEM)
     return pl.pallas_call(
         kernel,
@@ -120,9 +134,15 @@
             jax.ShapeDtypeStruct((count, half + cols), BF16),
             jax.ShapeDtypeStruct((NY, rows, cols), BF16),
         ],
-        in_specs=[smem, smem, *[vmem] * 4],
+        in_specs=[smem, smem, hbm, hbm, vmem, vmem],
         out_specs=[vmem] * 3,
-        compiler_params=PARAMS,
+        scratch_shapes=[
+            pltpu.VMEM((windows, count, window), BF16),
+            pltpu.VMEM(order.shape, BF16),
+            pltpu.SemaphoreType.DMA((windows,)),
+            pltpu.SemaphoreType.DMA,
+        ],
+        compiler_params=pltpu.CompilerParams(vmem_limit_bytes=56 * 2**20),
         cost_estimate=pl.CostEstimate(
             flops=2 * tokens.size * window, bytes_accessed=6 * tokens.size, transcendentals=0
         ),

time: 134 us -> 134 us (level)
  local copies, waits for them, and re-layouts: 8.81 us -> 5.01 us
  Pallas kernels: 13 us -> 16 us
    unnamed x22 -> x14, local copies, waits for them, and re-layouts: 7.89 us -> 4.1 us
    pallas_call x1, Pallas kernels: 2.01 us -> 5.01 us  [sort_columns(): pl.pallas_call(kernel, out_shape=[jax.ShapeDtypeStruct((count, half), BF1...]
where the time goes in v13:
time: 134 us; the launch traced here: 133 us
  starting transfers between devices  52.8 us (39%)
  waiting for transfers between devices  35.6 us (27%)
  blocking collectives  20.2 us (15%)
  Pallas kernels  16 us (12%)
  local copies, waits for them, and re-layouts  5.01 us (4%)
  other arithmetic  2.36 us (2%)
    ppermute x2, starting transfers between devices, swap(): return lax.ppermute(array, 'c', [(0, 1), (1, 0)])  18.5 us
    ppermute x6, starting transfers between devices, along_x(): return lax.ppermute(array, 'x', [(i, (i + step) % NX) for i in range(NX)])  16.2 us
    all_to_all x1, waiting for transfers between devices, reduce(): out = lax.all_to_all(rows.reshape(size, -1, rows.shape[1]), axis, 0, 0)  15.6 us
    ppermute x6, waiting for transfers between devices, along_x(): return lax.ppermute(array, 'x', [(i, (i + step) % NX) for i in range(NX)])  11.8 us
    all_to_all x1, starting transfers between devices, gather(): lax.all_to_all(jnp.broadcast_to(rows[None], (size, *rows.shape)), axis, 0...  11.3 us
    all_to_all x1, blocking collectives, body(): rows = lax.all_to_all(rows, 'y', 0, 0).reshape(-1, out_grad.shape[1])  10.6 us
    all_to_all x1, blocking collectives, reduce(): out = lax.all_to_all(rows.reshape(size, -1, rows.shape[1]), axis, 0, 0)  9.6 us
    pallas_call x3, Pallas kernels, call(): pl.pallas_call(kernel, out_shape=outs, grid_spec=pltpu.PrefetchScalarGrid...  7.37 us
  transfers between devices with their start and end apart: 10, of which 5 were waited for; matrix products, arithmetic and copies ran while one was open for 2% of the time, Pallas kernels for 2%

profile of v13, /device:TPU:1, one launch (start us, length us, event | category | flops | bytes accessed | tf_op | source)
XLA Modules:
  0.0 132.9 jit_solution(12049797922890679132)
XLA Ops:
  0.6 0.6 pad_add_fusion.place_ref
  1.2 5.0 %shard_map.76 = (bf16[128,2304]{1,0:T(8,128)(2,1)}, bf16[128,2816]{1,0:T(8,128)(2,1)}, bf16[8,6,512]{2,1,0:T(8,128)(2,1)}) custom-call(s32[3]{0:T(128)} %pad_add_fusion.place_ref, f32[1152]{0:T(1024)} %scales_ref.1, bf16[128,4608]{1,0:T(8,128)(2,1)} %tokens_ref.1, bf16[768,768]{1,0:T(8,128)(2,1)} %constant.31.clone.order_ref, bf16[128,512]{1,0:T(8,128)(2,1)} %grad_ref.5, ...), custom_call_target="tpu_custom_call" | custom-call | flops 905969664 | bytes 3538944 | tf_op jit(solution)/shard_map/pallas_call | solution.py:130
  6.2 12.4 %collective-permute-start = (bf16[128,2816]{1,0:T(8,128)(2,1)}, bf16[128,2816]{1,0:T(8,128)(2,1)S(1)}, u32[]{:S(2)}, u32[]{:S(2)}) collective-permute-start(bf16[128,2816]{1,0:T(8,128)(2,1)} %get-tuple-element.30), channel_id=1, source_target_pairs={{0,1},{1,0},{2,3},{3,2},{4,5},{5,4},{6,7},{7,6},{8,9},{9,8},{10,11... | collective-permute-start | bytes 2162696 | tf_op jit(solution)/shard_map/ppermute | solution.py:33
  18.7 10.6 %all_to_all.20 = bf16[8,6,512]{2,1,0:T(8,128)(2,1)S(1)} all-to-all(bf16[8,6,512]{2,1,0:T(8,128)(2,1)} %get-tuple-element.31), channel_id=1, replica_groups=mesh['z'=12,'y'=8,'x'=4,'c'=2] {'y'}, dimensions={0} | all-to-all | bytes 98304 | tf_op jit(solution)/shard_map/all_to_all | solution.py:306
  29.4 1.1 copy-done.3
  30.4 2.3 %shard_map.77 = (bf16[576,512]{1,0:T(8,128)(2,1)S(1)}, bf16[576,512]{1,0:T(8,128)(2,1)}, bf16[576,512]{1,0:T(8,128)(2,1)S(1)}, bf16[576,512]{1,0:T(8,128)(2,1)S(1)}) custom-call(s32[3]{0:T(128)S(1)} %copy-done, bf16[128,2304]{1,0:T(8,128)(2,1)S(1)} %copy-done.3, bf16[128,512]{1,0:T(8,128)(2,1)S(1)} %copy-done.1, ...), custom_call_target="tpu_custom_call" | custom-call | flops 603979776 | bytes 4718592 | tf_op jit(solution)/shard_map/pallas_call | solution.py:60
  32.8 0.8 copy-done.5
  33.6 1.9 %collective-permute-start.1 = (bf16[576,512]{1,0:T(8,128)(2,1)}, bf16[576,512]{1,0:T(8,128)(2,1)S(1)}, u32[]{:S(2)}, u32[]{:S(2)}) collective-permute-start(bf16[576,512]{1,0:T(8,128)(2,1)} %get-tuple-element.39), channel_id=1, source_target_pairs={{0,2},{2,4},{4,6},{6,0},{1,3},{3,5},{5,7},{7,1},{8,10},{10,12},{12... | collective-permute-start | bytes 1769480 | tf_op jit(solution)/shard_map/ppermute | solution.py:37
  35.5 1.9 %collective-permute-start.2 = (bf16[576,512]{1,0:T(8,128)(2,1)S(1)}, bf16[576,512]{1,0:T(8,128)(2,1)}, u32[]{:S(2)}, u32[]{:S(2)}) collective-permute-start(bf16[576,512]{1,0:T(8,128)(2,1)S(1)} %get-tuple-element.40), channel_id=1, source_target_pairs={{0,4},{2,6},{4,0},{6,2},{1,5},{3,7},{5,1},{7,3},{8,12},{10,14},{12... | collective-permute-start | bytes 1769480 | tf_op jit(solution)/shard_map/ppermute | solution.py:37
  37.4 4.6 %collective-permute-start.3 = (bf16[576,512]{1,0:T(8,128)(2,1)S(1)}, bf16[576,512]{1,0:T(8,128)(2,1)}, u32[]{:S(2)}, u32[]{:S(2)}) collective-permute-start(bf16[576,512]{1,0:T(8,128)(2,1)S(1)} %get-tuple-element.41), channel_id=1, source_target_pairs={{0,6},{2,0},{4,2},{6,4},{1,7},{3,1},{5,3},{7,5},{8,14},{10,8},{12,... | collective-permute-start | bytes 1769480 | tf_op jit(solution)/shard_map/ppermute | solution.py:37
  42.0 0.9 broadcast_in_dim.2
  42.9 11.3 %all-to-all-start.1 = ((bf16[12,48,512]{2,1,0:T(8,128)(2,1)}), bf16[12,48,512]{2,1,0:T(8,128)(2,1)S(1)}, u32[]{:S(2)}, u32[]{:S(2)}) async-start(bf16[12,48,512]{2,1,0:T(8,128)(2,1)} %broadcast_in_dim.2), calls=%async_computation.1 | async-start | bytes 1179648 | tf_op jit(solution)/shard_map/all_to_all | solution.py:41
  54.2 8.9 %collective-permute-done.1.refs_1_ = bf16[576,512]{1,0:T(8,128)(2,1)S(1)} collective-permute-done((bf16[576,512]{1,0:T(8,128)(2,1)}, bf16[576,512]{1,0:T(8,128)(2,1)S(1)}, u32[]{:S(2)}, u32[]{:S(2)}) %collective-permute-start.1) | collective-permute-done | bytes 589856 | tf_op jit(solution)/shard_map/ppermute | solution.py:37
  63.1 2.9 %collective-permute-done.3.refs_3_ = bf16[576,512]{1,0:T(8,128)(2,1)} collective-permute-done((bf16[576,512]{1,0:T(8,128)(2,1)S(1)}, bf16[576,512]{1,0:T(8,128)(2,1)}, u32[]{:S(2)}, u32[]{:S(2)}) %collective-permute-start.3) | collective-permute-done | bytes 589856 | tf_op jit(solution)/shard_map/ppermute | solution.py:37
  66.1 1.1 copy-done.6
  67.1 2.9 %shard_map.78 = bf16[576,512]{1,0:T(8,128)(2,1)} custom-call(s32[3]{0:T(128)S(1)} %copy-done, bf16[576,512]{1,0:T(8,128)(2,1)S(1)} %copy-done.6, bf16[576,512]{1,0:T(8,128)(2,1)S(1)} %collective-permute-done.1.refs_1_, bf16[576,512]{1,0:T(8,128)(2,1)} %collective-permute-done.2.refs_2_, bf16[576,512]{1,0:T(8,128)(2,1)} %collective-permute-done.3.refs_3_), custom_call_target="tpu_custom_call" | custom-call | flops 99999997952 | bytes 1179648 | tf_op jit(solution)/shard_map/pallas_call | solution.py:60
  70.0 7.0 %all-to-all-done.1 = bf16[12,48,512]{2,1,0:T(8,128)(2,1)S(1)} async-done(((bf16[12,48,512]{2,1,0:T(8,128)(2,1)}), bf16[12,48,512]{2,1,0:T(8,128)(2,1)S(1)}, u32[]{:S(2)}, u32[]{:S(2)}) %all-to-all-start.1) | async-done | bytes 589856 | tf_op jit(solution)/shard_map/all_to_all | solution.py:41
  77.0 6.7 %all-to-all-start.2 = ((bf16[12,48,512]{2,1,0:T(8,128)(2,1)}), bf16[12,48,512]{2,1,0:T(8,128)(2,1)}, u32[]{:S(2)}, u32[]{:S(2)}) async-start(bf16[12,48,512]{2,1,0:T(8,128)(2,1)} %bitcast.4), calls=%async_computation.2 | async-start | bytes 1179648 | tf_op jit(solution)/shard_map/all_to_all | solution.py:46
  83.8 1.9 %collective-permute-start.6 = (bf16[576,512]{1,0:T(8,128)(2,1)S(1)}, bf16[576,512]{1,0:T(8,128)(2,1)S(1)}, u32[]{:S(2)}, u32[]{:S(2)}) collective-permute-start(bf16[576,512]{1,0:T(8,128)(2,1)S(1)} %bitcast.5), channel_id=1, source_target_pairs={{0,6},{2,0},{4,2},{6,4},{1,7},{3,1},{5,3},{7,5},{8,14},{10,8},{12,... | collective-permute-start | bytes 1769480 | tf_op jit(solution)/shard_map/ppermute | solution.py:37
  85.7 4.0 %collective-permute-start.5 = (bf16[576,512]{1,0:T(8,128)(2,1)S(1)}, bf16[576,512]{1,0:T(8,128)(2,1)S(1)}, u32[]{:S(2)}, u32[]{:S(2)}) collective-permute-start(bf16[576,512]{1,0:T(8,128)(2,1)S(1)} %bitcast.6), channel_id=1, source_target_pairs={{0,4},{2,6},{4,0},{6,2},{1,5},{3,7},{5,1},{7,3},{8,12},{10,14},{12... | collective-permute-start | bytes 1769480 | tf_op jit(solution)/shard_map/ppermute | solution.py:37
  89.7 1.9 %collective-permute-start.4 = (bf16[576,512]{1,0:T(8,128)(2,1)S(1)}, bf16[576,512]{1,0:T(8,128)(2,1)S(1)}, u32[]{:S(2)}, u32[]{:S(2)}) collective-permute-start(bf16[576,512]{1,0:T(8,128)(2,1)S(1)} %bitcast.7), channel_id=1, source_target_pairs={{0,2},{2,4},{4,6},{6,0},{1,3},{3,5},{5,7},{7,1},{8,10},{10,12},{12... | collective-permute-start | bytes 1769480 | tf_op jit(solution)/shard_map/ppermute | solution.py:37
  91.6 15.6 %all-to-all-done.2 = bf16[12,48,512]{2,1,0:T(8,128)(2,1)} async-done(((bf16[12,48,512]{2,1,0:T(8,128)(2,1)}), bf16[12,48,512]{2,1,0:T(8,128)(2,1)}, u32[]{:S(2)}, u32[]{:S(2)}) %all-to-all-start.2) | async-done | bytes 589856 | tf_op jit(solution)/shard_map/all_to_all | solution.py:46
  107.2 1.2 reduce_sum.21
  108.4 9.6 %all_to_all.21 = bf16[8,6,512]{2,1,0:T(8,128)(2,1)S(1)} all-to-all(bf16[8,6,512]{2,1,0:T(8,128)(2,1)S(1)} %reshape.22), channel_id=1, replica_groups=mesh['z'=12,'y'=8,'x'=4,'c'=2] {'y'}, dimensions={0} | all-to-all | bytes 98304 | tf_op jit(solution)/shard_map/all_to_all | solution.py:46
  118.0 0.0 copy-start.2
  118.0 0.0 collective-permute-done.6.rest_3_
  118.1 1.1 copy-done.4
  119.2 2.1 %shard_map.79 = (bf16[128,2816]{1,0:T(8,128)(2,1)S(1)}, f32[128,512]{1,0:T(8,128)S(1)}, bf16[128,2304]{1,0:T(8,128)(2,1)S(1)}) custom-call(s32[3]{0:T(128)S(1)} %copy-done, bf16[128,2304]{1,0:T(8,128)(2,1)S(1)} %copy-done.4, bf16[128,512]{1,0:T(8,128)(2,1)S(1)} %copy-done.1, bf16[128,2816]{1,0:T(8,128)(2,1)S(1)} %collective-permute-done.theirs_ref, ...), custom_call_target="tpu_custom_call" | custom-call | flops 1207959552 | bytes 3145728 | tf_op jit(solution)/shard_map/pallas_call | solution.py:60
  121.3 6.1 %collective-permute-start.7 = (bf16[128,2816]{1,0:T(8,128)(2,1)S(1)}, bf16[128,2816]{1,0:T(8,128)(2,1)S(1)}, u32[]{:S(2)}, u32[]{:S(2)}) collective-permute-start(bf16[128,2816]{1,0:T(8,128)(2,1)S(1)} %get-tuple-element.51), channel_id=1, source_target_pairs={{0,1},{1,0},{2,3},{3,2},{4,5},{5,4},{6,7},{7,6},{8,9},{9,8},{10,11... | collective-permute-start | bytes 2162696 | tf_op jit(solution)/shard_map/ppermute | solution.py:33
  127.5 0.6 broadcast_multiply_fusion
  128.1 1.2 collective-permute-done.7.received_ref
  129.3 3.7 %shard_map.80 = (bf16[128,512]{1,0:T(8,128)(2,1)}, bf16[128,4608]{1,0:T(8,128)(2,1)}) custom-call(s32[3]{0:T(128)S(1)} %copy-done, f32[128,512]{1,0:T(8,128)S(1)} %get-tuple-element.49.part_ref, bf16[128,2304]{1,0:T(8,128)(2,1)S(1)} %get-tuple-element.50.columns_ref, bf16[128,2816]{1,0:T(8,128)(2,1)S(1)} %collective-permute-done.7.received_ref, ...), custom_call_target="tpu_custom_call" | custom-call | flops 905969664 | bytes 2359296 | tf_op jit(solution)/shard_map/pallas_call | solution.py:278
  (16 shorter events, 0.1 us)
Async XLA Ops:
  1.2 28.1 %copy-start = (s32[3]{0:T(128)S(1)}, s32[3]{0:T(128)}, u32[]{:S(2)}) copy-start(s32[3]{0:T(128)} %pad_add_fusion.place_ref) | copy-start | bytes 40
  1.2 28.1 %copy-start.1 = (bf16[128,512]{1,0:T(8,128)(2,1)S(1)}, bf16[128,512]{1,0:T(8,128)(2,1)}, u32[]{:S(2)}) copy-start(bf16[128,512]{1,0:T(8,128)(2,1)} %grad_ref.5) | copy-start | bytes 393220
  6.2 23.1 %collective-permute-start = (bf16[128,2816]{1,0:T(8,128)(2,1)}, bf16[128,2816]{1,0:T(8,128)(2,1)S(1)}, u32[]{:S(2)}, u32[]{:S(2)}) collective-permute-start(bf16[128,2816]{1,0:T(8,128)(2,1)} %get-tuple-element.30), channel_id=1, source_target_pairs={{0,1},{1,0},{2,3},{3,2},{4,5},{5,4},{6,7},{7,6},{8,9},{9,8},{10,11... | collective-permute-start | bytes 2162696 | tf_op jit(solution)/shard_map/ppermute | solution.py:33
  29.4 1.1 copy-start.3
  32.8 0.8 copy-start.5
  33.6 29.5 %collective-permute-start.1 = (bf16[576,512]{1,0:T(8,128)(2,1)}, bf16[576,512]{1,0:T(8,128)(2,1)S(1)}, u32[]{:S(2)}, u32[]{:S(2)}) collective-permute-start(bf16[576,512]{1,0:T(8,128)(2,1)} %get-tuple-element.39), channel_id=1, source_target_pairs={{0,2},{2,4},{4,6},{6,0},{1,3},{3,5},{5,7},{7,1},{8,10},{10,12},{12... | collective-permute-start | bytes 1769480 | tf_op jit(solution)/shard_map/ppermute | solution.py:37
  35.5 27.6 %collective-permute-start.2 = (bf16[576,512]{1,0:T(8,128)(2,1)S(1)}, bf16[576,512]{1,0:T(8,128)(2,1)}, u32[]{:S(2)}, u32[]{:S(2)}) collective-permute-start(bf16[576,512]{1,0:T(8,128)(2,1)S(1)} %get-tuple-element.40), channel_id=1, source_target_pairs={{0,4},{2,6},{4,0},{6,2},{1,5},{3,7},{5,1},{7,3},{8,12},{10,14},{12... | collective-permute-start | bytes 1769480 | tf_op jit(solution)/shard_map/ppermute | solution.py:37
  37.4 28.6 %collective-permute-start.3 = (bf16[576,512]{1,0:T(8,128)(2,1)S(1)}, bf16[576,512]{1,0:T(8,128)(2,1)}, u32[]{:S(2)}, u32[]{:S(2)}) collective-permute-start(bf16[576,512]{1,0:T(8,128)(2,1)S(1)} %get-tuple-element.41), channel_id=1, source_target_pairs={{0,6},{2,0},{4,2},{6,4},{1,7},{3,1},{5,3},{7,5},{8,14},{10,8},{12,... | collective-permute-start | bytes 1769480 | tf_op jit(solution)/shard_map/ppermute | solution.py:37
  42.9 34.2 %all-to-all-start.1 = ((bf16[12,48,512]{2,1,0:T(8,128)(2,1)}), bf16[12,48,512]{2,1,0:T(8,128)(2,1)S(1)}, u32[]{:S(2)}, u32[]{:S(2)}) async-start(bf16[12,48,512]{2,1,0:T(8,128)(2,1)} %broadcast_in_dim.2), calls=%async_computation.1 | async-start | bytes 1179648 | tf_op jit(solution)/shard_map/all_to_all | solution.py:41
  66.1 1.1 copy-start.6
  77.0 30.2 %all-to-all-start.2 = ((bf16[12,48,512]{2,1,0:T(8,128)(2,1)}), bf16[12,48,512]{2,1,0:T(8,128)(2,1)}, u32[]{:S(2)}, u32[]{:S(2)}) async-start(bf16[12,48,512]{2,1,0:T(8,128)(2,1)} %bitcast.4), calls=%async_computation.2 | async-start | bytes 1179648 | tf_op jit(solution)/shard_map/all_to_all | solution.py:46
  83.8 34.3 %collective-permute-start.6 = (bf16[576,512]{1,0:T(8,128)(2,1)S(1)}, bf16[576,512]{1,0:T(8,128)(2,1)S(1)}, u32[]{:S(2)}, u32[]{:S(2)}) collective-permute-start(bf16[576,512]{1,0:T(8,128)(2,1)S(1)} %bitcast.5), channel_id=1, source_target_pairs={{0,6},{2,0},{4,2},{6,4},{1,7},{3,1},{5,3},{7,5},{8,14},{10,8},{12,... | collective-permute-start | bytes 1769480 | tf_op jit(solution)/shard_map/ppermute | solution.py:37
  85.7 32.4 %collective-permute-start.5 = (bf16[576,512]{1,0:T(8,128)(2,1)S(1)}, bf16[576,512]{1,0:T(8,128)(2,1)S(1)}, u32[]{:S(2)}, u32[]{:S(2)}) collective-permute-start(bf16[576,512]{1,0:T(8,128)(2,1)S(1)} %bitcast.6), channel_id=1, source_target_pairs={{0,4},{2,6},{4,0},{6,2},{1,5},{3,7},{5,1},{7,3},{8,12},{10,14},{12... | collective-permute-start | bytes 1769480 | tf_op jit(solution)/shard_map/ppermute | solution.py:37
  89.7 28.4 %collective-permute-start.4 = (bf16[576,512]{1,0:T(8,128)(2,1)S(1)}, bf16[576,512]{1,0:T(8,128)(2,1)S(1)}, u32[]{:S(2)}, u32[]{:S(2)}) collective-permute-start(bf16[576,512]{1,0:T(8,128)(2,1)S(1)} %bitcast.7), channel_id=1, source_target_pairs={{0,2},{2,4},{4,6},{6,0},{1,3},{3,5},{5,7},{7,1},{8,10},{10,12},{12... | collective-permute-start | bytes 1769480 | tf_op jit(solution)/shard_map/ppermute | solution.py:37
  118.0 11.2 %copy-start.2 = (bf16[768,768]{1,0:T(8,128)(2,1)S(1)}, bf16[768,768]{1,0:T(8,128)(2,1)}, u32[]{:S(2)}) copy-start(bf16[768,768]{1,0:T(8,128)(2,1)} %constant.31.clone.order_ref) | copy-start | bytes 3538948
  118.1 1.2 copy-start.4
  121.3 7.9 %collective-permute-start.7 = (bf16[128,2816]{1,0:T(8,128)(2,1)S(1)}, bf16[128,2816]{1,0:T(8,128)(2,1)S(1)}, u32[]{:S(2)}, u32[]{:S(2)}) collective-permute-start(bf16[128,2816]{1,0:T(8,128)(2,1)S(1)} %get-tuple-element.51), channel_id=1, source_target_pairs={{0,1},{1,0},{2,3},{3,2},{4,5},{5,4},{6,7},{7,6},{8,9},{9,8},{10,11... | collective-permute-start | bytes 2162696 | tf_op jit(solution)/shard_map/ppermute | solution.py:33

commit v14 on v12

--- a/solution.py
+++ b/solution.py
@@ -14,7 +14,6 @@
 AXES = ("z", "y", "x", "c")
 BF16 = jnp.bfloat16
 F32 = jnp.float32
-LONG = 10**11
 PARAMS = pltpu.CompilerParams(vmem_limit_bytes=24 * 2**20)
 
 
@@ -207,15 +206,6 @@
     )
 
 
-def add_up(place, parts):
-    def kernel(place_ref, *refs):
-        *part_refs, out_ref = refs
-        out_ref[...] = sum(p[...].astype(F32) for p in part_refs).astype(BF16)
-
-    out = jax.ShapeDtypeStruct(parts[0].shape, BF16)
-    return call(kernel, [out], [whole(p.shape) for p in parts], [], LONG, (place, *parts))[0]
-
-
 def assemble(place, part, columns, received, order):
     count, half = columns.shape
     cols = part.shape[1]
@@ -290,7 +280,7 @@
     rows, *parts = lax.optimization_barrier((rows, *parts))
     parts = [parts[0], *(along_x(parts[step], step) for step in range(1, NX))]
     rows = gather(rows, "z", NZ)
-    total = add_up(place, parts)
+    total = sum(p.astype(F32) for p in parts).astype(BF16)
     total, rows = lax.optimization_barrier((total, rows))
     blocks = [rows, *(along_x(rows, step) for step in range(1, NX))]
 

time: 134 us -> 139 us (1.037)
  Pallas kernels: 13 us -> 9.3 us
  starting transfers between devices: 53.5 us -> 56.5 us
  waiting for transfers between devices: 35.6 us -> 38.1 us
    ppermute x6, waiting for transfers between devices: 11.1 us -> 24.5 us  [along_x(): return lax.ppermute(array, 'x', [(i, (i + step) % NX) for i in range(NX)])]
    all_to_all x1, waiting for transfers between devices: 7.7 us -> 0.01 us  [gather(): lax.all_to_all(jnp.broadcast_to(rows[None], (size, *rows.shape)), axis, 0...]
    ppermute x6, starting transfers between devices: 16.3 us -> 21.2 us  [along_x(): return lax.ppermute(array, 'x', [(i, (i + step) % NX) for i in range(NX)])]
    pallas_call x3 -> x2, Pallas kernels: 7.37 us -> 3.64 us  [call(): pl.pallas_call(kernel, out_shape=outs, grid_spec=pltpu.PrefetchScalarGrid...]
    all_to_all x1, waiting for transfers between devices: 15.6 us -> 12.4 us  [reduce(): out = lax.all_to_all(rows.reshape(size, -1, rows.shape[1]), axis, 0, 0)]
    all_to_all x1, starting transfers between devices: 6.69 us -> 9.05 us  [reduce(): out = lax.all_to_all(rows.reshape(size, -1, rows.shape[1]), axis, 0, 0)]
    ppermute x2, starting transfers between devices: 18.5 us -> 16.3 us  [swap(): return lax.ppermute(array, 'c', [(0, 1), (1, 0)])]
    all_to_all x1, starting transfers between devices: 12 us -> 9.88 us  [gather(): lax.all_to_all(jnp.broadcast_to(rows[None], (size, *rows.shape)), axis, 0...]
  transfers between devices with their start and end apart: 10 -> 10, of which waited for: 5 -> 6; matrix products, arithmetic and copies ran while one was open for 2% -> 2% of each run, Pallas kernels for 2% -> 0%
where the time goes in v14:
time: 139 us; the launch traced here: 137 us
  starting transfers between devices  56.5 us (41%)
  waiting for transfers between devices  38.1 us (27%)
  blocking collectives  19.3 us (14%)
  local copies, waits for them, and re-layouts  9.53 us (7%)
  Pallas kernels  9.3 us (7%)
  other arithmetic  3 us (2%)
    ppermute x6, waiting for transfers between devices, along_x(): return lax.ppermute(array, 'x', [(i, (i + step) % NX) for i in range(NX)])  24.5 us
    ppermute x6, starting transfers between devices, along_x(): return lax.ppermute(array, 'x', [(i, (i + step) % NX) for i in range(NX)])  21.2 us
    ppermute x2, starting transfers between devices, swap(): return lax.ppermute(array, 'c', [(0, 1), (1, 0)])  16.3 us
    all_to_all x1, waiting for transfers between devices, reduce(): out = lax.all_to_all(rows.reshape(size, -1, rows.shape[1]), axis, 0, 0)  12.4 us
    all_to_all x1, starting transfers between devices, gather(): lax.all_to_all(jnp.broadcast_to(rows[None], (size, *rows.shape)), axis, 0...  9.88 us
    all_to_all x1, blocking collectives, body(): rows = lax.all_to_all(rows, 'y', 0, 0).reshape(-1, out_grad.shape[1])  9.74 us
    all_to_all x1, blocking collectives, reduce(): out = lax.all_to_all(rows.reshape(size, -1, rows.shape[1]), axis, 0, 0)  9.6 us
    all_to_all x1, starting transfers between devices, reduce(): out = lax.all_to_all(rows.reshape(size, -1, rows.shape[1]), axis, 0, 0)  9.05 us
  transfers between devices with their start and end apart: 10, of which 6 were waited for; matrix products, arithmetic and copies ran while one was open for 2% of the time, Pallas kernels for 0%

profile of v14, /device:TPU:1, one launch (start us, length us, event | category | flops | bytes accessed | tf_op | source)
XLA Modules:
  0.0 136.7 jit_solution(18180620747787410967)
XLA Ops:
  0.7 1.3 copy-done
  2.0 0.9 copy-done.2
  4.3 1.3 copy-done.6
  5.6 2.0 %shard_map.76 = (bf16[128,2304]{1,0:T(8,128)(2,1)S(1)}, bf16[128,2816]{1,0:T(8,128)(2,1)S(1)}, bf16[8,6,512]{2,1,0:T(8,128)(2,1)S(1)}) custom-call(s32[3]{0:T(128)S(1)} %pad_add_fusion.place_ref, f32[1152]{0:T(1024)S(1)} %copy-done.4, bf16[128,4608]{1,0:T(8,128)(2,1)S(1)} %copy-done, bf16[768,768]{1,0:T(8,128)(2,1)S(1)} %copy-done.6, ...), custom_call_target="tpu_custom_call" | custom-call | flops 905969664 | bytes 3538944 | tf_op jit(solution)/shard_map/pallas_call | solution.py:115
  7.6 0.8 copy-done.8
  8.4 12.4 %collective-permute-start = (bf16[128,2816]{1,0:T(8,128)(2,1)S(1)}, bf16[128,2816]{1,0:T(8,128)(2,1)S(1)}, u32[]{:S(2)}, u32[]{:S(2)}) collective-permute-start(bf16[128,2816]{1,0:T(8,128)(2,1)S(1)} %get-tuple-element.30), channel_id=1, source_target_pairs={{0,1},{1,0},{2,3},{3,2},{4,5},{5,4},{6,7},{7,6},{8,9},{9,8},{10,11... | collective-permute-start | bytes 2162696 | tf_op jit(solution)/shard_map/ppermute | solution.py:32
  20.8 9.7 %all_to_all.20 = bf16[8,6,512]{2,1,0:T(8,128)(2,1)S(1)} all-to-all(bf16[8,6,512]{2,1,0:T(8,128)(2,1)S(1)} %get-tuple-element.31), channel_id=1, replica_groups=mesh['z'=12,'y'=8,'x'=4,'c'=2] {'y'}, dimensions={0} | all-to-all | bytes 98304 | tf_op jit(solution)/shard_map/all_to_all | solution.py:276
  30.6 1.1 copy-done.9
  31.7 1.5 %shard_map.77 = (bf16[576,512]{1,0:T(8,128)(2,1)S(1)}, bf16[576,512]{1,0:T(8,128)(2,1)S(1)}, bf16[576,512]{1,0:T(8,128)(2,1)S(1)}, bf16[576,512]{1,0:T(8,128)(2,1)S(1)}) custom-call(s32[3]{0:T(128)S(1)} %pad_add_fusion.place_ref, bf16[128,2304]{1,0:T(8,128)(2,1)S(1)} %copy-done.9, bf16[128,512]{1,0:T(8,128)(2,1)S(1)} %copy-done.3, ...), custom_call_target="tpu_custom_call" | custom-call | flops 603979776 | bytes 4718592 | tf_op jit(solution)/shard_map/pallas_call | solution.py:59
  33.2 0.8 copy-done.1
  34.0 0.9 broadcast_in_dim.2
  34.9 9.9 %all-to-all-start.1 = ((bf16[12,48,512]{2,1,0:T(8,128)(2,1)}), bf16[12,48,512]{2,1,0:T(8,128)(2,1)S(1)}, u32[]{:S(2)}, u32[]{:S(2)}) async-start(bf16[12,48,512]{2,1,0:T(8,128)(2,1)} %broadcast_in_dim.2), calls=%async_computation.1 | async-start | bytes 1179648 | tf_op jit(solution)/shard_map/all_to_all | solution.py:40
  44.8 3.1 %collective-permute-start.1 = (bf16[576,512]{1,0:T(8,128)(2,1)}, bf16[576,512]{1,0:T(8,128)(2,1)S(1)}, u32[]{:S(2)}, u32[]{:S(2)}) collective-permute-start(bf16[576,512]{1,0:T(8,128)(2,1)} %copy-done.1), channel_id=1, source_target_pairs={{0,2},{2,4},{4,6},{6,0},{1,3},{3,5},{5,7},{7,1},{8,10},{10,12},{12... | collective-permute-start | bytes 1769480 | tf_op jit(solution)/shard_map/ppermute | solution.py:36
  47.9 4.4 %collective-permute-start.2 = (bf16[576,512]{1,0:T(8,128)(2,1)S(1)}, bf16[576,512]{1,0:T(8,128)(2,1)S(1)}, u32[]{:S(2)}, u32[]{:S(2)}) collective-permute-start(bf16[576,512]{1,0:T(8,128)(2,1)S(1)} %get-tuple-element.40), channel_id=1, source_target_pairs={{0,4},{2,6},{4,0},{6,2},{1,5},{3,7},{5,1},{7,3},{8,12},{10,14},{12... | collective-permute-start | bytes 1769480 | tf_op jit(solution)/shard_map/ppermute | solution.py:36
  52.3 3.1 %collective-permute-start.3 = (bf16[576,512]{1,0:T(8,128)(2,1)S(1)}, bf16[576,512]{1,0:T(8,128)(2,1)S(1)}, u32[]{:S(2)}, u32[]{:S(2)}) collective-permute-start(bf16[576,512]{1,0:T(8,128)(2,1)S(1)} %get-tuple-element.41), channel_id=1, source_target_pairs={{0,6},{2,0},{4,2},{6,4},{1,7},{3,1},{5,3},{7,5},{8,14},{10,8},{12,... | collective-permute-start | bytes 1769480 | tf_op jit(solution)/shard_map/ppermute | solution.py:36
  55.4 5.7 %collective-permute-done.1 = bf16[576,512]{1,0:T(8,128)(2,1)S(1)} collective-permute-done((bf16[576,512]{1,0:T(8,128)(2,1)}, bf16[576,512]{1,0:T(8,128)(2,1)S(1)}, u32[]{:S(2)}, u32[]{:S(2)}) %collective-permute-start.1) | collective-permute-done | bytes 589856 | tf_op jit(solution)/shard_map/ppermute | solution.py:36
  61.1 13.6 %collective-permute-done.2 = bf16[576,512]{1,0:T(8,128)(2,1)S(1)} collective-permute-done((bf16[576,512]{1,0:T(8,128)(2,1)S(1)}, bf16[576,512]{1,0:T(8,128)(2,1)S(1)}, u32[]{:S(2)}, u32[]{:S(2)}) %collective-permute-start.2) | collective-permute-done | bytes 589856 | tf_op jit(solution)/shard_map/ppermute | solution.py:36
  74.7 2.5 %collective-permute-done.3 = bf16[576,512]{1,0:T(8,128)(2,1)S(1)} collective-permute-done((bf16[576,512]{1,0:T(8,128)(2,1)S(1)}, bf16[576,512]{1,0:T(8,128)(2,1)S(1)}, u32[]{:S(2)}, u32[]{:S(2)}) %collective-permute-start.3) | collective-permute-done | bytes 589856 | tf_op jit(solution)/shard_map/ppermute | solution.py:36
  77.3 1.1 add_convert_fusion
  78.4 9.1 %all-to-all-start.2 = ((bf16[12,48,512]{2,1,0:T(8,128)(2,1)}), bf16[12,48,512]{2,1,0:T(8,128)(2,1)}, u32[]{:S(2)}, u32[]{:S(2)}) async-start(bf16[12,48,512]{2,1,0:T(8,128)(2,1)} %bitcast.4), calls=%async_computation.2 | async-start | bytes 1179648 | tf_op jit(solution)/shard_map/all_to_all | solution.py:45
  87.5 5.3 %collective-permute-start.6 = (bf16[576,512]{1,0:T(8,128)(2,1)S(1)}, bf16[576,512]{1,0:T(8,128)(2,1)S(1)}, u32[]{:S(2)}, u32[]{:S(2)}) collective-permute-start(bf16[576,512]{1,0:T(8,128)(2,1)S(1)} %bitcast.5), channel_id=1, source_target_pairs={{0,6},{2,0},{4,2},{6,4},{1,7},{3,1},{5,3},{7,5},{8,14},{10,8},{12,... | collective-permute-start | bytes 1769480 | tf_op jit(solution)/shard_map/ppermute | solution.py:36
  92.8 3.5 %collective-permute-start.5 = (bf16[576,512]{1,0:T(8,128)(2,1)S(1)}, bf16[576,512]{1,0:T(8,128)(2,1)S(1)}, u32[]{:S(2)}, u32[]{:S(2)}) collective-permute-start(bf16[576,512]{1,0:T(8,128)(2,1)S(1)} %bitcast.6), channel_id=1, source_target_pairs={{0,4},{2,6},{4,0},{6,2},{1,5},{3,7},{5,1},{7,3},{8,12},{10,14},{12... | collective-permute-start | bytes 1769480 | tf_op jit(solution)/shard_map/ppermute | solution.py:36
  96.3 1.9 %collective-permute-start.4 = (bf16[576,512]{1,0:T(8,128)(2,1)S(1)}, bf16[576,512]{1,0:T(8,128)(2,1)S(1)}, u32[]{:S(2)}, u32[]{:S(2)}) collective-permute-start(bf16[576,512]{1,0:T(8,128)(2,1)S(1)} %bitcast.7), channel_id=1, source_target_pairs={{0,2},{2,4},{4,6},{6,0},{1,3},{3,5},{5,7},{7,1},{8,10},{10,12},{12... | collective-permute-start | bytes 1769480 | tf_op jit(solution)/shard_map/ppermute | solution.py:36
  98.2 12.4 %all-to-all-done.2 = bf16[12,48,512]{2,1,0:T(8,128)(2,1)} async-done(((bf16[12,48,512]{2,1,0:T(8,128)(2,1)}), bf16[12,48,512]{2,1,0:T(8,128)(2,1)}, u32[]{:S(2)}, u32[]{:S(2)}) %all-to-all-start.2) | async-done | bytes 589856 | tf_op jit(solution)/shard_map/all_to_all | solution.py:45
  110.6 1.2 reduce_sum.21
  111.8 9.6 %all_to_all.21 = bf16[8,6,512]{2,1,0:T(8,128)(2,1)S(1)} all-to-all(bf16[8,6,512]{2,1,0:T(8,128)(2,1)S(1)} %reshape.22), channel_id=1, replica_groups=mesh['z'=12,'y'=8,'x'=4,'c'=2] {'y'}, dimensions={0} | all-to-all | bytes 98304 | tf_op jit(solution)/shard_map/all_to_all | solution.py:45
  121.5 2.6 %collective-permute-done.4.rest_1_ = bf16[576,512]{1,0:T(8,128)(2,1)S(1)} collective-permute-done((bf16[576,512]{1,0:T(8,128)(2,1)S(1)}, bf16[576,512]{1,0:T(8,128)(2,1)S(1)}, u32[]{:S(2)}, u32[]{:S(2)}) %collective-permute-start.4) | collective-permute-done | bytes 589856 | tf_op jit(solution)/shard_map/ppermute | solution.py:36
  124.1 1.1 copy-done.10
  125.2 2.1 %shard_map.78 = (bf16[128,2816]{1,0:T(8,128)(2,1)S(1)}, f32[128,512]{1,0:T(8,128)S(1)}, bf16[128,2304]{1,0:T(8,128)(2,1)S(1)}) custom-call(s32[3]{0:T(128)S(1)} %pad_add_fusion.place_ref, bf16[128,2304]{1,0:T(8,128)(2,1)S(1)} %copy-done.10, bf16[128,512]{1,0:T(8,128)(2,1)S(1)} %copy-done.3, bf16[128,2816]{1,0:T(8,128)(2,1)S(1)} %collective-permute-done.theirs_ref, ...), custom_call_target="tpu_custom_call" | custom-call | flops 1207959552 | bytes 3145728 | tf_op jit(solution)/shard_map/pallas_call | solution.py:59
  127.3 3.9 %collective-permute-start.7 = (bf16[128,2816]{1,0:T(8,128)(2,1)S(1)}, bf16[128,2816]{1,0:T(8,128)(2,1)S(1)}, u32[]{:S(2)}, u32[]{:S(2)}) collective-permute-start(bf16[128,2816]{1,0:T(8,128)(2,1)S(1)} %get-tuple-element.51), channel_id=1, source_target_pairs={{0,1},{1,0},{2,3},{3,2},{4,5},{5,4},{6,7},{7,6},{8,9},{9,8},{10,11... | collective-permute-start | bytes 2162696 | tf_op jit(solution)/shard_map/ppermute | solution.py:32
  131.8 1.2 collective-permute-done.7.received_ref
  133.0 3.7 %shard_map.79 = (bf16[128,512]{1,0:T(8,128)(2,1)}, bf16[128,4608]{1,0:T(8,128)(2,1)}) custom-call(s32[3]{0:T(128)S(1)} %pad_add_fusion.place_ref, f32[128,512]{1,0:T(8,128)S(1)} %get-tuple-element.49.part_ref, bf16[128,2304]{1,0:T(8,128)(2,1)S(1)} %get-tuple-element.50.columns_ref, bf16[128,2816]{1,0:T(8,128)(2,1)S(1)} %collective-permute-done.7.received_ref, ...), custom_call_target="tpu_custom_call" | custom-call | flops 905969664 | bytes 2359296 | tf_op jit(solution)/shard_map/pallas_call | solution.py:248
  (24 shorter events, 2.2 us)
Async XLA Ops:
  0.7 1.3 copy-start
  2.0 0.9 copy-start.2
  2.9 0.7 copy-start.4
  3.6 0.7 copy-start.5
  4.3 1.3 copy-start.6
  5.6 25.0 %copy-start.3 = (bf16[128,512]{1,0:T(8,128)(2,1)S(1)}, bf16[128,512]{1,0:T(8,128)(2,1)}, u32[]{:S(2)}) copy-start(bf16[128,512]{1,0:T(8,128)(2,1)} %grad_ref.5) | copy-start | bytes 393220
  7.6 0.8 copy-start.8
  8.4 22.2 %collective-permute-start = (bf16[128,2816]{1,0:T(8,128)(2,1)S(1)}, bf16[128,2816]{1,0:T(8,128)(2,1)S(1)}, u32[]{:S(2)}, u32[]{:S(2)}) collective-permute-start(bf16[128,2816]{1,0:T(8,128)(2,1)S(1)} %get-tuple-element.30), channel_id=1, source_target_pairs={{0,1},{1,0},{2,3},{3,2},{4,5},{5,4},{6,7},{7,6},{8,9},{9,8},{10,11... | collective-permute-start | bytes 2162696 | tf_op jit(solution)/shard_map/ppermute | solution.py:32
  30.6 1.1 copy-start.9
  33.2 0.8 copy-start.1
  34.9 43.5 %all-to-all-start.1 = ((bf16[12,48,512]{2,1,0:T(8,128)(2,1)}), bf16[12,48,512]{2,1,0:T(8,128)(2,1)S(1)}, u32[]{:S(2)}, u32[]{:S(2)}) async-start(bf16[12,48,512]{2,1,0:T(8,128)(2,1)} %broadcast_in_dim.2), calls=%async_computation.1 | async-start | bytes 1179648 | tf_op jit(solution)/shard_map/all_to_all | solution.py:40
  44.8 16.3 %collective-permute-start.1 = (bf16[576,512]{1,0:T(8,128)(2,1)}, bf16[576,512]{1,0:T(8,128)(2,1)S(1)}, u32[]{:S(2)}, u32[]{:S(2)}) collective-permute-start(bf16[576,512]{1,0:T(8,128)(2,1)} %copy-done.1), channel_id=1, source_target_pairs={{0,2},{2,4},{4,6},{6,0},{1,3},{3,5},{5,7},{7,1},{8,10},{10,12},{12... | collective-permute-start | bytes 1769480 | tf_op jit(solution)/shard_map/ppermute | solution.py:36
  47.9 26.8 %collective-permute-start.2 = (bf16[576,512]{1,0:T(8,128)(2,1)S(1)}, bf16[576,512]{1,0:T(8,128)(2,1)S(1)}, u32[]{:S(2)}, u32[]{:S(2)}) collective-permute-start(bf16[576,512]{1,0:T(8,128)(2,1)S(1)} %get-tuple-element.40), channel_id=1, source_target_pairs={{0,4},{2,6},{4,0},{6,2},{1,5},{3,7},{5,1},{7,3},{8,12},{10,14},{12... | collective-permute-start | bytes 1769480 | tf_op jit(solution)/shard_map/ppermute | solution.py:36
  52.3 25.0 %collective-permute-start.3 = (bf16[576,512]{1,0:T(8,128)(2,1)S(1)}, bf16[576,512]{1,0:T(8,128)(2,1)S(1)}, u32[]{:S(2)}, u32[]{:S(2)}) collective-permute-start(bf16[576,512]{1,0:T(8,128)(2,1)S(1)} %get-tuple-element.41), channel_id=1, source_target_pairs={{0,6},{2,0},{4,2},{6,4},{1,7},{3,1},{5,3},{7,5},{8,14},{10,8},{12,... | collective-permute-start | bytes 1769480 | tf_op jit(solution)/shard_map/ppermute | solution.py:36
  78.4 32.2 %all-to-all-start.2 = ((bf16[12,48,512]{2,1,0:T(8,128)(2,1)}), bf16[12,48,512]{2,1,0:T(8,128)(2,1)}, u32[]{:S(2)}, u32[]{:S(2)}) async-start(bf16[12,48,512]{2,1,0:T(8,128)(2,1)} %bitcast.4), calls=%async_computation.2 | async-start | bytes 1179648 | tf_op jit(solution)/shard_map/all_to_all | solution.py:45
  87.5 34.0 %collective-permute-start.6 = (bf16[576,512]{1,0:T(8,128)(2,1)S(1)}, bf16[576,512]{1,0:T(8,128)(2,1)S(1)}, u32[]{:S(2)}, u32[]{:S(2)}) collective-permute-start(bf16[576,512]{1,0:T(8,128)(2,1)S(1)} %bitcast.5), channel_id=1, source_target_pairs={{0,6},{2,0},{4,2},{6,4},{1,7},{3,1},{5,3},{7,5},{8,14},{10,8},{12,... | collective-permute-start | bytes 1769480 | tf_op jit(solution)/shard_map/ppermute | solution.py:36
  92.8 28.6 %collective-permute-start.5 = (bf16[576,512]{1,0:T(8,128)(2,1)S(1)}, bf16[576,512]{1,0:T(8,128)(2,1)S(1)}, u32[]{:S(2)}, u32[]{:S(2)}) collective-permute-start(bf16[576,512]{1,0:T(8,128)(2,1)S(1)} %bitcast.6), channel_id=1, source_target_pairs={{0,4},{2,6},{4,0},{6,2},{1,5},{3,7},{5,1},{7,3},{8,12},{10,14},{12... | collective-permute-start | bytes 1769480 | tf_op jit(solution)/shard_map/ppermute | solution.py:36
  96.3 27.8 %collective-permute-start.4 = (bf16[576,512]{1,0:T(8,128)(2,1)S(1)}, bf16[576,512]{1,0:T(8,128)(2,1)S(1)}, u32[]{:S(2)}, u32[]{:S(2)}) collective-permute-start(bf16[576,512]{1,0:T(8,128)(2,1)S(1)} %bitcast.7), channel_id=1, source_target_pairs={{0,2},{2,4},{4,6},{6,0},{1,3},{3,5},{5,7},{7,1},{8,10},{10,12},{12... | collective-permute-start | bytes 1769480 | tf_op jit(solution)/shard_map/ppermute | solution.py:36
  121.4 11.6 %copy-start.7 = (bf16[768,768]{1,0:T(8,128)(2,1)S(1)}, bf16[768,768]{1,0:T(8,128)(2,1)}, u32[]{:S(2)}) copy-start(bf16[768,768]{1,0:T(8,128)(2,1)} %constant.31.clone.order_ref) | copy-start | bytes 3538948
  124.1 1.1 copy-start.10
  127.3 5.7 %collective-permute-start.7 = (bf16[128,2816]{1,0:T(8,128)(2,1)S(1)}, bf16[128,2816]{1,0:T(8,128)(2,1)S(1)}, u32[]{:S(2)}, u32[]{:S(2)}) collective-permute-start(bf16[128,2816]{1,0:T(8,128)(2,1)S(1)} %get-tuple-element.51), channel_id=1, source_target_pairs={{0,1},{1,0},{2,3},{3,2},{4,5},{5,4},{6,7},{7,6},{8,9},{9,8},{10,11... | collective-permute-start | bytes 2162696 | tf_op jit(solution)/shard_map/ppermute | solution.py:32
